TPU v7x, 32 devices: a whole 2x2x4 slice. The times are simulated.
32 devices in a mesh: page: 8 (over y, x, core), tok: 4 (over z).
Axes of the slice: x: 2, y: 2, z: 4, core: 2. Of those that a mesh axis runs over, the one named last changes fastest.
Arguments:
- tokens: bfloat16 [4480, 768], P(('page', 'tok')), may hold values from -6 to 6
- w_query: bfloat16 [768, 768], replicated, may hold values from -0.21875 to 0.21875
- w_key: bfloat16 [768, 768], replicated, may hold values from -0.21875 to 0.21875
- w_value: bfloat16 [768, 768], replicated, may hold values from -0.21875 to 0.21875
- w_out: bfloat16 [768, 768], replicated, may hold values from -1.75 to 1.75
- w_inner: bfloat16 [768, 3072], replicated, may hold values from -0.21875 to 0.21875
- w_outer: bfloat16 [3072, 768], replicated, may hold values from -0.109375 to 0.109375
- gain_one: float32 [768], replicated, may hold values from 0.5 to 1.5
- shift_one: float32 [768], replicated, may hold values from -3 to 3
- gain_two: float32 [768], replicated, may hold values from 0.5 to 1.5
- shift_two: float32 [768], replicated, may hold values from -3 to 3
- table_line: float32 [12, 32], replicated, may hold values from -3 to 3
- table_horiz: float32 [12, 32], replicated, may hold values from -3 to 3
- table_vert: float32 [12, 32], replicated, may hold values from -3 to 3
- region_weight: float32 [12], replicated, may hold values from -3 to 3
- region_ids: int32 [4480], P(('page', 'tok')), may hold values from 0 to 59
- line_pos: int32 [4480], P(('page', 'tok')), may hold values from 0 to 559
- box_horiz: int32 [4480], P(('page', 'tok')), may hold values from 0 to 63
- box_vert: int32 [4480], P(('page', 'tok')), may hold values from 0 to 63
- cotangent: bfloat16 [4480, 768], P(('page', 'tok')), may hold values from -6 to 6
Outputs:
- block_out: bfloat16 [4480, 768], P(('page', 'tok'))
- d_tokens: bfloat16 [4480, 768], P(('page', 'tok'))
- grad_w_query: float32 [768, 768], P(('page', 'tok'))
- grad_w_key: float32 [768, 768], P(('page', 'tok'))
- grad_w_value: float32 [768, 768], P(('page', 'tok'))
- grad_w_out: float32 [768, 768], P(('page', 'tok'))
- grad_w_inner: float32 [768, 3072], P(('page', 'tok'))
- grad_w_outer: float32 [3072, 768], P(('page', 'tok'))
- grad_gain_one: float32 [768], replicated
- grad_shift_one: float32 [768], replicated
- grad_gain_two: float32 [768], replicated
- grad_shift_two: float32 [768], replicated
- grad_table_line: float32 [12, 32], replicated
- grad_table_horiz: float32 [12, 32], replicated
- grad_table_vert: float32 [12, 32], replicated
- grad_region_weight: float32 [12], replicated
All inputs are finite; a program needn't handle non-finite values.
Results may differ from a plain program's by a relative error of at most 0.02.
Values may be sent and summed in bfloat16 or wider, within the bound.
No kernel may reach another device: no remote copies, remote signals or barrier semaphores. Data moves between devices by JAX's collectives and lax.ppermute only.
A program may use at most 128 MiB of HBM per device.

v0:
```python
import math

import jax
import jax.numpy as jnp
from jax import lax
from jax.experimental import pallas as pl
from jax.experimental.pallas import tpu as pltpu
from jax.sharding import PartitionSpec as P

REL = 32
BOXES = 64
BF = jnp.bfloat16
F32 = jnp.float32
I32 = jnp.int32
NEG = -1e30
LANES = 128
MIB = 2**20


def vmem():
    return pl.BlockSpec(memory_space=pltpu.VMEM)


def smem():
    return pl.BlockSpec(memory_space=pltpu.SMEM)


def like(shape, kind):
    return jax.ShapeDtypeStruct(shape, kind)


def launch(kernel, operands, in_specs, name, limit, out_shape, scratch_shapes=(), after=()):
    count = len(operands)

    def body(*refs):
        kernel(*refs[:count], *refs[count + len(after) :])

    return pl.pallas_call(
        body,
        out_shape=out_shape,
        in_specs=in_specs + [pl.BlockSpec(memory_space=pl.ANY)] * len(after),
        out_specs=[vmem()] * len(out_shape),
        scratch_shapes=list(scratch_shapes),
        compiler_params=pltpu.CompilerParams(vmem_limit_bytes=limit * MIB),
        name=name,
    )(*operands, *after)


def dot_nn(left, right):
    return lax.dot_general(left, right, (((1,), (0,)), ((), ())), preferred_element_type=F32)


def dot_nt(left, right):
    return lax.dot_general(left, right, (((1,), (1,)), ((), ())), preferred_element_type=F32)


def look(table_row, index):
    return jnp.take_along_axis(jnp.broadcast_to(table_row, index.shape), index, axis=1)


def two_parts(value):
    high = value.astype(BF)
    return high, (value - high.astype(F32)).astype(BF)


def key_places(info, shard, rows, keys):
    pieces = []
    for at in range(3):
        wide = jnp.concatenate(
            [info[:, at * 256 : (at + 1) * 256], jnp.zeros((16, keys - 256), F32)], 1
        )
        pieces.append(pltpu.roll(wide, shard * rows, 1) if shard else wide)
    return pieces


def line_index(query_at, key_at):
    bucket = jnp.clip(key_at[1:2, :] - query_at[:, 1:2], -(REL // 2), REL // 2 - 1) + REL // 2
    same = jnp.where(query_at[:, 0:1] == key_at[0:1, :], REL, 0)
    return jnp.where(key_at[4:5, :] > 0, bucket + same, 2 * REL)


def attn_forward(
    token_shards, row_count, w_query, w_key, w_value, line_table, box_table, query_at
):
    rows, width = token_shards[0].shape
    head_count = line_table.shape[0]
    shards = len(token_shards)
    keys = -(-rows * shards // LANES) * LANES

    def kernel(*refs):
        tok_refs = refs[:shards]
        wq, wk, wv, line_ref, box_ref, q_at = refs[shards : shards + 6]
        mix_ref, q_ref, k_ref, v_ref, x_ref, p_ref, k_at, line_idx, box_idx, hots = refs[
            shards + 6 :
        ]
        places = [jnp.zeros((16, keys), F32)] * 3
        for at in range(shards):
            info = tok_refs[at][rows - 16 :, :].astype(F32)
            places = [
                left + right for left, right in zip(places, key_places(info, at, rows, keys))
            ]
        lane = lax.broadcasted_iota(I32, (1, keys), 1)
        live = jnp.zeros((1, keys), I32)
        for at in range(shards):
            inside = (lane >= at * rows) & (lane < at * rows + row_count)
            live = jnp.where(inside, 1, live)
        k_at[...] = jnp.zeros_like(k_at)
        k_at[0:1] = places[0][14:15].astype(I32)
        k_at[1:2] = (places[1][14:15] * 32.0 + places[2][14:15]).astype(I32)
        k_at[2:3] = places[0][15:16].astype(I32)
        k_at[3:4] = places[1][15:16].astype(I32)
        k_at[4:5] = live
        for at in range(shards):
            x_ref[at * rows : (at + 1) * rows] = tok_refs[at][...]
        if keys > shards * rows:
            x_ref[shards * rows :] = jnp.zeros((keys - shards * rows, width), BF)
        q_ref[...] = (dot_nn(tok_refs[0][...], wq[...]) * 0.125).astype(BF)
        k_ref[...] = dot_nn(x_ref[...], wk[...]).astype(BF)
        v_ref[...] = dot_nn(x_ref[...], wv[...]).astype(BF)
        line_idx[...] = line_index(q_at, k_at)
        lane = lax.broadcasted_iota(I32, (rows, LANES), 1)
        place = jnp.where(lane < BOXES, q_at[:, 2:3], q_at[:, 3:4])
        bucket = jnp.clip((lane & (BOXES - 1)) - place, -(REL // 2), REL // 2 - 1) + REL // 2
        box_idx[...] = bucket + jnp.where(lane < BOXES, 0, REL)
        sub = lax.broadcasted_iota(I32, (LANES, keys), 0)
        place = jnp.where(sub < BOXES, k_at[2:3, :], k_at[3:4, :])
        hot = ((sub & (BOXES - 1)) == place).astype(F32).astype(BF)
        hots[0:LANES] = hot
        hots[LANES:] = hot

        def pair(at, carry):
            col = pl.ds(pl.multiple_of(at * LANES, LANES), LANES)
            q_pair, k_pair, v_pair = q_ref[:, col], k_ref[:, col], v_ref[:, col]
            mixed = []
            for half in range(2):
                head = 2 * at + half
                mine = (lane < 64) if half == 0 else (lane >= 64)
                q_one = jnp.where(mine, q_pair, jnp.zeros_like(q_pair))
                high, low = two_parts(look(box_ref[pl.ds(head, 1), :], box_idx[...]))
                score = dot_nt(q_one, k_pair) + dot_nn(jnp.concatenate([high, low], 1), hots[...])
                line_row = line_ref[pl.ds(head, 1), :]
                score = score + jnp.concatenate(
                    [
                        look(line_row, line_idx[:, cut : cut + LANES])
                        for cut in range(0, keys, LANES)
                    ],
                    1,
                )
                grown = jnp.exp(score - jnp.max(score, axis=1, keepdims=True))
                probs = grown * (1.0 / jnp.sum(grown, axis=1, keepdims=True))
                low_probs = probs.astype(BF)
                p_ref[pl.ds(head, 1)] = low_probs[None]
                mixed.append(dot_nn(low_probs, v_pair))
            mix_ref[:, col] = jnp.where(lane < 64, mixed[0], mixed[1]).astype(BF)
            return carry

        lax.fori_loop(0, width // LANES, pair, 0)

    return launch(
        kernel,
        (*token_shards, w_query, w_key, w_value, line_table, box_table, query_at),
        [vmem()] * (shards + 6),
        "attn_forward",
        8,
        (
            like((rows, width), BF),
            like((rows, width), BF),
            like((keys, width), BF),
            like((keys, width), BF),
            like((keys, width), BF),
            like((head_count, rows, keys), BF),
            like((8, keys), I32),
        ),
        [
            pltpu.VMEM((rows, keys), I32),
            pltpu.VMEM((rows, LANES), I32),
            pltpu.VMEM((2 * LANES, keys), BF),
        ],
    )


def row_mean(value):
    return jnp.mean(value, axis=1, keepdims=True)


def all_sum(value):
    return jnp.sum(jnp.sum(value, axis=1, keepdims=True), axis=0, keepdims=True)


def normal(value):
    centered = value - row_mean(value)
    scale = lax.rsqrt(row_mean(centered * centered) + 1e-05)
    return centered * scale, scale


def normal_back(d_normal, n, scale):
    return scale * (d_normal - row_mean(d_normal) - n * row_mean(d_normal * n))


FF_CUT = 512


def feed_forward(mix, tokens, w_out, w_inner, w_outer, vectors, cotangent):
    rows, width = tokens.shape
    hidden_units = w_inner.shape[1]

    def kernel(mix_ref, tok, wo, wi, wu, vec, cot, *outs):
        block, hid, n_one, r_one, act, slope, d_sec, d_out, sums, total = outs
        n, r = normal(tok[...].astype(F32) + dot_nn(mix_ref[...], wo[...]))
        n_one[...] = n
        r_one[...] = jnp.broadcast_to(r, r_one.shape)
        hidden = n * vec[0:1, :] + vec[1:2, :]
        hid[...] = hidden.astype(BF)
        total[...] = hidden
        for cut in range(0, hidden_units, FF_CUT):
            inner = dot_nn(hid[...], wi[:, cut : cut + FF_CUT])
            upper = 0.5 + 0.5 * lax.erf(inner * (0.5**0.5))
            active = (inner * upper).astype(BF)
            act[:, cut : cut + FF_CUT] = active
            bell = jnp.exp(-0.5 * inner * inner) * (2.0 * math.pi) ** -0.5
            slope[:, cut : cut + FF_CUT] = upper + inner * bell
            total[...] += dot_nn(active, wu[cut : cut + FF_CUT, :])
        n, r = normal(total[...])
        block[...] = (n * vec[2:3, :] + vec[3:4, :]).astype(BF)
        grad = cot[...].astype(F32)
        sums[0:1, :] = jnp.sum(grad * n, axis=0, keepdims=True)
        sums[1:2, :] = jnp.sum(grad, axis=0, keepdims=True)
        second = normal_back(grad * vec[2:3, :], n, r)
        d_sec[...] = second
        d_out[...] = second.astype(BF)

    return launch(
        kernel,
        (mix, tokens, w_out, w_inner, w_outer, vectors, cotangent),
        [vmem()] * 7,
        "feed_forward",
        10,
        (
            like((rows, width), BF),
            like((rows, width), BF),
            like((rows, width), F32),
            like((rows, LANES), F32),
            like((rows, hidden_units), BF),
            like((rows, hidden_units), F32),
            like((rows, width), F32),
            like((rows, width), BF),
            like((2, width), F32),
        ),
        [pltpu.VMEM((rows, width), F32)],
    )


def feed_back(d_outer, d_second, slope, n_one, r_one, w_inner, w_outer, vectors, after):
    rows, width = d_outer.shape
    hidden_units = w_inner.shape[1]

    def kernel(d_out, d_sec, slope_ref, n_ref, r_ref, wi, wu, vec, d_in, d_first, d_attn, sums):
        d_first[...] = d_sec[...]
        for cut in range(0, hidden_units, FF_CUT):
            grad = dot_nt(d_out[...], wu[cut : cut + FF_CUT, :])
            grad = (grad * slope_ref[:, cut : cut + FF_CUT]).astype(BF)
            d_in[:, cut : cut + FF_CUT] = grad
            d_first[...] += dot_nt(grad, wi[:, cut : cut + FF_CUT])
        d_hidden = d_first[...]
        n = n_ref[...]
        sums[0:1, :] = jnp.sum(d_hidden * n, axis=0, keepdims=True)
        sums[1:2, :] = jnp.sum(d_hidden, axis=0, keepdims=True)
        first = normal_back(d_hidden * vec[0:1, :], n, r_ref[:, 0:1])
        d_first[...] = first
        d_attn[...] = first.astype(BF)

    return launch(
        kernel,
        (d_outer, d_second, slope, n_one, r_one, w_inner, w_outer, vectors),
        [vmem()] * 8,
        "feed_back",
        10,
        (
            like((rows, hidden_units), BF),
            like((rows, width), F32),
            like((rows, width), BF),
            like((2, width), F32),
        ),
        after=after,
    )


def attn_back(
    d_attn, probs, query, keys_all, values_all, w_out, query_at, key_at, first_pair, pairs, name, after
):
    rows, width = d_attn.shape
    columns = pairs * LANES
    head_count, _, keys = probs.shape
    half_span = REL // 2

    def kernel(*refs):
        d_at, p_ref, q_ref, k_ref, v_ref, wo, q_at, k_at = refs[:8]
        dq_ref, dk_ref, dv_ref, tables = refs[8:12]
        d_heads, heads_t, q_t, line_idx, key_hots, line_hots, row_hots, line_rows, rolls = refs[12:]
        base = first_pair * LANES
        grad = dot_nt(d_at[...], wo[base : base + columns, :])
        d_heads[...] = grad.astype(BF)
        heads_t[...] = grad.T.astype(BF)
        q_t[...] = q_ref[:, base : base + columns].astype(F32).T.astype(BF)
        line_idx[...] = line_index(q_at, k_at)
        lane = lax.broadcasted_iota(I32, (rows, LANES), 1)
        sub = lax.broadcasted_iota(I32, (LANES, keys), 0)
        place = jnp.where(sub < BOXES, k_at[2:3, :], k_at[3:4, :])
        key_hots[0:LANES] = ((sub & (BOXES - 1)) == place).astype(F32).astype(BF)
        key_hots[LANES:] = (sub == k_at[0:1, :]).astype(F32).astype(BF)
        line_hots[...] = (sub == (k_at[1:2, :] & (LANES - 1))).astype(F32).astype(BF)
        place = jnp.where(lane < BOXES, q_at[:, 2:3], q_at[:, 3:4])
        row_hots[...] = ((BOXES - 1 - (lane & (BOXES - 1))) == place).astype(F32).T.astype(BF)
        line_rows[...] = (
            ((LANES - 1 - lane) == (q_at[:, 1:2] & (LANES - 1))).astype(F32).T.astype(BF)
        )
        region_hot = (lane == q_at[:, 0:1]).astype(F32)
        tables[...] = jnp.zeros_like(tables)
        rolls[...] = jnp.zeros_like(rolls)
        square_row = lax.broadcasted_iota(I32, (LANES, LANES), 0)
        square_lane = lax.broadcasted_iota(I32, (LANES, LANES), 1)
        one_lane = lax.broadcasted_iota(I32, (1, LANES), 1)
        def rolled(square):
            return jnp.sum(
                pltpu.roll(square, 0, 1, stride=1, stride_axis=0), axis=0, keepdims=True
            )

        def pair(at, carry):
            col = pl.ds(pl.multiple_of(at * LANES, LANES), LANES)
            key_col = pl.ds(pl.multiple_of(base + at * LANES, LANES), LANES)
            d_pair, k_pair, v_pair = d_heads[:, col], k_ref[:, key_col], v_ref[:, key_col]
            back = []
            for half in range(2):
                head = 2 * (first_pair + at) + half
                own = pl.ds(pl.multiple_of(at * LANES + 64 * half, 64), 64)
                mine = (lane < 64) if half == 0 else (lane >= 64)
                d_one = jnp.where(mine, d_pair, jnp.zeros_like(d_pair))
                d_probs = dot_nt(d_one, v_pair)
                low_probs = p_ref[head]
                p_one = low_probs.astype(F32)
                row_dot = jnp.sum(p_one * d_probs, axis=1, keepdims=True)
                d_score = p_one * (d_probs - row_dot)
                low_score = d_score.astype(BF)
                back.append(dot_nn(low_score, k_pair))
                dk_ref[own, :] = dot_nn(q_t[own, :], low_score).astype(BF)
                dv_ref[own, :] = dot_nn(heads_t[own, :], low_probs).astype(BF)
                at_keys = dot_nt(low_score, key_hots[...])
                in_region = all_sum(at_keys[:, LANES:] * region_hot)
                boxes = at_keys[:, :LANES]
                whole = all_sum(jnp.where(lane < BOXES, boxes, 0.0))
                high, low = two_parts(boxes)
                square = dot_nn(row_hots[...], high) + dot_nn(row_hots[...], low)
                horiz = rolled(jnp.where((square_row < 64) & (square_lane < 64), square, 0.0))
                vert = pltpu.roll(
                    jnp.where((square_row >= 64) & (square_lane >= 64), square, 0.0),
                    64,
                    1,
                    stride=1,
                    stride_axis=0,
                )
                vert = jnp.sum(vert, axis=0, keepdims=True)
                near = line_idx[...] & (REL - 1)
                wide = low_score.astype(F32)
                inside = jnp.where((near > 0) & (near < REL - 1), wide, 0.0).astype(BF)
                before = all_sum(jnp.where(near == 0, wide, 0.0))
                high, low = two_parts(dot_nt(inside, line_hots[...]))
                square = dot_nn(line_rows[...], high) + dot_nn(line_rows[...], low)
                line = rolled(square)
                within = all_sum(square)
                rolls[0, pl.ds(head, 1), :] = horiz
                rolls[1, pl.ds(head, 1), :] = vert
                rolls[2, pl.ds(head, 1), :] = line
                row = jnp.where(one_lane == 0, before, 0.0)
                row = row + jnp.where(one_lane == REL - 1, whole - before - within, 0.0)
                row = row + jnp.where(one_lane == 3 * REL, in_region, 0.0)
                tables[pl.ds(head, 1), :] = row
            dq_ref[:, col] = (jnp.where(lane < 64, back[0], back[1]) * 0.125).astype(BF)
            return carry

        lax.fori_loop(0, pairs, pair, 0)
        bucket = square_lane & (REL - 1)

        def from_distance(distance):
            return jnp.clip(distance, -half_span, half_span - 1) + half_span

        horiz_map = (
            (from_distance(square_row - (BOXES - 1)) == bucket)
            & (square_lane >= REL)
            & (square_lane < 2 * REL)
        ).astype(F32)
        around = jnp.where(square_row < BOXES, square_row + 1, square_row + 1 - LANES)
        vert_map = (
            (from_distance(around) == bucket)
            & (square_lane >= 2 * REL)
            & (square_lane < 3 * REL)
        ).astype(F32)
        line_map = ((from_distance(around) == bucket) & (square_lane < REL)).astype(F32)

        def exact(left, right):
            return lax.dot_general(
                left,
                right,
                (((1,), (0,)), ((), ())),
                precision=lax.Precision.HIGHEST,
                preferred_element_type=F32,
            )

        tables[...] += (
            exact(rolls[0], horiz_map) + exact(rolls[1], vert_map) + exact(rolls[2], line_map)
        )

    return launch(
        kernel,
        (d_attn, probs, query, keys_all, values_all, w_out, query_at, key_at),
        [vmem()] * 8,
        name,
        8,
        (
            like((rows, columns), BF),
            like((columns, keys), BF),
            like((columns, keys), BF),
            like((16, LANES), F32),
        ),
        [
            pltpu.VMEM((rows, columns), BF),
            pltpu.VMEM((columns, rows), BF),
            pltpu.VMEM((columns, rows), BF),
            pltpu.VMEM((rows, keys), I32),
            pltpu.VMEM((2 * LANES, keys), BF),
            pltpu.VMEM((LANES, keys), BF),
            pltpu.VMEM((LANES, rows), BF),
            pltpu.VMEM((LANES, rows), BF),
            pltpu.VMEM((3, 16, LANES), F32),
        ],
        after,
    )


def rows_back(d_first, parts, weights, shards, after):
    rows, width = d_first.shape

    def kernel(*refs):
        first, wq, wk, wv = refs[:4]
        part_refs = refs[4 : 4 + 3 * len(parts)]
        own, *sent = refs[4 + 3 * len(parts) :]
        for at in range(shards - 1, -1, -1):
            cut = slice(at * rows, (at + 1) * rows)
            total, place = None, 0
            for group in range(len(parts)):
                _, dk, dv = part_refs[3 * group : 3 * group + 3]
                col = slice(place, place + dk.shape[0])
                value = dot_nn(wk[:, col], dk[:, cut]) + dot_nn(wv[:, col], dv[:, cut])
                total = value if total is None else total + value
                place += dk.shape[0]
            if at:
                sent[at - 1][...] = total.T.astype(BF)
                continue
            result, place = first[...] + total.T, 0
            for group in range(len(parts)):
                dq = part_refs[3 * group]
                col = slice(place, place + dq.shape[1])
                result = result + dot_nt(dq[...], wq[:, col])
                place += dq.shape[1]
            own[...] = result

    flat = [array for part in parts for array in part]
    return launch(
        kernel,
        (d_first, *weights, *flat),
        [vmem()] * (4 + len(flat)),
        "rows_back",
        8,
        (like((rows, width), F32),) + (like((rows, width), BF),) * (shards - 1),
        after=after,
    )


def swap(array_in, axis_name, flip):
    size = lax.axis_size(axis_name)
    return lax.ppermute(array_in, axis_name, [(at, at ^ flip) for at in range(size)])


def tok_shards(array_in):
    return [array_in] + [swap(array_in, "tok", step) for step in range(1, lax.axis_size("tok"))]


def xor_terms(groups, name, after=()):
    pages = lax.axis_size("page")
    page_index = lax.axis_index("page")
    width = groups[0][0].shape[1]
    rows = width // pages
    cols = [right.shape[1] if form == "nn" else right.shape[0] for _, right, form in groups]
    if rows % 16:
        whole = jnp.concatenate(
            [
                lax.dot_general(
                    left,
                    right,
                    (((0,), (0 if form == "nn" else 1,)), ((), ())),
                    preferred_element_type=F32,
                ).astype(BF)
                for left, right, form in groups
            ],
            1,
        ).reshape(pages, rows, -1)
        order = page_index ^ jnp.arange(pages)
        whole = jnp.take(whole, order, axis=0)
        return whole[0::2], whole[1::2]
    lefts, which = [], []
    for left, _, _ in groups:
        found = [at for at, item in enumerate(lefts) if item is left]
        which.append(found[0] if found else len(lefts))
        if not found:
            lefts.append(left)

    def kernel(page_ref, *refs):
        left_refs = refs[: len(lefts)]
        right_refs = refs[len(lefts) : len(lefts) + len(groups)]
        keep, send = refs[len(lefts) + len(groups) : len(lefts) + len(groups) + 2]
        turned = refs[len(lefts) + len(groups) + 2 :][: len(lefts)]
        picked = refs[2 * len(lefts) + len(groups) + 2 :]
        for left_ref, turned_ref in zip(left_refs, turned):
            turned_ref[...] = (
                left_ref[...].astype(F32).T.astype(BF).reshape(pages, rows, left_ref.shape[0])
            )
        page = page_ref[0]
        for odd, out in ((1, send), (0, keep)):
            for at, turned_ref in enumerate(turned):
                for step in range(pages // 2):
                    picked[at][step * rows : (step + 1) * rows] = turned_ref[
                        page ^ (2 * step + odd)
                    ]
            place = 0
            for at_left, right_ref, (_, _, form), count in zip(which, right_refs, groups, cols):
                for cut in range(0, count, 256):
                    end = min(cut + 256, count)
                    if form == "nn":
                        value = dot_nn(picked[at_left][...], right_ref[:, cut:end])
                    else:
                        value = dot_nt(picked[at_left][...], right_ref[cut:end, :])
                    out[:, :, place + cut : place + end] = value.astype(BF).reshape(
                        pages // 2, rows, end - cut
                    )
                place += count

    out = like((pages // 2, rows, sum(cols)), BF)
    return launch(
        kernel,
        (
            page_index.reshape(1).astype(I32),
            *lefts,
            *[right for _, right, _ in groups],
        ),
        [smem()] + [vmem()] * (len(lefts) + len(groups)),
        name,
        10,
        (out, out),
        [pltpu.VMEM((pages, rows, left.shape[0]), BF) for left in lefts]
        + [pltpu.VMEM((pages // 2 * rows, left.shape[0]), BF) for left in lefts],
        after,
    )


def split_sum(pairs, picks, name, after=()):
    def kernel(*refs):
        ins, outs = refs[: 2 * len(pairs)], refs[2 * len(pairs) :]
        for out, (pair, items, first, count) in zip(outs, picks):
            for at, item in enumerate(items):
                cut = slice(first, first + count)
                out[at] = ins[2 * pair][item, :, cut] + ins[2 * pair + 1][item, :, cut]

    rows = pairs[0][0].shape[1]
    return launch(
        kernel,
        [array for pair in pairs for array in pair],
        [vmem()] * (2 * len(pairs)),
        name,
        4,
        tuple(like((len(items), rows, count), BF) for _, items, _, count in picks),
        after=after,
    )


def tok_split(pairs, name, after=()):
    toks = lax.axis_size("tok")
    rows, cols = pairs[0][0].shape[1:]
    share = rows // toks
    arrays = [array.reshape(toks, share, cols) for pair in pairs for array in pair]

    def kernel(tok_ref, *refs):
        ins, outs = refs[: len(arrays)], refs[len(arrays) :]
        for step in range(toks):
            at = tok_ref[0] ^ step
            for pair in range(len(pairs)):
                value = ins[2 * pair][at].astype(F32) + ins[2 * pair + 1][at].astype(F32)
                out = outs[step]
                out[:, pair * cols : (pair + 1) * cols] = value.astype(out.dtype)

    full = (share, cols * len(pairs))
    return launch(
        kernel,
        (lax.axis_index("tok").reshape(1).astype(I32), *arrays),
        [smem()] + [vmem()] * len(arrays),
        name,
        4,
        (like(full, F32),) + (like(full, BF),) * (toks - 1),
        after=after,
    )


class Reduction:
    def __init__(self, keep, send, name):
        self.name = name
        self.pairs = [(keep, swap(send, "page", 1))]
        bits = [1 << at for at in range(1, lax.axis_size("page").bit_length() - 1)]
        self.orders = [bits, bits[::-1]]
        self.items = [list(range(0, lax.axis_size("page"), 2))] * 2

    def step(self, after=()):
        at_step = len(self.orders[0])
        cols = self.pairs[0][0].shape[2]
        first = len(self.pairs) == 1
        width = cols // 2 if first else cols
        picks, kept_items = [], []
        for half in range(2):
            bit = self.orders[half][0]
            items = self.items[half]
            where = (0, half * width) if first else (half, 0)
            for wanted in (bit, 0):
                chosen = [at for at, item in enumerate(items) if item & bit == wanted]
                picks.append((where[0], chosen, where[1], width))
            kept_items.append([item for item in items if not item & bit])
        outs = split_sum(self.pairs, picks, f"{self.name}_sum{at_step}", after)
        self.last = outs[-1]
        self.pairs = [
            (outs[2 * half + 1], swap(outs[2 * half], "page", self.orders[half][0]))
            for half in range(2)
        ]
        self.items = kept_items
        self.orders = [order[1:] for order in self.orders]

    def to_tok(self, after=()):
        while self.orders[0]:
            self.step(after)
        own, *sent = tok_split(self.pairs, f"{self.name}_tok", after)
        self.last = own
        self.shares = [own] + [swap(piece, "tok", at + 1) for at, piece in enumerate(sent)]

    def result(self):
        total = self.shares[0]
        for piece in self.shares[1:]:
            total = total + piece.astype(F32)
        return total


def sum_all(vector):
    bit = 1
    while bit < lax.axis_size("page"):
        vector = vector + swap(vector, "page", bit)
        bit *= 2
    bit = 1
    while bit < lax.axis_size("tok"):
        vector = vector + swap(vector, "tok", bit)
        bit *= 2
    return vector


def on_device(
    tokens,
    w_query,
    w_key,
    w_value,
    w_out,
    w_inner,
    w_outer,
    gain_one,
    shift_one,
    gain_two,
    shift_two,
    table_line,
    table_horiz,
    table_vert,
    region_weight,
    region_ids,
    line_pos,
    box_horiz,
    box_vert,
    cotangent,
):
    row_count, width = tokens.shape
    shards = lax.axis_size("tok")
    rows = -(-(row_count + 2) // 16) * 16

    def padded(array_in):
        return jnp.pad(array_in, ((0, rows - row_count), (0, 0)))

    def spread(*lines):
        return jnp.concatenate(
            [jnp.pad(line, (0, 256 - row_count)) for line in lines]
            + [jnp.zeros(width - 256 * len(lines), I32)]
        )

    info = jnp.stack(
        [spread(region_ids, line_pos // 32, line_pos % 32), spread(box_horiz, box_vert)]
    ).astype(BF)
    padded_tokens = jnp.concatenate(
        [tokens, jnp.zeros((rows - row_count - 2, width), BF), info], 0
    )
    token_shards = tok_shards(padded_tokens)
    places = jnp.stack([region_ids, line_pos, box_horiz, box_vert], 1)
    query_at = jnp.pad(places, ((0, rows - row_count), (0, 4)))
    line_table = jnp.concatenate(
        [
            table_line,
            table_line + region_weight[:, None],
            jnp.full((table_line.shape[0], LANES - 2 * REL), NEG, F32),
        ],
        1,
    )
    box_table = jnp.pad(
        jnp.concatenate([table_horiz, table_vert], 1), ((0, 0), (0, LANES - 2 * REL))
    )
    vectors = jnp.stack([gain_one, shift_one, gain_two, shift_two], 0)

    mix, query, keys_all, values_all, tokens_all, probs, key_at = attn_forward(
        token_shards, row_count, w_query, w_key, w_value, line_table, box_table, query_at
    )
    block, hidden, n_one, r_one, active, slope, d_second, d_outer, sums_two = feed_forward(
        mix, padded_tokens, w_out, w_inner, w_outer, vectors, padded(cotangent)
    )
    terms = xor_terms([(active, d_outer, "nn")], "outer_terms")
    outer = Reduction(*terms, "outer")
    d_inner, d_first, d_attn, sums_one = feed_back(
        d_outer, d_second, slope, n_one, r_one, w_inner, w_outer, vectors, (terms[0],)
    )
    outer.step((d_attn,))
    terms = xor_terms(
        [(hidden, d_inner, "nn"), (mix, d_attn, "nn")], "inner_terms", (outer.last,)
    )
    inner = Reduction(*terms, "inner")
    half_pairs = width // LANES // 2
    parts, table_parts, done = [], [], terms[0]
    for group in range(2):
        *part, table_part = attn_back(
            d_attn,
            probs,
            query,
            keys_all,
            values_all,
            w_out,
            query_at,
            key_at,
            group * half_pairs,
            half_pairs,
            f"attn_back{group}",
            (done,),
        )
        parts.append(part)
        table_parts.append(table_part)
        if group == 0:
            inner.step((table_part,))
            outer.step((inner.last,))
            done = outer.last
    terms = xor_terms(
        [(padded_tokens, part[0], "nn") for part in parts]
        + [(tokens_all, part[1], "nt") for part in parts]
        + [(tokens_all, part[2], "nt") for part in parts],
        "attn_terms",
    )
    attn = Reduction(*terms, "attn")
    d_own, *sent = rows_back(
        d_first, parts, (w_query, w_key, w_value), shards, (terms[0],)
    )
    inner.step((d_own,))
    attn.step((inner.last,))
    outer.to_tok((attn.last,))
    back = [swap(piece, "tok", at + 1) for at, piece in enumerate(sent)]
    small = jnp.concatenate(
        [
            sums_one.reshape(-1, LANES),
            sums_two.reshape(-1, LANES),
            table_parts[0] + table_parts[1],
        ],
        0,
    )
    small = sum_all(small)
    attn.step((outer.last,))
    inner.to_tok((attn.last,))
    attn.to_tok((inner.last,))
    for piece in back:
        d_own = d_own + piece.astype(F32)
    d_tokens = d_own[:row_count].astype(BF)
    vector_rows = width // LANES
    vector_sums = small[: 4 * vector_rows].reshape(4, width)
    tables = small[4 * vector_rows :][: table_line.shape[0]]
    grad_attn = attn.result()
    grad_attn = [grad_attn[:, at * width : (at + 1) * width] for at in range(3)]
    grad_inner = inner.result()
    units = w_inner.shape[1]
    return (
        block[:row_count],
        d_tokens,
        *grad_attn,
        grad_inner[:, units:],
        grad_inner[:, :units],
        outer.result(),
        vector_sums[0],
        vector_sums[1],
        vector_sums[2],
        vector_sums[3],
        tables[:, 0:REL],
        tables[:, REL : 2 * REL],
        tables[:, 2 * REL : 3 * REL],
        tables[:, 3 * REL],
    )


def solution(mesh):
    placed = (
        P(("page", "tok"), None),
        P(),
        P(),
        P(),
        P(),
        P(),
        P(),
        P(),
        P(),
        P(),
        P(),
        P(),
        P(),
        P(),
        P(),
        P(("page", "tok")),
        P(("page", "tok")),
        P(("page", "tok")),
        P(("page", "tok")),
        P(("page", "tok"), None),
    )
    return jax.shard_map(
        on_device,
        mesh=mesh,
        in_specs=placed,
        out_specs=(
            P(("page", "tok"), None),
            P(("page", "tok"), None),
            P(("page", "tok"), None),
            P(("page", "tok"), None),
            P(("page", "tok"), None),
            P(("page", "tok"), None),
            P(("page", "tok"), None),
            P(("page", "tok"), None),
            P(),
            P(),
            P(),
            P(),
            P(),
            P(),
            P(),
            P(),
        ),
        check_vma=False,
    )
```

profile of v0, /device:TPU:0, one launch (start us, length us, event | category | flops | bytes accessed | tf_op | source)
XLA Modules:
  0.0 189.0 jit_solution(12513726507201896399)
XLA Ops:
  4.6 3.1 %collective-permute-start = (bf16[144,768]{1,0:T(8,128)(2,1)S(1)}, bf16[144,768]{1,0:T(8,128)(2,1)S(1)}, u32[]{:S(2)}, u32[]{:S(2)}) collective-permute-start(bf16[144,768]{1,0:T(8,128)(2,1)S(1)} %pad_maximum_fusion.refs_0_.refs_1_), channel_id=1, source_target_pairs={{0,1},{1,0},{2,3},{3,2},{4,5},{5,4},{6,7},{7,6},{8,9},{9,8},{10,11... | collective-permute-start | bytes 663560 | tf_op jit(solution)/shard_map/ppermute | solution.py:480
  7.7 2.6 %collective-permute-start.1 = (bf16[144,768]{1,0:T(8,128)(2,1)S(1)}, bf16[144,768]{1,0:T(8,128)(2,1)S(1)}, u32[]{:S(2)}, u32[]{:S(2)}) collective-permute-start(bf16[144,768]{1,0:T(8,128)(2,1)S(1)} %pad_maximum_fusion.refs_0_.refs_1_), channel_id=1, source_target_pairs={{0,2},{1,3},{2,0},{3,1},{4,6},{5,7},{6,4},{7,5},{8,10},{9,11},{10,... | collective-permute-start | bytes 663560 | tf_op jit(solution)/shard_map/ppermute | solution.py:480
  17.1 9.3 %collective-permute-done.1.refs_2_ = bf16[144,768]{1,0:T(8,128)(2,1)S(1)} collective-permute-done((bf16[144,768]{1,0:T(8,128)(2,1)S(1)}, bf16[144,768]{1,0:T(8,128)(2,1)S(1)}, u32[]{:S(2)}, u32[]{:S(2)}) %collective-permute-start.1) | collective-permute-done | bytes 221216 | tf_op jit(solution)/shard_map/ppermute | solution.py:480
  26.5 1.3 copy-done.4
  27.7 1.3 copy-done.6
  29.0 1.3 copy-done.8
  30.3 9.7 %attn_forward.1 = (bf16[144,768]{1,0:T(8,128)(2,1)S(1)}, bf16[144,768]{1,0:T(8,128)(2,1)S(1)}, bf16[640,768]{1,0:T(8,128)(2,1)S(1)}, bf16[640,768]{1,0:T(8,128)(...) custom-call(bf16[144,768]{1,0:T(8,128)(2,1)S(1)} %pad_maximum_fusion.refs_0_.refs_1_, ...), custom_call_target="tpu_custom_call" | custom-call | tf_op jit(solution)/shard_map/attn_forward/pallas_call | solution.py:38
  40.0 2.3 %copy-done.1 = bf16[3072,768]{1,0:T(8,128)(2,1)S(1)} copy-done((bf16[3072,768]{1,0:T(8,128)(2,1)S(1)}, bf16[3072,768]{1,0:T(8,128)(2,1)}, u32[]{:S(2)}) %copy-start.1) | copy-done | bytes 4718616
  42.4 1.3 copy-done.2
  43.6 4.1 %feed_forward.1 = (bf16[144,768]{1,0:T(8,128)(2,1)}, bf16[144,768]{1,0:T(8,128)(2,1)S(1)}, f32[144,768]{1,0:T(8,128)S(1)}, f32[144,128]{1,0:T(8,128)S(1)}, bf16[...) custom-call(bf16[144,768]{1,0:T(8,128)(2,1)S(1)} %get-tuple-element., ...), custom_call_target="tpu_custom_call" | custom-call | tf_op jit(solution)/shard_map/feed_forward/pallas_call | solution.py:38
  47.7 1.9 outer_terms.1
  49.7 3.6 %feed_back.1 = (bf16[144,3072]{1,0:T(8,128)(2,1)S(1)}, f32[144,768]{1,0:T(8,128)S(1)}, bf16[144,768]{1,0:T(8,128)(2,1)S(1)}, f32[2,768]{1,0:T(2,128)S(1)}) custom-call(bf16[144,768]{1,0:T(8,128)(2,1)S(1)} %get-tuple-element.92.refs_2_.refs_0_, f32[144,768]{1,0:T(8,128)S(1)} %get-tuple-element.93.refs_1_, f32[144,3072]{1,0:T(8,128)S(1)} %get-tuple-element.94.refs_2_, ...), custom_call_target="tpu_custom_call" | custom-call | tf_op jit(solution)/shard_map/feed_back/pallas_call | solution.py:38
  54.5 1.9 inner_terms.1
  56.8 1.5 collective-permute-start.4
  58.3 1.5 collective-permute-start.5
  59.8 8.6 %attn_back0.1 = (bf16[144,384]{1,0:T(8,128)(2,1)S(1)}, bf16[384,640]{1,0:T(8,128)(2,1)S(1)}, bf16[384,640]{1,0:T(8,128)(2,1)S(1)}, f32[16,128]{1,0:T(8,128)S(1)}) custom-call(bf16[144,768]{1,0:T(8,128)(2,1)S(1)} %get-tuple-element.100.refs_2_.refs_4_.refs_0_, bf16[12,144,640]{2,1,0:T(8,128)(2,1)S(1)} %get-tuple-element.101.refs_1_, ...), custom_call_target="tpu_custom_call" | custom-call | tf_op jit(solution)/shard_map/attn_back0/pallas_call | solution.py:38
  68.5 1.5 inner_sum2.1
  69.9 2.3 %collective-permute-done.4.refs_1_ = bf16[2,384,384]{2,1,0:T(8,128)(2,1)S(1)} collective-permute-done((bf16[2,384,384]{2,1,0:T(8,128)(2,1)S(1)}, bf16[2,384,384]{2,1,0:T(8,128)(2,1)S(1)}, u32[]{:S(2)}, u32[]{:S(2)}) %collective-permute-start.4) | collective-permute-done | bytes 589856 | tf_op jit(solution)/shard_map/ppermute | solution.py:480
  76.7 8.4 %attn_back1.1 = (bf16[144,384]{1,0:T(8,128)(2,1)S(1)}, bf16[384,640]{1,0:T(8,128)(2,1)S(1)}, bf16[384,640]{1,0:T(8,128)(2,1)S(1)}, f32[16,128]{1,0:T(8,128)S(1)}) custom-call(bf16[144,768]{1,0:T(8,128)(2,1)S(1)} %get-tuple-element.100.refs_2_.refs_4_.refs_0_, bf16[12,144,640]{2,1,0:T(8,128)(2,1)S(1)} %get-tuple-element.101.refs_1_, ...), custom_call_target="tpu_custom_call" | custom-call | tf_op jit(solution)/shard_map/attn_back1/pallas_call | solution.py:38
  85.2 3.3 %attn_terms.1 = (bf16[4,96,2304]{2,1,0:T(8,128)(2,1)S(1)}, bf16[4,96,2304]{2,1,0:T(8,128)(2,1)}) custom-call(s32[1]{0:T(128)} %bitcast.4.refs_0_, bf16[144,768]{1,0:T(8,128)(2,1)S(1)} %pad_maximum_fusion.refs_0_.refs_1_, bf16[640,768]{1,0:T(8,128)(2,1)S(1)} %get-tuple-element.124.refs_2_, bf16[144,384]{1,0:T(8,128)(2,1)S(1)} %get-tuple-element.111.refs_3_.refs_4_, ...), custom_call_target="tpu_custom_call" | custom-call | tf_op jit(solution)/shard_map/attn_terms/pallas_call | solution.py:38
  89.2 1.5 collective-permute-start.12
  92.1 1.3 copy-done.9
  99.4 4.3 %rows_back.1 = (f32[144,768]{1,0:T(8,128)S(1)}, bf16[144,768]{1,0:T(8,128)(2,1)}, bf16[144,768]{1,0:T(8,128)(2,1)S(1)}, bf16[144,768]{1,0:T(8,128)(2,1)S(1)}) custom-call(f32[144,768]{1,0:T(8,128)S(1)} %copy-done.27, bf16[768,768]{1,0:T(8,128)(2,1)S(1)} %copy-done.5, bf16[768,768]{1,0:T(8,128)(2,1)S(1)} %copy-done.7, bf16[768,768]{1,0:T(8,128)(2,1)S(1)} %copy-done.9, ...), custom_call_target="tpu_custom_call" | custom-call | tf_op jit(solution)/shard_map/rows_back/pallas_call | solution.py:38
  105.1 3.9 %collective-permute-start.7 = (bf16[144,768]{1,0:T(8,128)(2,1)}, bf16[144,768]{1,0:T(8,128)(2,1)}, u32[]{:S(2)}, u32[]{:S(2)}) collective-permute-start(bf16[144,768]{1,0:T(8,128)(2,1)} %get-tuple-element.127), channel_id=1, source_target_pairs={{0,1},{1,0},{2,3},{3,2},{4,5},{5,4},{6,7},{7,6},{8,9},{9,8},{10,11... | collective-permute-start | bytes 663560 | tf_op jit(solution)/shard_map/ppermute | solution.py:480
  109.0 1.6 collective-permute-start.31
  110.5 2.3 %collective-permute-done.31 = f32[40,128]{1,0:T(8,128)S(1)} collective-permute-done((f32[40,128]{1,0:T(8,128)S(1)}, f32[40,128]{1,0:T(8,128)S(1)}, u32[]{:S(2)}, u32[]{:S(2)}) %collective-permute-start.31) | collective-permute-done | bytes 20512 | tf_op jit(solution)/shard_map/ppermute | solution.py:480
  113.3 3.3 %collective-permute-done.32 = f32[40,128]{1,0:T(8,128)S(1)} collective-permute-done((f32[40,128]{1,0:T(8,128)S(1)}, f32[40,128]{1,0:T(8,128)S(1)}, u32[]{:S(2)}, u32[]{:S(2)}) %collective-permute-start.32) | collective-permute-done | bytes 20512 | tf_op jit(solution)/shard_map/ppermute | solution.py:480
  116.6 3.8 %collective-permute-done.33 = f32[40,128]{1,0:T(8,128)S(1)} collective-permute-done((f32[40,128]{1,0:T(8,128)S(1)}, f32[40,128]{1,0:T(8,128)S(1)}, u32[]{:S(2)}, u32[]{:S(2)}) %collective-permute-start.33) | collective-permute-done | bytes 20512 | tf_op jit(solution)/shard_map/ppermute | solution.py:480
  121.4 3.7 %collective-permute-done.34 = f32[40,128]{1,0:T(8,128)S(1)} collective-permute-done((f32[40,128]{1,0:T(8,128)S(1)}, f32[40,128]{1,0:T(8,128)S(1)}, u32[]{:S(2)}, u32[]{:S(2)}) %collective-permute-start.34) | collective-permute-done | bytes 20512 | tf_op jit(solution)/shard_map/ppermute | solution.py:480
  125.6 1.5 collective-permute-start.16
  130.4 1.5 inner_sum1.1
  132.0 1.7 attn_sum2.1
  134.5 1.3 collective-permute-start.14
  136.5 2.5 %collective-permute-done.8 = bf16[144,768]{1,0:T(8,128)(2,1)S(1)} collective-permute-done((bf16[144,768]{1,0:T(8,128)(2,1)}, bf16[144,768]{1,0:T(8,128)(2,1)S(1)}, u32[]{:S(2)}, u32[]{:S(2)}) %collective-permute-start.8) | collective-permute-done | bytes 221216 | tf_op jit(solution)/shard_map/ppermute | solution.py:480
  139.0 3.3 %collective-permute-start.9 = (bf16[144,768]{1,0:T(8,128)(2,1)S(1)}, bf16[144,768]{1,0:T(8,128)(2,1)S(1)}, u32[]{:S(2)}, u32[]{:S(2)}) collective-permute-start(bf16[144,768]{1,0:T(8,128)(2,1)S(1)} %copy-done.33), channel_id=1, source_target_pairs={{0,3},{1,2},{2,1},{3,0},{4,7},{5,6},{6,5},{7,4},{8,11},{9,10},{10,... | collective-permute-start | bytes 663560 | tf_op jit(solution)/shard_map/ppermute | solution.py:480
  142.9 2.4 %collective-permute-start.19 = (bf16[1,96,1920]{2,1,0:T(8,128)(2,1)S(1)}, bf16[1,96,1920]{2,1,0:T(8,128)(2,1)S(1)}, u32[]{:S(2)}, u32[]{:S(2)}) collective-permute-start(bf16[1,96,1920]{2,1,0:T(8,128)(2,1)S(1)} %get-tuple-element.148), channel_id=1, source_target_pairs={{0,16},{4,20},{8,24},{12,28},{16,0},{20,4},{24,8},{28,12},{1,17},{... | collective-permute-start | bytes 1105928 | tf_op jit(solution)/shard_map/ppermute | solution.py:480
  146.1 2.8 %collective-permute-done.9 = bf16[144,768]{1,0:T(8,128)(2,1)S(1)} collective-permute-done((bf16[144,768]{1,0:T(8,128)(2,1)S(1)}, bf16[144,768]{1,0:T(8,128)(2,1)S(1)}, u32[]{:S(2)}, u32[]{:S(2)}) %collective-permute-start.9) | collective-permute-done | bytes 221216 | tf_op jit(solution)/shard_map/ppermute | solution.py:480
  149.0 4.3 %collective-permute-start.28 = (bf16[96,768]{1,0:T(8,128)(2,1)S(1)}, bf16[96,768]{1,0:T(8,128)(2,1)S(1)}, u32[]{:S(2)}, u32[]{:S(2)}) collective-permute-start(bf16[96,768]{1,0:T(8,128)(2,1)S(1)} %get-tuple-element.159), channel_id=1, source_target_pairs={{0,2},{1,3},{2,0},{3,1},{4,6},{5,7},{6,4},{7,5},{8,10},{9,11},{10,... | collective-permute-start | bytes 442376 | tf_op jit(solution)/shard_map/ppermute | solution.py:480
  153.3 1.7 fusion.2
  156.0 3.8 %collective-permute-start.25 = (bf16[24,3840]{1,0:T(8,128)(2,1)S(1)}, bf16[24,3840]{1,0:T(8,128)(2,1)S(1)}, u32[]{:S(2)}, u32[]{:S(2)}) collective-permute-start(bf16[24,3840]{1,0:T(8,128)(2,1)S(1)} %get-tuple-element.156), channel_id=1, source_target_pairs={{0,2},{1,3},{2,0},{3,1},{4,6},{5,7},{6,4},{7,5},{8,10},{9,11},{10,... | collective-permute-start | bytes 552968 | tf_op jit(solution)/shard_map/ppermute | solution.py:480
  159.9 4.2 %collective-permute-done.28 = bf16[96,768]{1,0:T(8,128)(2,1)S(1)} collective-permute-done((bf16[96,768]{1,0:T(8,128)(2,1)S(1)}, bf16[96,768]{1,0:T(8,128)(2,1)S(1)}, u32[]{:S(2)}, u32[]{:S(2)}) %collective-permute-start.28) | collective-permute-done | bytes 147488 | tf_op jit(solution)/shard_map/ppermute | solution.py:480
  164.1 6.0 %collective-permute-start.17 = (bf16[1,96,1152]{2,1,0:T(8,128)(2,1)S(1)}, bf16[1,96,1152]{2,1,0:T(8,128)(2,1)S(1)}, u32[]{:S(2)}, u32[]{:S(2)}) collective-permute-start(bf16[1,96,1152]{2,1,0:T(8,128)(2,1)S(1)} %get-tuple-element.144), channel_id=1, source_target_pairs={{0,16},{4,20},{8,24},{12,28},{16,0},{20,4},{24,8},{28,12},{1,17},{... | collective-permute-start | bytes 663560 | tf_op jit(solution)/shard_map/ppermute | solution.py:480
  170.9 3.1 %collective-permute-done.17 = bf16[1,96,1152]{2,1,0:T(8,128)(2,1)S(1)} collective-permute-done((bf16[1,96,1152]{2,1,0:T(8,128)(2,1)S(1)}, bf16[1,96,1152]{2,1,0:T(8,128)(2,1)S(1)}, u32[]{:S(2)}, u32[]{:S(2)}) %collective-permute-start.17) | collective-permute-done | bytes 221216 | tf_op jit(solution)/shard_map/ppermute | solution.py:480
  174.0 2.0 %collective-permute-done.18 = bf16[1,96,1152]{2,1,0:T(8,128)(2,1)S(1)} collective-permute-done((bf16[1,96,1152]{2,1,0:T(8,128)(2,1)S(1)}, bf16[1,96,1152]{2,1,0:T(8,128)(2,1)S(1)}, u32[]{:S(2)}, u32[]{:S(2)}) %collective-permute-start.18) | collective-permute-done | bytes 221216 | tf_op jit(solution)/shard_map/ppermute | solution.py:480
  176.1 4.1 %collective-permute-start.21 = (bf16[24,2304]{1,0:T(8,128)(2,1)S(1)}, bf16[24,2304]{1,0:T(8,128)(2,1)S(1)}, u32[]{:S(2)}, u32[]{:S(2)}) collective-permute-start(bf16[24,2304]{1,0:T(8,128)(2,1)S(1)} %get-tuple-element.152), channel_id=1, source_target_pairs={{0,1},{1,0},{2,3},{3,2},{4,5},{5,4},{6,7},{7,6},{8,9},{9,8},{10,11... | collective-permute-start | bytes 331784 | tf_op jit(solution)/shard_map/ppermute | solution.py:480
  180.2 1.4 collective-permute-start.22
  181.6 1.4 collective-permute-start.23
  184.5 3.8 %collective-permute-done.22 = bf16[24,2304]{1,0:T(8,128)(2,1)S(1)} collective-permute-done((bf16[24,2304]{1,0:T(8,128)(2,1)S(1)}, bf16[24,2304]{1,0:T(8,128)(2,1)S(1)}, u32[]{:S(2)}, u32[]{:S(2)}) %collective-permute-start.22) | collective-permute-done | bytes 110624 | tf_op jit(solution)/shard_map/ppermute | solution.py:480
  (159 shorter events, 38.8 us)
Async XLA Ops:
  3.5 46.1 %slice-start = ((s8[4718592]{0:T(1024)(128)(4,1)}), s8[524288]{0:T(1024)(128)(4,1)S(1)}, s32[]{:S(2)}) async-start(s8[4718592]{0:T(1024)(128)(4,1)} %bitcast.27), calls=%async_computation | async-start | bytes 1048576
  4.6 12.5 %collective-permute-start = (bf16[144,768]{1,0:T(8,128)(2,1)S(1)}, bf16[144,768]{1,0:T(8,128)(2,1)S(1)}, u32[]{:S(2)}, u32[]{:S(2)}) collective-permute-start(bf16[144,768]{1,0:T(8,128)(2,1)S(1)} %pad_maximum_fusion.refs_0_.refs_1_), channel_id=1, source_target_pairs={{0,1},{1,0},{2,3},{3,2},{4,5},{5,4},{6,7},{7,6},{8,9},{9,8},{10,11... | collective-permute-start | bytes 663560 | tf_op jit(solution)/shard_map/ppermute | solution.py:480
  7.7 18.7 %collective-permute-start.1 = (bf16[144,768]{1,0:T(8,128)(2,1)S(1)}, bf16[144,768]{1,0:T(8,128)(2,1)S(1)}, u32[]{:S(2)}, u32[]{:S(2)}) collective-permute-start(bf16[144,768]{1,0:T(8,128)(2,1)S(1)} %pad_maximum_fusion.refs_0_.refs_1_), channel_id=1, source_target_pairs={{0,2},{1,3},{2,0},{3,1},{4,6},{5,7},{6,4},{7,5},{8,10},{9,11},{10,... | collective-permute-start | bytes 663560 | tf_op jit(solution)/shard_map/ppermute | solution.py:480
  10.3 16.1 %collective-permute-start.2 = (bf16[144,768]{1,0:T(8,128)(2,1)S(1)}, bf16[144,768]{1,0:T(8,128)(2,1)S(1)}, u32[]{:S(2)}, u32[]{:S(2)}) collective-permute-start(bf16[144,768]{1,0:T(8,128)(2,1)S(1)} %pad_maximum_fusion.refs_0_.refs_1_), channel_id=1, source_target_pairs={{0,3},{1,2},{2,1},{3,0},{4,7},{5,6},{6,5},{7,4},{8,11},{9,10},{10,... | collective-permute-start | bytes 663560 | tf_op jit(solution)/shard_map/ppermute | solution.py:480
  14.9 25.1 %copy-start = (bf16[768,3072]{1,0:T(8,128)(2,1)S(1)}, bf16[768,3072]{1,0:T(8,128)(2,1)}, u32[]{:S(2)}) copy-start(bf16[768,3072]{1,0:T(8,128)(2,1)} %refs_5_.5) | copy-start | bytes 14155780
  43.6 6.0 %slice-start.1 = ((s8[4718592]{0:T(1024)(128)(4,1)}), s8[4194304]{0:T(1024)(128)(4,1)S(1)}, s32[]{:S(2)}) async-start(s8[4718592]{0:T(1024)(128)(4,1)} %bitcast.27), calls=%async_computation.1 | async-start | bytes 8388608
  49.6 4.6 %collective-permute-start.3 = (bf16[4,384,768]{2,1,0:T(8,128)(2,1)S(1)}, bf16[4,384,768]{2,1,0:T(8,128)(2,1)S(1)}, u32[]{:S(2)}, u32[]{:S(2)}) collective-permute-start(bf16[4,384,768]{2,1,0:T(8,128)(2,1)S(1)} %get-tuple-element.108), channel_id=1, source_target_pairs={{0,4},{4,0},{8,12},{12,8},{16,20},{20,16},{24,28},{28,24},{1,5},{5... | collective-permute-start | bytes 7077896 | tf_op jit(solution)/shard_map/ppermute | solution.py:480
  54.5 5.3 %copy-start.3 = (bf16[768,768]{1,0:T(8,128)(2,1)S(1)}, bf16[768,768]{1,0:T(8,128)(2,1)}, u32[]{:S(2)}) copy-start(bf16[768,768]{1,0:T(8,128)(2,1)} %refs_5_.7) | copy-start | bytes 3538948
  56.4 12.0 %collective-permute-start.6 = (bf16[4,96,3840]{2,1,0:T(8,128)(2,1)S(1)}, bf16[4,96,3840]{2,1,0:T(8,128)(2,1)S(1)}, u32[]{:S(2)}, u32[]{:S(2)}) collective-permute-start(bf16[4,96,3840]{2,1,0:T(8,128)(2,1)S(1)} %get-tuple-element.117), channel_id=1, source_target_pairs={{0,4},{4,0},{8,12},{12,8},{16,20},{20,16},{24,28},{28,24},{1,5},{5... | collective-permute-start | bytes 8847368 | tf_op jit(solution)/shard_map/ppermute | solution.py:480
  56.8 15.4 %collective-permute-start.4 = (bf16[2,384,384]{2,1,0:T(8,128)(2,1)S(1)}, bf16[2,384,384]{2,1,0:T(8,128)(2,1)S(1)}, u32[]{:S(2)}, u32[]{:S(2)}) collective-permute-start(bf16[2,384,384]{2,1,0:T(8,128)(2,1)S(1)} %get-tuple-element.115), channel_id=1, source_target_pairs={{0,8},{4,12},{8,0},{12,4},{16,24},{20,28},{24,16},{28,20},{1,9},{5... | collective-permute-start | bytes 1769480 | tf_op jit(solution)/shard_map/ppermute | solution.py:480
  58.3 15.1 %collective-permute-start.5 = (bf16[2,384,384]{2,1,0:T(8,128)(2,1)S(1)}, bf16[2,384,384]{2,1,0:T(8,128)(2,1)S(1)}, u32[]{:S(2)}, u32[]{:S(2)}) collective-permute-start(bf16[2,384,384]{2,1,0:T(8,128)(2,1)S(1)} %get-tuple-element.116), channel_id=1, source_target_pairs={{0,16},{4,20},{8,24},{12,28},{16,0},{20,4},{24,8},{28,12},{1,17},{... | collective-permute-start | bytes 1769480 | tf_op jit(solution)/shard_map/ppermute | solution.py:480
  68.4 16.7 %copy-start.12 = (bf16[384,640]{1,0:T(8,128)(2,1)}, bf16[384,640]{1,0:T(8,128)(2,1)S(1)}, u32[]{:S(2)}) copy-start(bf16[384,640]{1,0:T(8,128)(2,1)S(1)} %get-tuple-element.112.refs_5_) | copy-start | bytes 1474564
  68.4 16.7 %copy-start.14 = (bf16[384,640]{1,0:T(8,128)(2,1)}, bf16[384,640]{1,0:T(8,128)(2,1)S(1)}, u32[]{:S(2)}) copy-start(bf16[384,640]{1,0:T(8,128)(2,1)S(1)} %get-tuple-element.113.refs_7_.refs_6_) | copy-start | bytes 1474564
  69.9 15.1 %copy-start.22 = (bf16[2,96,1920]{2,1,0:T(8,128)(2,1)}, bf16[2,96,1920]{2,1,0:T(8,128)(2,1)S(1)}, u32[]{:S(2)}) copy-start(bf16[2,96,1920]{2,1,0:T(8,128)(2,1)S(1)} %get-tuple-element.131.refs_0_) | copy-start | bytes 2211844
  76.0 9.1 %copy-start.20 = (bf16[1,384,384]{2,1,0:T(8,128)(2,1)}, bf16[1,384,384]{2,1,0:T(8,128)(2,1)S(1)}, u32[]{:S(2)}) copy-start(bf16[1,384,384]{2,1,0:T(8,128)(2,1)S(1)} %get-tuple-element.120.refs_8_) | copy-start | bytes 884740
  85.1 3.5 %copy-start.24 = (bf16[144,384]{1,0:T(8,128)(2,1)}, bf16[144,384]{1,0:T(8,128)(2,1)S(1)}, u32[]{:S(2)}) copy-start(bf16[144,384]{1,0:T(8,128)(2,1)S(1)} %get-tuple-element.121.refs_4_.refs_7_) | copy-start | bytes 331780
  85.1 5.7 %copy-start.5 = (bf16[768,768]{1,0:T(8,128)(2,1)S(1)}, bf16[768,768]{1,0:T(8,128)(2,1)}, u32[]{:S(2)}) copy-start(bf16[768,768]{1,0:T(8,128)(2,1)} %refs_1_.1) | copy-start | bytes 3538948
  88.5 43.5 %collective-permute-start.10 = (bf16[4,96,2304]{2,1,0:T(8,128)(2,1)}, bf16[4,96,2304]{2,1,0:T(8,128)(2,1)}, u32[]{:S(2)}, u32[]{:S(2)}) collective-permute-start(bf16[4,96,2304]{2,1,0:T(8,128)(2,1)} %get-tuple-element.130), channel_id=1, source_target_pairs={{0,4},{4,0},{8,12},{12,8},{16,20},{20,16},{24,28},{28,24},{1,5},{5... | collective-permute-start | bytes 5308424 | tf_op jit(solution)/shard_map/ppermute | solution.py:480
  88.6 37.0 %collective-permute-start.11 = (bf16[2,96,1920]{2,1,0:T(8,128)(2,1)}, bf16[2,96,1920]{2,1,0:T(8,128)(2,1)}, u32[]{:S(2)}, u32[]{:S(2)}) collective-permute-start(bf16[2,96,1920]{2,1,0:T(8,128)(2,1)} %get-tuple-element.132), channel_id=1, source_target_pairs={{0,8},{4,12},{8,0},{12,4},{16,24},{20,28},{24,16},{28,20},{1,9},{5... | collective-permute-start | bytes 2211848 | tf_op jit(solution)/shard_map/ppermute | solution.py:480
  89.2 38.0 %collective-permute-start.12 = (bf16[2,96,1920]{2,1,0:T(8,128)(2,1)}, bf16[2,96,1920]{2,1,0:T(8,128)(2,1)}, u32[]{:S(2)}, u32[]{:S(2)}) collective-permute-start(bf16[2,96,1920]{2,1,0:T(8,128)(2,1)} %get-tuple-element.133), channel_id=1, source_target_pairs={{0,16},{4,20},{8,24},{12,28},{16,0},{20,4},{24,8},{28,12},{1,17},{... | collective-permute-start | bytes 2211848 | tf_op jit(solution)/shard_map/ppermute | solution.py:480
  90.7 18.2 %collective-permute-start.30 = (f32[40,128]{1,0:T(8,128)S(1)}, f32[40,128]{1,0:T(8,128)S(1)}, u32[]{:S(2)}, u32[]{:S(2)}) collective-permute-start(f32[40,128]{1,0:T(8,128)S(1)} %pad_maximum_fusion.1), channel_id=1, source_target_pairs={{0,4},{4,0},{8,12},{12,8},{16,20},{20,16},{24,28},{28,24},{1,5},{5... | collective-permute-start | bytes 61448 | tf_op jit(solution)/shard_map/ppermute | solution.py:480
  105.1 29.4 %collective-permute-start.7 = (bf16[144,768]{1,0:T(8,128)(2,1)}, bf16[144,768]{1,0:T(8,128)(2,1)}, u32[]{:S(2)}, u32[]{:S(2)}) collective-permute-start(bf16[144,768]{1,0:T(8,128)(2,1)} %get-tuple-element.127), channel_id=1, source_target_pairs={{0,1},{1,0},{2,3},{3,2},{4,5},{5,4},{6,7},{7,6},{8,9},{9,8},{10,11... | collective-permute-start | bytes 663560 | tf_op jit(solution)/shard_map/ppermute | solution.py:480
  109.0 3.8 %collective-permute-start.31 = (f32[40,128]{1,0:T(8,128)S(1)}, f32[40,128]{1,0:T(8,128)S(1)}, u32[]{:S(2)}, u32[]{:S(2)}) collective-permute-start(f32[40,128]{1,0:T(8,128)S(1)} %fusion.17), channel_id=1, source_target_pairs={{0,8},{4,12},{8,0},{12,4},{16,24},{20,28},{24,16},{28,20},{1,9},{5... | collective-permute-start | bytes 61448 | tf_op jit(solution)/shard_map/ppermute | solution.py:480
  112.8 3.8 %collective-permute-start.32 = (f32[40,128]{1,0:T(8,128)S(1)}, f32[40,128]{1,0:T(8,128)S(1)}, u32[]{:S(2)}, u32[]{:S(2)}) collective-permute-start(f32[40,128]{1,0:T(8,128)S(1)} %add.102), channel_id=1, source_target_pairs={{0,16},{4,20},{8,24},{12,28},{16,0},{20,4},{24,8},{28,12},{1,17},{... | collective-permute-start | bytes 61448 | tf_op jit(solution)/shard_map/ppermute | solution.py:480
  116.6 3.8 %collective-permute-start.33 = (f32[40,128]{1,0:T(8,128)S(1)}, f32[40,128]{1,0:T(8,128)S(1)}, u32[]{:S(2)}, u32[]{:S(2)}) collective-permute-start(f32[40,128]{1,0:T(8,128)S(1)} %add.103), channel_id=1, source_target_pairs={{0,1},{1,0},{2,3},{3,2},{4,5},{5,4},{6,7},{7,6},{8,9},{9,8},{10,11... | collective-permute-start | bytes 61448 | tf_op jit(solution)/shard_map/ppermute | solution.py:480
  120.4 4.7 %collective-permute-start.34 = (f32[40,128]{1,0:T(8,128)S(1)}, f32[40,128]{1,0:T(8,128)S(1)}, u32[]{:S(2)}, u32[]{:S(2)}) collective-permute-start(f32[40,128]{1,0:T(8,128)S(1)} %add.104), channel_id=1, source_target_pairs={{0,2},{1,3},{2,0},{3,1},{4,6},{5,7},{6,4},{7,5},{8,10},{9,11},{10,... | collective-permute-start | bytes 61448 | tf_op jit(solution)/shard_map/ppermute | solution.py:480
  125.1 17.8 %collective-permute-start.15 = (bf16[1,384,384]{2,1,0:T(8,128)(2,1)}, bf16[1,384,384]{2,1,0:T(8,128)(2,1)S(1)}, u32[]{:S(2)}, u32[]{:S(2)}) collective-permute-start(bf16[1,384,384]{2,1,0:T(8,128)(2,1)} %copy-done.31), channel_id=1, source_target_pairs={{0,16},{4,20},{8,24},{12,28},{16,0},{20,4},{24,8},{28,12},{1,17},{... | collective-permute-start | bytes 884744 | tf_op jit(solution)/shard_map/ppermute | solution.py:480
  125.6 19.7 %collective-permute-start.16 = (bf16[1,384,384]{2,1,0:T(8,128)(2,1)}, bf16[1,384,384]{2,1,0:T(8,128)(2,1)S(1)}, u32[]{:S(2)}, u32[]{:S(2)}) collective-permute-start(bf16[1,384,384]{2,1,0:T(8,128)(2,1)} %copy-done.30), channel_id=1, source_target_pairs={{0,8},{4,12},{8,0},{12,4},{16,24},{20,28},{24,16},{28,20},{1,9},{5... | collective-permute-start | bytes 884744 | tf_op jit(solution)/shard_map/ppermute | solution.py:480
  127.2 11.8 %collective-permute-start.8 = (bf16[144,768]{1,0:T(8,128)(2,1)}, bf16[144,768]{1,0:T(8,128)(2,1)S(1)}, u32[]{:S(2)}, u32[]{:S(2)}) collective-permute-start(bf16[144,768]{1,0:T(8,128)(2,1)} %copy-done.34), channel_id=1, source_target_pairs={{0,2},{1,3},{2,0},{3,1},{4,6},{5,7},{6,4},{7,5},{8,10},{9,11},{10,... | collective-permute-start | bytes 663560 | tf_op jit(solution)/shard_map/ppermute | solution.py:480
  131.9 7.1 %copy-start.33 = (bf16[144,768]{1,0:T(8,128)(2,1)S(1)}, bf16[144,768]{1,0:T(8,128)(2,1)}, u32[]{:S(2)}) copy-start(bf16[144,768]{1,0:T(8,128)(2,1)} %copy-done.32) | copy-start | bytes 663556
  131.9 14.1 %copy-start.21 = (bf16[1,384,384]{2,1,0:T(8,128)(2,1)S(1)}, bf16[1,384,384]{2,1,0:T(8,128)(2,1)}, u32[]{:S(2)}) copy-start(bf16[1,384,384]{2,1,0:T(8,128)(2,1)} %copy-done.20) | copy-start | bytes 884740
  131.9 14.1 %copy-start.29 = (bf16[1,384,384]{2,1,0:T(8,128)(2,1)S(1)}, bf16[1,384,384]{2,1,0:T(8,128)(2,1)}, u32[]{:S(2)}) copy-start(bf16[1,384,384]{2,1,0:T(8,128)(2,1)} %copy-done.28) | copy-start | bytes 884740
  133.7 15.3 %collective-permute-start.13 = (bf16[2,96,1152]{2,1,0:T(8,128)(2,1)S(1)}, bf16[2,96,1152]{2,1,0:T(8,128)(2,1)S(1)}, u32[]{:S(2)}, u32[]{:S(2)}) collective-permute-start(bf16[2,96,1152]{2,1,0:T(8,128)(2,1)S(1)} %get-tuple-element.136), channel_id=1, source_target_pairs={{0,8},{4,12},{8,0},{12,4},{16,24},{20,28},{24,16},{28,20},{1,9},{5... | collective-permute-start | bytes 1327112 | tf_op jit(solution)/shard_map/ppermute | solution.py:480
  134.5 18.7 %collective-permute-start.14 = (bf16[2,96,1152]{2,1,0:T(8,128)(2,1)S(1)}, bf16[2,96,1152]{2,1,0:T(8,128)(2,1)S(1)}, u32[]{:S(2)}, u32[]{:S(2)}) collective-permute-start(bf16[2,96,1152]{2,1,0:T(8,128)(2,1)S(1)} %get-tuple-element.138), channel_id=1, source_target_pairs={{0,16},{4,20},{8,24},{12,28},{16,0},{20,4},{24,8},{28,12},{1,17},{... | collective-permute-start | bytes 1327112 | tf_op jit(solution)/shard_map/ppermute | solution.py:480
  139.0 10.0 %collective-permute-start.9 = (bf16[144,768]{1,0:T(8,128)(2,1)S(1)}, bf16[144,768]{1,0:T(8,128)(2,1)S(1)}, u32[]{:S(2)}, u32[]{:S(2)}) collective-permute-start(bf16[144,768]{1,0:T(8,128)(2,1)S(1)} %copy-done.33), channel_id=1, source_target_pairs={{0,3},{1,2},{2,1},{3,0},{4,7},{5,6},{6,5},{7,4},{8,11},{9,10},{10,... | collective-permute-start | bytes 663560 | tf_op jit(solution)/shard_map/ppermute | solution.py:480
  142.9 12.3 %collective-permute-start.19 = (bf16[1,96,1920]{2,1,0:T(8,128)(2,1)S(1)}, bf16[1,96,1920]{2,1,0:T(8,128)(2,1)S(1)}, u32[]{:S(2)}, u32[]{:S(2)}) collective-permute-start(bf16[1,96,1920]{2,1,0:T(8,128)(2,1)S(1)} %get-tuple-element.148), channel_id=1, source_target_pairs={{0,16},{4,20},{8,24},{12,28},{16,0},{20,4},{24,8},{28,12},{1,17},{... | collective-permute-start | bytes 1105928 | tf_op jit(solution)/shard_map/ppermute | solution.py:480
  145.3 9.9 %collective-permute-start.20 = (bf16[1,96,1920]{2,1,0:T(8,128)(2,1)S(1)}, bf16[1,96,1920]{2,1,0:T(8,128)(2,1)S(1)}, u32[]{:S(2)}, u32[]{:S(2)}) collective-permute-start(bf16[1,96,1920]{2,1,0:T(8,128)(2,1)S(1)} %get-tuple-element.149), channel_id=1, source_target_pairs={{0,8},{4,12},{8,0},{12,4},{16,24},{20,28},{24,16},{28,20},{1,9},{5... | collective-permute-start | bytes 1105928 | tf_op jit(solution)/shard_map/ppermute | solution.py:480
  149.0 10.8 %collective-permute-start.27 = (bf16[96,768]{1,0:T(8,128)(2,1)S(1)}, bf16[96,768]{1,0:T(8,128)(2,1)S(1)}, u32[]{:S(2)}, u32[]{:S(2)}) collective-permute-start(bf16[96,768]{1,0:T(8,128)(2,1)S(1)} %get-tuple-element.158), channel_id=1, source_target_pairs={{0,1},{1,0},{2,3},{3,2},{4,5},{5,4},{6,7},{7,6},{8,9},{9,8},{10,11... | collective-permute-start | bytes 442376 | tf_op jit(solution)/shard_map/ppermute | solution.py:480
  149.0 15.2 %collective-permute-start.28 = (bf16[96,768]{1,0:T(8,128)(2,1)S(1)}, bf16[96,768]{1,0:T(8,128)(2,1)S(1)}, u32[]{:S(2)}, u32[]{:S(2)}) collective-permute-start(bf16[96,768]{1,0:T(8,128)(2,1)S(1)} %get-tuple-element.159), channel_id=1, source_target_pairs={{0,2},{1,3},{2,0},{3,1},{4,6},{5,7},{6,4},{7,5},{8,10},{9,11},{10,... | collective-permute-start | bytes 442376 | tf_op jit(solution)/shard_map/ppermute | solution.py:480
  153.2 16.8 %collective-permute-start.29 = (bf16[96,768]{1,0:T(8,128)(2,1)S(1)}, bf16[96,768]{1,0:T(8,128)(2,1)S(1)}, u32[]{:S(2)}, u32[]{:S(2)}) collective-permute-start(bf16[96,768]{1,0:T(8,128)(2,1)S(1)} %get-tuple-element.160), channel_id=1, source_target_pairs={{0,3},{1,2},{2,1},{3,0},{4,7},{5,6},{6,5},{7,4},{8,11},{9,10},{10,... | collective-permute-start | bytes 442376 | tf_op jit(solution)/shard_map/ppermute | solution.py:480
  155.4 26.2 %collective-permute-start.24 = (bf16[24,3840]{1,0:T(8,128)(2,1)S(1)}, bf16[24,3840]{1,0:T(8,128)(2,1)S(1)}, u32[]{:S(2)}, u32[]{:S(2)}) collective-permute-start(bf16[24,3840]{1,0:T(8,128)(2,1)S(1)} %get-tuple-element.155), channel_id=1, source_target_pairs={{0,1},{1,0},{2,3},{3,2},{4,5},{5,4},{6,7},{7,6},{8,9},{9,8},{10,11... | collective-permute-start | bytes 552968 | tf_op jit(solution)/shard_map/ppermute | solution.py:480
  156.0 27.0 %collective-permute-start.25 = (bf16[24,3840]{1,0:T(8,128)(2,1)S(1)}, bf16[24,3840]{1,0:T(8,128)(2,1)S(1)}, u32[]{:S(2)}, u32[]{:S(2)}) collective-permute-start(bf16[24,3840]{1,0:T(8,128)(2,1)S(1)} %get-tuple-element.156), channel_id=1, source_target_pairs={{0,2},{1,3},{2,0},{3,1},{4,6},{5,7},{6,4},{7,5},{8,10},{9,11},{10,... | collective-permute-start | bytes 552968 | tf_op jit(solution)/shard_map/ppermute | solution.py:480
  159.8 23.2 %collective-permute-start.26 = (bf16[24,3840]{1,0:T(8,128)(2,1)S(1)}, bf16[24,3840]{1,0:T(8,128)(2,1)S(1)}, u32[]{:S(2)}, u32[]{:S(2)}) collective-permute-start(bf16[24,3840]{1,0:T(8,128)(2,1)S(1)} %get-tuple-element.157), channel_id=1, source_target_pairs={{0,3},{1,2},{2,1},{3,0},{4,7},{5,6},{6,5},{7,4},{8,11},{9,10},{10,... | collective-permute-start | bytes 552968 | tf_op jit(solution)/shard_map/ppermute | solution.py:480
  164.1 9.9 %collective-permute-start.17 = (bf16[1,96,1152]{2,1,0:T(8,128)(2,1)S(1)}, bf16[1,96,1152]{2,1,0:T(8,128)(2,1)S(1)}, u32[]{:S(2)}, u32[]{:S(2)}) collective-permute-start(bf16[1,96,1152]{2,1,0:T(8,128)(2,1)S(1)} %get-tuple-element.144), channel_id=1, source_target_pairs={{0,16},{4,20},{8,24},{12,28},{16,0},{20,4},{24,8},{28,12},{1,17},{... | collective-permute-start | bytes 663560 | tf_op jit(solution)/shard_map/ppermute | solution.py:480
  170.1 5.9 %collective-permute-start.18 = (bf16[1,96,1152]{2,1,0:T(8,128)(2,1)S(1)}, bf16[1,96,1152]{2,1,0:T(8,128)(2,1)S(1)}, u32[]{:S(2)}, u32[]{:S(2)}) collective-permute-start(bf16[1,96,1152]{2,1,0:T(8,128)(2,1)S(1)} %get-tuple-element.146), channel_id=1, source_target_pairs={{0,8},{4,12},{8,0},{12,4},{16,24},{20,28},{24,16},{28,20},{1,9},{5... | collective-permute-start | bytes 663560 | tf_op jit(solution)/shard_map/ppermute | solution.py:480
  176.1 8.3 %collective-permute-start.21 = (bf16[24,2304]{1,0:T(8,128)(2,1)S(1)}, bf16[24,2304]{1,0:T(8,128)(2,1)S(1)}, u32[]{:S(2)}, u32[]{:S(2)}) collective-permute-start(bf16[24,2304]{1,0:T(8,128)(2,1)S(1)} %get-tuple-element.152), channel_id=1, source_target_pairs={{0,1},{1,0},{2,3},{3,2},{4,5},{5,4},{6,7},{7,6},{8,9},{9,8},{10,11... | collective-permute-start | bytes 331784 | tf_op jit(solution)/shard_map/ppermute | solution.py:480
  180.2 8.0 %collective-permute-start.22 = (bf16[24,2304]{1,0:T(8,128)(2,1)S(1)}, bf16[24,2304]{1,0:T(8,128)(2,1)S(1)}, u32[]{:S(2)}, u32[]{:S(2)}) collective-permute-start(bf16[24,2304]{1,0:T(8,128)(2,1)S(1)} %get-tuple-element.153), channel_id=1, source_target_pairs={{0,2},{1,3},{2,0},{3,1},{4,6},{5,7},{6,4},{7,5},{8,10},{9,11},{10,... | collective-permute-start | bytes 331784 | tf_op jit(solution)/shard_map/ppermute | solution.py:480
  181.6 6.6 %collective-permute-start.23 = (bf16[24,2304]{1,0:T(8,128)(2,1)S(1)}, bf16[24,2304]{1,0:T(8,128)(2,1)S(1)}, u32[]{:S(2)}, u32[]{:S(2)}) collective-permute-start(bf16[24,2304]{1,0:T(8,128)(2,1)S(1)} %get-tuple-element.154), channel_id=1, source_target_pairs={{0,3},{1,2},{2,1},{3,0},{4,7},{5,6},{6,5},{7,4},{8,11},{9,10},{10,... | collective-permute-start | bytes 331784 | tf_op jit(solution)/shard_map/ppermute | solution.py:480
  (24 other events, 30.1 us)
where the time goes:
time: 190 us; the launch traced here: 189 us
  Pallas kernels  51.6 us (27%)
  starting transfers between devices  50.9 us (27%)
  waiting for transfers between devices  44.6 us (23%)
  local copies, waits for them, and re-layouts  31.5 us (17%)
  other arithmetic  9.33 us (5%)
    pallas_call x18, Pallas kernels, launch(): pl.pallas_call(body, out_shape=out_shape, in_specs=in_specs + [pl.BlockSp...  51.6 us
    ppermute x35, starting transfers between devices, swap(): lax.ppermute(array_in, axis_name, [(at, at ^ flip) for at in range(size)])  50.9 us
    ppermute x35, waiting for transfers between devices, swap(): lax.ppermute(array_in, axis_name, [(at, at ^ flip) for at in range(size)])  44.6 us
    unnamed x74, local copies, waits for them, and re-layouts  23.4 us
    another operation x5, other arithmetic  4.47 us
  transfers between devices with their start and end apart: 35, of which 15 were waited for; matrix products, arithmetic and copies ran while one was open for 7% of the time, Pallas kernels for 12%

commit v1 on v0

--- a/solution.py
+++ b/solution.py
@@ -21,29 +21,59 @@
     return pl.BlockSpec(memory_space=pltpu.VMEM)
 
 
-def smem():
-    return pl.BlockSpec(memory_space=pltpu.SMEM)
-
-
 def like(shape, kind):
     return jax.ShapeDtypeStruct(shape, kind)
 
 
-def launch(kernel, operands, in_specs, name, limit, out_shape, scratch_shapes=(), after=()):
-    count = len(operands)
-
-    def body(*refs):
-        kernel(*refs[:count], *refs[count + len(after) :])
+class Later:
+    def __init__(self, stage, index):
+        self.stage, self.index = stage, index
+        self.shape, self.dtype = stage.outs[index].shape, stage.outs[index].dtype
+
+
+class Stage:
+    def __init__(self, body, operands, specs, outs, scratch=()):
+        self.body, self.operands, self.specs = body, list(operands), list(specs)
+        self.outs, self.scratch = list(outs), list(scratch)
+        self.results = [Later(self, index) for index in range(len(self.outs))]
+
+
+def run(stages, name, limit, after=()):
+    arrays, specs, place = [], [], {}
+    for stage in stages:
+        for operand, spec in zip(stage.operands, stage.specs):
+            if not isinstance(operand, Later) and id(operand) not in place:
+                place[id(operand)] = len(arrays)
+                arrays.append(operand)
+                specs.append(spec)
+    out_shape = [out for stage in stages for out in stage.outs]
+
+    def kernel(*refs):
+        ins = refs[: len(arrays)]
+        outs = list(refs[len(arrays) + len(after) :][: len(out_shape)])
+        scratch = list(refs[len(arrays) + len(after) + len(out_shape) :])
+        given = {}
+        for stage in stages:
+            own = [outs.pop(0) for _ in stage.outs]
+            spare = [scratch.pop(0) for _ in stage.scratch]
+            given[id(stage)] = own
+            read = [
+                given[id(item.stage)][item.index]
+                if isinstance(item, Later)
+                else ins[place[id(item)]]
+                for item in stage.operands
+            ]
+            stage.body(*read, *own, *spare)
 
     return pl.pallas_call(
-        body,
-        out_shape=out_shape,
-        in_specs=in_specs + [pl.BlockSpec(memory_space=pl.ANY)] * len(after),
+        kernel,
+        out_shape=tuple(out_shape),
+        in_specs=specs + [pl.BlockSpec(memory_space=pl.ANY)] * len(after),
         out_specs=[vmem()] * len(out_shape),
-        scratch_shapes=list(scratch_shapes),
+        scratch_shapes=[item for stage in stages for item in stage.scratch],
         compiler_params=pltpu.CompilerParams(vmem_limit_bytes=limit * MIB),
         name=name,
-    )(*operands, *after)
+    )(*arrays, *after)
 
 
 def dot_nn(left, right):
@@ -79,9 +109,7 @@
     return jnp.where(key_at[4:5, :] > 0, bucket + same, 2 * REL)
 
 
-def attn_forward(
-    token_shards, row_count, w_query, w_key, w_value, line_table, box_table, query_at
-):
+def attn_forward(token_shards, row_count, weights, line_table, box_table, query_at):
     rows, width = token_shards[0].shape
     head_count = line_table.shape[0]
     shards = len(token_shards)
@@ -89,10 +117,9 @@
 
     def kernel(*refs):
         tok_refs = refs[:shards]
-        wq, wk, wv, line_ref, box_ref, q_at = refs[shards : shards + 6]
-        mix_ref, q_ref, k_ref, v_ref, x_ref, p_ref, k_at, line_idx, box_idx, hots = refs[
-            shards + 6 :
-        ]
+        wk, wv, wq, line_ref, box_ref, q_at = refs[shards : shards + 6]
+        mix_ref, q_ref, k_ref, v_ref, x_ref, p_ref, k_at = refs[shards + 6 : shards + 13]
+        line_idx, box_idx, hots = refs[shards + 13 :]
         places = [jnp.zeros((16, keys), F32)] * 3
         for at in range(shards):
             info = tok_refs[at][rows - 16 :, :].astype(F32)
@@ -114,9 +141,9 @@
             x_ref[at * rows : (at + 1) * rows] = tok_refs[at][...]
         if keys > shards * rows:
             x_ref[shards * rows :] = jnp.zeros((keys - shards * rows, width), BF)
-        q_ref[...] = (dot_nn(tok_refs[0][...], wq[...]) * 0.125).astype(BF)
         k_ref[...] = dot_nn(x_ref[...], wk[...]).astype(BF)
         v_ref[...] = dot_nn(x_ref[...], wv[...]).astype(BF)
+        q_ref[...] = (dot_nn(tok_refs[0][...], wq[...]) * 0.125).astype(BF)
         line_idx[...] = line_index(q_at, k_at)
         lane = lax.broadcasted_iota(I32, (rows, LANES), 1)
         place = jnp.where(lane < BOXES, q_at[:, 2:3], q_at[:, 3:4])
@@ -156,12 +183,10 @@
 
         lax.fori_loop(0, width // LANES, pair, 0)
 
-    return launch(
+    return Stage(
         kernel,
-        (*token_shards, w_query, w_key, w_value, line_table, box_table, query_at),
+        (*token_shards, *weights, line_table, box_table, query_at),
         [vmem()] * (shards + 6),
-        "attn_forward",
-        8,
         (
             like((rows, width), BF),
             like((rows, width), BF),
@@ -200,8 +225,9 @@
 FF_CUT = 512
 
 
-def feed_forward(mix, tokens, w_out, w_inner, w_outer, vectors, cotangent):
+def feed_forward(mix, tokens, row_count, w_out, w_inner, w_outer, vectors, cotangent):
     rows, width = tokens.shape
+
     hidden_units = w_inner.shape[1]
 
     def kernel(mix_ref, tok, wo, wi, wu, vec, cot, *outs):
@@ -221,7 +247,7 @@
             slope[:, cut : cut + FF_CUT] = upper + inner * bell
             total[...] += dot_nn(active, wu[cut : cut + FF_CUT, :])
         n, r = normal(total[...])
-        block[...] = (n * vec[2:3, :] + vec[3:4, :]).astype(BF)
+        block[...] = (n * vec[2:3, :] + vec[3:4, :])[:row_count].astype(BF)
         grad = cot[...].astype(F32)
         sums[0:1, :] = jnp.sum(grad * n, axis=0, keepdims=True)
         sums[1:2, :] = jnp.sum(grad, axis=0, keepdims=True)
@@ -229,14 +255,12 @@
         d_sec[...] = second
         d_out[...] = second.astype(BF)
 
-    return launch(
+    return Stage(
         kernel,
         (mix, tokens, w_out, w_inner, w_outer, vectors, cotangent),
         [vmem()] * 7,
-        "feed_forward",
-        10,
         (
-            like((rows, width), BF),
+            like((row_count, width), BF),
             like((rows, width), BF),
             like((rows, width), F32),
             like((rows, LANES), F32),
@@ -250,11 +274,13 @@
     )
 
 
-def feed_back(d_outer, d_second, slope, n_one, r_one, w_inner, w_outer, vectors, after):
+def feed_back(d_outer, d_second, slope, n_one, r_one, w_inner, w_outer, w_out, vectors):
     rows, width = d_outer.shape
     hidden_units = w_inner.shape[1]
 
-    def kernel(d_out, d_sec, slope_ref, n_ref, r_ref, wi, wu, vec, d_in, d_first, d_attn, sums):
+    def kernel(*refs):
+        d_out, d_sec, slope_ref, n_ref, r_ref, wi, wu, wo, vec = refs[:9]
+        d_in, d_first, d_attn, sums, d_heads = refs[9:]
         d_first[...] = d_sec[...]
         for cut in range(0, hidden_units, FF_CUT):
             grad = dot_nt(d_out[...], wu[cut : cut + FF_CUT, :])
@@ -268,39 +294,36 @@
         first = normal_back(d_hidden * vec[0:1, :], n, r_ref[:, 0:1])
         d_first[...] = first
         d_attn[...] = first.astype(BF)
-
-    return launch(
+        d_heads[...] = dot_nt(d_attn[...], wo[...]).astype(BF)
+
+    return Stage(
         kernel,
-        (d_outer, d_second, slope, n_one, r_one, w_inner, w_outer, vectors),
-        [vmem()] * 8,
-        "feed_back",
-        10,
+        (d_outer, d_second, slope, n_one, r_one, w_inner, w_outer, w_out, vectors),
+        [vmem()] * 9,
         (
             like((rows, hidden_units), BF),
             like((rows, width), F32),
             like((rows, width), BF),
             like((2, width), F32),
+            like((rows, width), BF),
         ),
-        after=after,
     )
 
 
 def attn_back(
-    d_attn, probs, query, keys_all, values_all, w_out, query_at, key_at, first_pair, pairs, name, after
+    d_heads, probs, query, keys_all, values_all, query_at, key_at, first_pair, pairs
 ):
-    rows, width = d_attn.shape
+    rows, width = d_heads.shape
     columns = pairs * LANES
     head_count, _, keys = probs.shape
     half_span = REL // 2
 
     def kernel(*refs):
-        d_at, p_ref, q_ref, k_ref, v_ref, wo, q_at, k_at = refs[:8]
-        dq_ref, dk_ref, dv_ref, tables = refs[8:12]
-        d_heads, heads_t, q_t, line_idx, key_hots, line_hots, row_hots, line_rows, rolls = refs[12:]
+        d_ref, p_ref, q_ref, k_ref, v_ref, q_at, k_at = refs[:7]
+        dq_ref, dk_ref, dv_ref, tables = refs[7:11]
+        heads_t, q_t, line_idx, key_hots, line_hots, row_hots, line_rows, rolls = refs[11:]
         base = first_pair * LANES
-        grad = dot_nt(d_at[...], wo[base : base + columns, :])
-        d_heads[...] = grad.astype(BF)
-        heads_t[...] = grad.T.astype(BF)
+        heads_t[...] = d_ref[:, base : base + columns].astype(F32).T.astype(BF)
         q_t[...] = q_ref[:, base : base + columns].astype(F32).T.astype(BF)
         line_idx[...] = line_index(q_at, k_at)
         lane = lax.broadcasted_iota(I32, (rows, LANES), 1)
@@ -328,7 +351,7 @@
         def pair(at, carry):
             col = pl.ds(pl.multiple_of(at * LANES, LANES), LANES)
             key_col = pl.ds(pl.multiple_of(base + at * LANES, LANES), LANES)
-            d_pair, k_pair, v_pair = d_heads[:, col], k_ref[:, key_col], v_ref[:, key_col]
+            d_pair, k_pair, v_pair = d_ref[:, key_col], k_ref[:, key_col], v_ref[:, key_col]
             back = []
             for half in range(2):
                 head = 2 * (first_pair + at) + half
@@ -409,12 +432,10 @@
             exact(rolls[0], horiz_map) + exact(rolls[1], vert_map) + exact(rolls[2], line_map)
         )
 
-    return launch(
+    return Stage(
         kernel,
-        (d_attn, probs, query, keys_all, values_all, w_out, query_at, key_at),
-        [vmem()] * 8,
-        name,
-        8,
+        (d_heads, probs, query, keys_all, values_all, query_at, key_at),
+        [vmem()] * 7,
         (
             like((rows, columns), BF),
             like((columns, keys), BF),
@@ -422,7 +443,6 @@
             like((16, LANES), F32),
         ),
         [
-            pltpu.VMEM((rows, columns), BF),
             pltpu.VMEM((columns, rows), BF),
             pltpu.VMEM((columns, rows), BF),
             pltpu.VMEM((rows, keys), I32),
@@ -432,17 +452,38 @@
             pltpu.VMEM((LANES, rows), BF),
             pltpu.VMEM((3, 16, LANES), F32),
         ],
-        after,
-    )
-
-
-def rows_back(d_first, parts, weights, shards, after):
+    )
+
+
+def fetch(weights):
+    count = len(weights)
+
+    def kernel(*refs):
+        copies = [
+            pltpu.make_async_copy(far, near, refs[-1].at[at])
+            for at, (far, near) in enumerate(zip(refs[:count], refs[count:-1]))
+        ]
+        for copy in copies:
+            copy.start()
+        for copy in copies:
+            copy.wait()
+
+    return Stage(
+        kernel,
+        weights,
+        [pl.BlockSpec(memory_space=pltpu.HBM)] * count,
+        [like(weight.shape, BF) for weight in weights],
+        [pltpu.SemaphoreType.DMA((count,))],
+    )
+
+
+def rows_back(d_first, parts, weights, shards):
     rows, width = d_first.shape
 
     def kernel(*refs):
         first, wq, wk, wv = refs[:4]
         part_refs = refs[4 : 4 + 3 * len(parts)]
-        own, *sent = refs[4 + 3 * len(parts) :]
+        own, send, keep = refs[4 + 3 * len(parts) :]
         for at in range(shards - 1, -1, -1):
             cut = slice(at * rows, (at + 1) * rows)
             total, place = None, 0
@@ -452,8 +493,11 @@
                 value = dot_nn(wk[:, col], dk[:, cut]) + dot_nn(wv[:, col], dv[:, cut])
                 total = value if total is None else total + value
                 place += dk.shape[0]
+            if at % 2:
+                send[at // 2] = total.T.astype(BF)
+                continue
             if at:
-                sent[at - 1][...] = total.T.astype(BF)
+                keep[at // 2 - 1] = total.T.astype(BF)
                 continue
             result, place = first[...] + total.T, 0
             for group in range(len(parts)):
@@ -464,14 +508,53 @@
             own[...] = result
 
     flat = [array for part in parts for array in part]
-    return launch(
+    return Stage(
         kernel,
         (d_first, *weights, *flat),
         [vmem()] * (4 + len(flat)),
-        "rows_back",
-        8,
-        (like((rows, width), F32),) + (like((rows, width), BF),) * (shards - 1),
-        after=after,
+        (
+            like((rows, width), F32),
+            like((shards // 2, rows, width), BF),
+            like((shards // 2 - 1, rows, width), BF),
+        ),
+    )
+
+
+def rows_step(own, keep, got):
+    def kernel(own_ref, keep_ref, got_ref, out, send):
+        out[...] = own_ref[...] + got_ref[0].astype(F32)
+        send[...] = keep_ref[0] + got_ref[1]
+
+    return Stage(kernel, (own, keep, got), [vmem()] * 3, (like(own.shape, F32), like(own.shape, BF)))
+
+
+def rows_result(own, got, row_count):
+    def kernel(own_ref, got_ref, out):
+        out[...] = (own_ref[...] + got_ref[...].astype(F32))[:row_count].astype(BF)
+
+    return Stage(kernel, (own, got), [vmem()] * 2, (like((row_count, own.shape[1]), BF),))
+
+
+def pack(sums, tables):
+    width = sums[0].shape[1]
+    height = sum(item.shape[0] for item in sums) * width // LANES
+
+    def kernel(*refs):
+        out, place = refs[-1], 0
+        for ref in refs[: len(sums)]:
+            for row in range(ref.shape[0]):
+                for cut in range(0, width, LANES):
+                    out[place : place + 1] = ref[row : row + 1, cut : cut + LANES]
+                    place += 1
+        total = refs[len(sums)][...]
+        for ref in refs[len(sums) + 1 : -1]:
+            total = total + ref[...]
+        out[place : place + total.shape[0]] = total
+        out[place + total.shape[0] :] = jnp.zeros_like(out[place + total.shape[0] :])
+
+    operands = (*sums, *tables)
+    return Stage(
+        kernel, operands, [vmem()] * len(operands), (like((-(-(height + tables[0].shape[0]) // 16) * 16, LANES), F32),)
     )
 
 
@@ -484,28 +567,41 @@
     return [array_in] + [swap(array_in, "tok", step) for step in range(1, lax.axis_size("tok"))]
 
 
-def xor_terms(groups, name, after=()):
+def two_halves(value):
+    high, low = two_parts(value)
+    return jnp.concatenate([high.astype(F32), low.astype(F32)], 0)
+
+
+def whole_value(halves):
+    return halves[: halves.shape[0] // 2] + halves[halves.shape[0] // 2 :]
+
+
+def put_load(out, item, value):
+    halves = two_halves(value)
+    rows, cols = out.shape[1:]
+    count = halves.shape[0] // rows
+    for at in range(count):
+        low = cols - (count - at) * LANES
+        out[item, :, low : low + LANES] = halves[at * rows : (at + 1) * rows].astype(BF)
+
+
+class Cut:
+    def __init__(self, array, low, high):
+        self.array, self.low, self.high = array, low, high
+
+
+def cut_of(right, form):
+    if isinstance(right, Cut):
+        return right
+    return Cut(right, 0, right.shape[form == "nn"])
+
+
+def xor_terms(groups, cuts, load=None):
     pages = lax.axis_size("page")
-    page_index = lax.axis_index("page")
     width = groups[0][0].shape[1]
     rows = width // pages
-    cols = [right.shape[1] if form == "nn" else right.shape[0] for _, right, form in groups]
-    if rows % 16:
-        whole = jnp.concatenate(
-            [
-                lax.dot_general(
-                    left,
-                    right,
-                    (((0,), (0 if form == "nn" else 1,)), ((), ())),
-                    preferred_element_type=F32,
-                ).astype(BF)
-                for left, right, form in groups
-            ],
-            1,
-        ).reshape(pages, rows, -1)
-        order = page_index ^ jnp.arange(pages)
-        whole = jnp.take(whole, order, axis=0)
-        return whole[0::2], whole[1::2]
+    rights = [cut_of(right, form) for _, right, form in groups]
+    cols = [right.high - right.low for right in rights]
     lefts, which = [], []
     for left, _, _ in groups:
         found = [at for at, item in enumerate(lefts) if item is left]
@@ -513,156 +609,374 @@
         if not found:
             lefts.append(left)
 
-    def kernel(page_ref, *refs):
+    def kernel(*refs):
+        if load is not None:
+            load_ref, refs = refs[0], refs[1:]
         left_refs = refs[: len(lefts)]
         right_refs = refs[len(lefts) : len(lefts) + len(groups)]
-        keep, send = refs[len(lefts) + len(groups) : len(lefts) + len(groups) + 2]
-        turned = refs[len(lefts) + len(groups) + 2 :][: len(lefts)]
-        picked = refs[2 * len(lefts) + len(groups) + 2 :]
+        keep, *sends = refs[len(lefts) + len(groups) :][: 1 + len(cuts)]
+        rest = refs[1 + len(cuts) + len(lefts) + len(groups) :]
+        turned, picked = rest[: len(lefts)], rest[len(lefts) :]
         for left_ref, turned_ref in zip(left_refs, turned):
             turned_ref[...] = (
                 left_ref[...].astype(F32).T.astype(BF).reshape(pages, rows, left_ref.shape[0])
             )
-        page = page_ref[0]
-        for odd, out in ((1, send), (0, keep)):
+        page = lax.axis_index("page")
+        for odd in (1, 0):
             for at, turned_ref in enumerate(turned):
                 for step in range(pages // 2):
                     picked[at][step * rows : (step + 1) * rows] = turned_ref[
                         page ^ (2 * step + odd)
                     ]
             place = 0
-            for at_left, right_ref, (_, _, form), count in zip(which, right_refs, groups, cols):
+            outs = [out for out, count in zip(sends, cuts) for _ in range(count)]
+            for at_left, right_ref, right, (_, _, form), count, out in zip(
+                which, right_refs, rights, groups, cols, outs if odd else [keep] * len(groups)
+            ):
+                if odd and place and out is not last:
+                    place = 0
+                last = out
                 for cut in range(0, count, 256):
                     end = min(cut + 256, count)
+                    used = slice(right.low + cut, right.low + end)
                     if form == "nn":
-                        value = dot_nn(picked[at_left][...], right_ref[:, cut:end])
+                        value = dot_nn(picked[at_left][...], right_ref[:, used])
                     else:
-                        value = dot_nt(picked[at_left][...], right_ref[cut:end, :])
+                        value = dot_nt(picked[at_left][...], right_ref[used, :])
                     out[:, :, place + cut : place + end] = value.astype(BF).reshape(
                         pages // 2, rows, end - cut
                     )
                 place += count
-
-    out = like((pages // 2, rows, sum(cols)), BF)
-    return launch(
+        if load is not None:
+            put_load(sends[-1], 0, load_ref[...])
+
+    sizes, first = [sum(cols)], 0
+    for count in cuts:
+        sizes.append(sum(cols[first : first + count]))
+        first += count
+    if load is not None:
+        sizes[-1] += LANES
+    extra = [] if load is None else [load]
+    return Stage(
         kernel,
         (
-            page_index.reshape(1).astype(I32),
+            *extra,
             *lefts,
-            *[right for _, right, _ in groups],
+            *[right.array for right in rights],
         ),
-        [smem()] + [vmem()] * (len(lefts) + len(groups)),
-        name,
-        10,
-        (out, out),
+        [vmem()] * (len(extra) + len(lefts) + len(groups)),
+        [like((pages // 2, rows, size), BF) for size in sizes],
         [pltpu.VMEM((pages, rows, left.shape[0]), BF) for left in lefts]
         + [pltpu.VMEM((pages // 2 * rows, left.shape[0]), BF) for left in lefts],
-        after,
-    )
-
-
-def split_sum(pairs, picks, name, after=()):
-    def kernel(*refs):
-        ins, outs = refs[: 2 * len(pairs)], refs[2 * len(pairs) :]
-        for out, (pair, items, first, count) in zip(outs, picks):
-            for at, item in enumerate(items):
-                cut = slice(first, first + count)
-                out[at] = ins[2 * pair][item, :, cut] + ins[2 * pair + 1][item, :, cut]
-
-    rows = pairs[0][0].shape[1]
-    return launch(
-        kernel,
-        [array for pair in pairs for array in pair],
-        [vmem()] * (2 * len(pairs)),
-        name,
-        4,
-        tuple(like((len(items), rows, count), BF) for _, items, _, count in picks),
-        after=after,
-    )
-
-
-def tok_split(pairs, name, after=()):
-    toks = lax.axis_size("tok")
-    rows, cols = pairs[0][0].shape[1:]
-    share = rows // toks
-    arrays = [array.reshape(toks, share, cols) for pair in pairs for array in pair]
-
-    def kernel(tok_ref, *refs):
-        ins, outs = refs[: len(arrays)], refs[len(arrays) :]
-        for step in range(toks):
-            at = tok_ref[0] ^ step
-            for pair in range(len(pairs)):
-                value = ins[2 * pair][at].astype(F32) + ins[2 * pair + 1][at].astype(F32)
-                out = outs[step]
-                out[:, pair * cols : (pair + 1) * cols] = value.astype(out.dtype)
-
-    full = (share, cols * len(pairs))
-    return launch(
-        kernel,
-        (lax.axis_index("tok").reshape(1).astype(I32), *arrays),
-        [smem()] + [vmem()] * len(arrays),
-        name,
-        4,
-        (like(full, F32),) + (like(full, BF),) * (toks - 1),
-        after=after,
-    )
+    )
+
+
+def plain_terms(groups):
+    pages, parts = lax.axis_size("page"), []
+    for left, right, form in groups:
+        cut = cut_of(right, form)
+        side = int(form == "nn")
+        used = lax.slice_in_dim(cut.array, cut.low, cut.high, axis=side)
+        part = lax.dot_general(
+            left, used, (((0,), (1 - side,)), ((), ())), preferred_element_type=F32
+        )
+        parts.append(part.astype(BF))
+    whole = jnp.concatenate(parts, 1)
+    whole = whole.reshape(pages, whole.shape[0] // pages, whole.shape[1])
+    whole = jnp.take(whole, lax.axis_index("page") ^ jnp.arange(pages), axis=0)
+    return whole[0::2], [whole[1::2]]
+
+
+def with_terms(stages, sums, name, limit, after=(), load=None, cuts=None):
+    width, pages = sums[0][0][0].shape[1], lax.axis_size("page")
+    if width // pages % 16:
+        outs = run(stages, name, limit, after) if stages else ()
+        order = [item for stage in stages for item in stage.results]
+
+        def real(item):
+            return outs[order.index(item)] if isinstance(item, Later) else item
+
+        return [
+            plain_terms([(real(left), real(right), form) for left, right, form in groups])
+            for groups in sums
+        ], outs
+    last = [xor_terms(groups, cuts or [len(groups)], load) for groups in sums]
+    outs = run([*stages, *last], name, limit, after)
+    each = 1 + len(cuts or [0])
+    count = len(outs) - each * len(sums)
+    terms = [(outs[at], list(outs[at + 1 : at + each])) for at in range(count, len(outs), each)]
+    return terms, outs[:count]
+
+
+def plain_sum(pair):
+    def kernel(left, right, out):
+        out[...] = left[...] + right[...]
+
+    return Stage(kernel, pair, [vmem()] * 2, (like(pair[0].shape, pair[0].dtype),))
+
+
+class Rider:
+    def __init__(self, vector, path):
+        self.path = [("page", 1)] + path
+        self.move(vector)
+
+    def stage(self):
+        return plain_sum(self.pair)
+
+    def move(self, vector):
+        self.pair = (vector, swap(vector, *self.path.pop(0)))
+
+
+def add_columns(kept, got, at, low, high, kind):
+    ends = set()
+    for pieces in (kept, got):
+        place = 0
+        for piece in pieces:
+            place += piece.shape[-1]
+            ends.add(place)
+    ends = sorted(end for end in ends if low < end < high) + [high]
+
+    def read(pieces, first, last):
+        place = 0
+        for piece in pieces:
+            if place <= first and last <= place + piece.shape[-1]:
+                return piece[(*at, slice(None), slice(first - place, last - place))].astype(kind)
+            place += piece.shape[-1]
+
+    values, first = [], low
+    for end in ends:
+        values.append(read(kept, first, end) + read(got, first, end))
+        first = end
+    return values[0] if len(values) == 1 else jnp.concatenate(values, 1)
 
 
 class Reduction:
-    def __init__(self, keep, send, name):
-        self.name = name
-        self.pairs = [(keep, swap(send, "page", 1))]
-        bits = [1 << at for at in range(1, lax.axis_size("page").bit_length() - 1)]
-        self.orders = [bits, bits[::-1]]
-        self.items = [list(range(0, lax.axis_size("page"), 2))] * 2
-
-    def step(self, after=()):
-        at_step = len(self.orders[0])
-        cols = self.pairs[0][0].shape[2]
-        first = len(self.pairs) == 1
-        width = cols // 2 if first else cols
-        picks, kept_items = [], []
-        for half in range(2):
-            bit = self.orders[half][0]
-            items = self.items[half]
-            where = (0, half * width) if first else (half, 0)
-            for wanted in (bit, 0):
-                chosen = [at for at, item in enumerate(items) if item & bit == wanted]
-                picks.append((where[0], chosen, where[1], width))
-            kept_items.append([item for item in items if not item & bit])
-        outs = split_sum(self.pairs, picks, f"{self.name}_sum{at_step}", after)
-        self.last = outs[-1]
-        self.pairs = [
-            (outs[2 * half + 1], swap(outs[2 * half], "page", self.orders[half][0]))
-            for half in range(2)
+    def __init__(self, terms, name, turn=False, tok_first=False):
+        keep, sends = terms
+        pages, toks = lax.axis_size("page"), lax.axis_size("tok")
+        self.name, self.count, self.pages, self.toks = name, 0, pages, toks
+        bits = [1 << at for at in range(1, pages.bit_length() - 1)]
+        page_path = [("page", bit) for bit in (bits[::-1] if turn else bits)]
+        tok_path = [("tok", 1 << at) for at in range(toks.bit_length() - 1)]
+        self.path = tok_path + page_path if tok_first else page_path + tok_path
+        self.labels, self.split = list(range(0, pages, 2)), False
+        self.kept, self.got = [keep], [swap(piece, "page", 1) for piece in sends]
+
+    def join(self, other):
+        self.kept, self.got = self.kept + other.kept, self.got + other.got
+
+    def step(self, after=(), rider=None, cuts=None):
+        begun = self.count > 0
+        self.halve(after, rider, cuts)
+        while begun and self.path and self.path[0][0] == "page":
+            self.halve(after, rider)
+
+    def halve(self, after=(), rider=None, cuts=None):
+        axis, bit = self.path.pop(0)
+        flag = bit if axis == "page" else bit * self.pages
+        first = axis == "tok" and not self.split
+        arrays, toks = [*self.kept, *self.got], self.toks
+        rows, cols = self.kept[0].shape[1], sum(array.shape[2] for array in self.kept)
+        if first:
+            rows //= toks
+            arrays = [a.reshape(a.shape[0], toks, rows, a.shape[2]) for a in arrays]
+            self.labels = [at + self.pages * r for at in self.labels for r in range(toks)]
+            self.split = True
+        labels = self.labels
+        cuts = cuts or [cols]
+        send = [at for at, label in enumerate(labels) if label & flag]
+        keep = [at for at, label in enumerate(labels) if not label & flag]
+        held = len(self.kept)
+        kind = BF if self.path else F32
+
+        def kernel(*refs):
+            tok = lax.axis_index("tok")
+            kept, got = refs[:held], refs[held : len(arrays)]
+            keep_out, *outs = refs[len(arrays) :]
+
+            def total(at, low, high, out_kind):
+                at = (at // toks, tok ^ (at % toks)) if first else (at,)
+                return add_columns(kept, got, at, low, high, out_kind)
+
+            low = 0
+            for out, width in zip(outs, cuts):
+                for place, at in enumerate(send):
+                    out[place] = total(at, low, low + width, BF)
+                low += width
+            for place, at in enumerate(keep):
+                keep_out[place] = total(at, 0, cols, kind)
+
+        stages = [
+            Stage(
+                kernel,
+                arrays,
+                [vmem()] * len(arrays),
+                [like((len(keep), rows, cols), kind)]
+                + [like((len(send), rows, width), BF) for width in cuts],
+            )
         ]
-        self.items = kept_items
-        self.orders = [order[1:] for order in self.orders]
-
-    def to_tok(self, after=()):
-        while self.orders[0]:
-            self.step(after)
-        own, *sent = tok_split(self.pairs, f"{self.name}_tok", after)
+        if rider:
+            stages.append(rider.stage())
+        self.count += 1
+        outs = run(stages, f"{self.name}_step{self.count}", 4, after)
+        self.labels = [labels[at] for at in keep]
+        self.last = outs[0]
+        self.kept = [outs[0]]
+        self.got = [swap(piece, axis, bit) for piece in outs[1 : 1 + len(cuts)]]
+        if rider:
+            rider.move(outs[-1])
+
+    def until(self, left, after=(), rider=None):
+        while len(self.path) > left:
+            self.halve(after, rider)
+
+    def result(self, columns, after=()):
+        kept, got = self.kept[0], self.got[0]
+
+        def kernel(kept_ref, got_ref, *outs):
+            low = 0
+            for out, width in zip(outs, columns):
+                cut = slice(low, low + width)
+                out[...] = kept_ref[0, :, cut] + got_ref[0, :, cut].astype(F32)
+                low += width
+
+        stage = Stage(
+            kernel,
+            (kept, got),
+            [vmem()] * 2,
+            [like((kept.shape[1], width), F32) for width in columns],
+        )
+        return run([stage], f"{self.name}_result", 4, after)
+
+
+class Direct:
+    def __init__(self, terms, load, name):
+        self.kept, sends = terms
+        self.first = self.kept
+        self.got = [swap(piece, "page", 1) for piece in sends]
+        self.load, self.name = load, name
+
+    def step(self, after):
+        items, rows, cols = self.kept.shape
+        toks = lax.axis_size("tok")
+        sent = [like((1, rows, cols + LANES), BF)] * (items - 1)
+
+        def kernel(kept, load, *refs):
+            got, (own, load_out, *outs) = refs[: len(self.got)], refs[len(self.got) :]
+            value = whole_value(two_halves(load[...]))
+            value = value + whole_value(got[-1][0, :, -LANES:].astype(F32))
+            load_out[...] = value
+            for at in range(items):
+                low = 0
+                for piece in got:
+                    width = min(piece.shape[2], cols - low)
+                    cut = slice(low, low + width)
+                    if at:
+                        outs[at - 1][0, :, cut] = kept[at, :, cut] + piece[at, :, :width]
+                    else:
+                        own[:, cut] = kept[at, :, cut].astype(F32) + piece[at, :, :width].astype(F32)
+                    low += width
+            for out in outs:
+                put_load(out, 0, value)
+
+        operands = (self.kept, self.load, *self.got)
+        stage = Stage(
+            kernel,
+            operands,
+            [vmem()] * len(operands),
+            [like((rows, cols), F32), like(self.load.shape, F32), *sent],
+        )
+        own, self.load, *sends = run([stage], f"{self.name}_step1", 6, after)
         self.last = own
-        self.shares = [own] + [swap(piece, "tok", at + 1) for at, piece in enumerate(sent)]
-
-    def result(self):
-        total = self.shares[0]
-        for piece in self.shares[1:]:
-            total = total + piece.astype(F32)
-        return total
-
-
-def sum_all(vector):
-    bit = 1
-    while bit < lax.axis_size("page"):
-        vector = vector + swap(vector, "page", bit)
-        bit *= 2
-    bit = 1
-    while bit < lax.axis_size("tok"):
-        vector = vector + swap(vector, "tok", bit)
-        bit *= 2
-    return vector
+        self.kept = own.reshape(toks, rows // toks, cols)
+        self.got = [
+            swap(piece, "page", 2 * (at + 1)).reshape(toks, rows // toks, cols + LANES)
+            for at, piece in enumerate(sends)
+        ]
+
+    def along(self, after):
+        toks, rows, cols = self.kept.shape
+        blocks = 2 * self.load.shape[0] // rows
+
+        def kernel(kept, load, one, two, three, own, load_out, *outs):
+            tok = lax.axis_index("tok")
+            halves = [
+                whole_value(piece[:, :, cols:].astype(F32).reshape(toks * rows, LANES))
+                for piece in (one, two, three)
+            ]
+            mine = whole_value(two_halves(load[...]))
+            value = (mine + halves[0]) + (halves[1] + halves[2])
+            load_out[...] = value
+            for step in range(toks):
+                at = tok ^ step
+                total = kept[at] + one[at, :, :cols].astype(F32)
+                total = total + two[at, :, :cols].astype(F32) + three[at, :, :cols].astype(F32)
+                if step:
+                    outs[step - 1][0, :, :cols] = total.astype(BF)
+                    put_load(outs[step - 1], 0, value)
+                else:
+                    own[...] = total
+
+        stage = Stage(
+            kernel,
+            (self.kept, self.load, *self.got),
+            [vmem()] * 5,
+            [like((rows, cols), F32), like(self.load.shape, F32)]
+            + [like((1, rows, cols + blocks * LANES), BF)] * (toks - 1),
+        )
+        self.kept, self.load, *sends = run([stage], f"{self.name}_step2", 6, after)
+        self.last = self.kept
+        self.got = [swap(piece, "tok", at + 1) for at, piece in enumerate(sends)]
+
+    def result(self, columns, after):
+        rows, cols = self.kept.shape
+        blocks = 2 * self.load.shape[0] // rows
+
+        def kernel(kept, load, one, two, three, load_out, *outs):
+            halves = []
+            for piece in (one, two, three):
+                parts = [
+                    piece[0, :, cols + at * LANES :][:, :LANES].astype(F32) for at in range(blocks)
+                ]
+                halves.append(whole_value(jnp.concatenate(parts, 0)))
+            mine = whole_value(two_halves(load[...]))
+            load_out[...] = (mine + halves[0]) + (halves[1] + halves[2])
+            low = 0
+            for out, width in zip(outs, columns):
+                cut = slice(low, low + width)
+                total = kept[:, cut] + one[0, :, cut].astype(F32)
+                out[...] = total + two[0, :, cut].astype(F32) + three[0, :, cut].astype(F32)
+                low += width
+
+        stage = Stage(
+            kernel,
+            (self.kept, self.load, *self.got),
+            [vmem()] * 5,
+            [like(self.load.shape, F32)] + [like((rows, width), F32) for width in columns],
+        )
+        load, *outs = run([stage], f"{self.name}_result", 6, after)
+        self.last = load
+        return outs, load
+
+
+class Halved:
+    def __init__(self, terms, load, name):
+        self.sum = Reduction(terms, name)
+        self.first = self.sum.kept[0]
+        self.rider = Rider(load, list(self.sum.path))
+
+    def step(self, after):
+        self.sum.step(after, self.rider)
+        self.last = self.sum.last
+
+    def along(self, after):
+        self.sum.until(0, after, self.rider)
+        self.last = self.sum.last
+
+    def result(self, columns, after):
+        outs = self.sum.result(columns, after)
+        self.last = outs[0]
+        return outs, self.rider.pair[0] + self.rider.pair[1]
 
 
 def on_device(
@@ -722,88 +1036,126 @@
     )
     vectors = jnp.stack([gain_one, shift_one, gain_two, shift_two], 0)
 
-    mix, query, keys_all, values_all, tokens_all, probs, key_at = attn_forward(
-        token_shards, row_count, w_query, w_key, w_value, line_table, box_table, query_at
-    )
-    block, hidden, n_one, r_one, active, slope, d_second, d_outer, sums_two = feed_forward(
-        mix, padded_tokens, w_out, w_inner, w_outer, vectors, padded(cotangent)
-    )
-    terms = xor_terms([(active, d_outer, "nn")], "outer_terms")
-    outer = Reduction(*terms, "outer")
-    d_inner, d_first, d_attn, sums_one = feed_back(
-        d_outer, d_second, slope, n_one, r_one, w_inner, w_outer, vectors, (terms[0],)
-    )
-    outer.step((d_attn,))
-    terms = xor_terms(
-        [(hidden, d_inner, "nn"), (mix, d_attn, "nn")], "inner_terms", (outer.last,)
-    )
-    inner = Reduction(*terms, "inner")
-    half_pairs = width // LANES // 2
-    parts, table_parts, done = [], [], terms[0]
-    for group in range(2):
-        *part, table_part = attn_back(
-            d_attn,
-            probs,
-            query,
-            keys_all,
-            values_all,
-            w_out,
-            query_at,
-            key_at,
-            group * half_pairs,
-            half_pairs,
-            f"attn_back{group}",
-            (done,),
+    w_query, w_key, w_value, w_out, w_inner, w_outer = run(
+        [fetch((w_query, w_key, w_value, w_out, w_inner, w_outer))], "fetch", 1, (padded_tokens,)
+    )
+    first = attn_forward(
+        token_shards,
+        row_count,
+        (w_key, w_value, w_query),
+        line_table,
+        box_table,
+        query_at,
+    )
+    second = feed_forward(
+        first.results[0],
+        padded_tokens,
+        row_count,
+        w_out,
+        w_inner,
+        w_outer,
+        vectors,
+        padded(cotangent),
+    )
+    terms, outs = with_terms(
+        [first, second],
+        [[(second.results[4], second.results[7], "nn")]],
+        "forward",
+        10,
+    )
+    mix, query, keys_all, values_all, tokens_all, probs, key_at = outs[:7]
+    block, hidden, n_one, r_one, active, slope, d_second, d_outer, sums_two = outs[7:]
+    outer = Reduction(terms[0], "outer")
+    back = feed_back(d_outer, d_second, slope, n_one, r_one, w_inner, w_outer, w_out, vectors)
+    d_inner, d_first, d_attn, sums_one, d_heads = run([back], "feed_back", 8, (outer.kept[0],))
+    unit = width // 6
+    outer.step((d_attn,), cuts=[2 * unit, 4 * unit])
+    main = 15 * unit
+    terms, _ = with_terms(
+        [],
+        [
+            [(hidden, Cut(d_inner, 0, main), "nn")],
+            [(hidden, Cut(d_inner, main, w_inner.shape[1]), "nn"), (mix, d_attn, "nn")],
+        ],
+        "inner_terms",
+        10,
+        (d_attn, outer.last),
+    )
+    inner = Reduction(terms[0], "inner", turn=True)
+    out = Reduction(terms[1], "out")
+    third = width // LANES // 3
+
+    def heads_back(at):
+        return attn_back(
+            d_heads, probs, query, keys_all, values_all, query_at, key_at, at * third, third
         )
-        parts.append(part)
-        table_parts.append(table_part)
-        if group == 0:
-            inner.step((table_part,))
-            outer.step((inner.last,))
-            done = outer.last
-    terms = xor_terms(
-        [(padded_tokens, part[0], "nn") for part in parts]
-        + [(tokens_all, part[1], "nt") for part in parts]
-        + [(tokens_all, part[2], "nt") for part in parts],
-        "attn_terms",
-    )
-    attn = Reduction(*terms, "attn")
-    d_own, *sent = rows_back(
-        d_first, parts, (w_query, w_key, w_value), shards, (terms[0],)
-    )
+
+    *part_one, tables_one = run([heads_back(0)], "attn_back", 10, (out.kept[0],))
+    inner.step((tables_one, *outer.got[:1]), cuts=[15 * unit])
+    out.step((inner.last,), cuts=[15 * unit])
+    *part_two, tables_two = run(
+        [heads_back(1)], "attn_more", 10, (out.last,)
+    )
+    stage = heads_back(2)
+    parts = [part_one, part_two, stage.results[:3]]
+    whole_tiles = lax.axis_size("page") == 8 and width // lax.axis_size("page") % 16 == 0
+    *last_part, _, small = run(
+        [stage, pack((sums_one, sums_two), (tables_one, tables_two, stage.results[3]))],
+        "attn_rest",
+        10,
+        (tables_two,),
+    )
+    parts[2] = last_part
+
+    def attn_sum(after):
+        terms, _ = with_terms(
+            [],
+            [
+                [(padded_tokens, part[0], "nn") for part in parts]
+                + [(tokens_all, part[1], "nt") for part in parts]
+                + [(tokens_all, part[2], "nt") for part in parts]
+            ],
+            "attn_terms",
+            10,
+            after,
+            load=small if whole_tiles else None,
+            cuts=[9],
+        )
+        return (Direct if whole_tiles else Halved)(terms[0], small, "attn")
+
+    outer.step((small,))
+    inner.step((outer.last,))
+    attn = attn_sum((inner.last, ))
+    d_own, rows_sent, rows_kept = run(
+        [rows_back(d_first, parts, (w_query, w_key, w_value), shards)], "rows_back", 10, (attn.first,)
+    )
+    rows_got = swap(rows_sent, "tok", 1)
+    attn.step((d_own,))
+    out.step((attn.last,))
+    outer.step((out.last,))
+    d_own, rows_sent = run(
+        [rows_step(d_own, rows_kept, rows_got)], "rows_step", 4, (outer.last,)
+    )
+    rows_got = swap(rows_sent, "tok", 2)
+    inner.join(out)
     inner.step((d_own,))
-    attn.step((inner.last,))
-    outer.to_tok((attn.last,))
-    back = [swap(piece, "tok", at + 1) for at, piece in enumerate(sent)]
-    small = jnp.concatenate(
-        [
-            sums_one.reshape(-1, LANES),
-            sums_two.reshape(-1, LANES),
-            table_parts[0] + table_parts[1],
-        ],
-        0,
-    )
-    small = sum_all(small)
-    attn.step((outer.last,))
-    inner.to_tok((attn.last,))
-    attn.to_tok((inner.last,))
-    for piece in back:
-        d_own = d_own + piece.astype(F32)
-    d_tokens = d_own[:row_count].astype(BF)
+    attn.along((inner.last,))
+    outer.step((attn.last,))
+    inner.step((outer.last,))
+    (d_tokens,) = run([rows_result(d_own, rows_got, row_count)], "rows_result", 4, (inner.last,))
+    (grad_outer,) = outer.result([width], (d_tokens,))
+    grad_inner, grad_out = inner.result([w_inner.shape[1], width], (grad_outer,))
+    grad_attn, small = attn.result([width] * 3, (grad_inner,))
     vector_rows = width // LANES
     vector_sums = small[: 4 * vector_rows].reshape(4, width)
     tables = small[4 * vector_rows :][: table_line.shape[0]]
-    grad_attn = attn.result()
-    grad_attn = [grad_attn[:, at * width : (at + 1) * width] for at in range(3)]
-    grad_inner = inner.result()
-    units = w_inner.shape[1]
     return (
-        block[:row_count],
+        block,
         d_tokens,
         *grad_attn,
-        grad_inner[:, units:],
-        grad_inner[:, :units],
-        outer.result(),
+        grad_out,
+        grad_inner,
+        grad_outer,
         vector_sums[0],
         vector_sums[1],
         vector_sums[2],

time: 190 us -> 163 us (0.86)
  starting transfers between devices: 50.9 us -> 28.3 us
  local copies, waits for them, and re-layouts: 31.5 us -> 17.3 us
  waiting for transfers between devices: 44.6 us -> 58.3 us
  other arithmetic: 9.33 us -> 5.51 us
    ppermute x35 -> x26, starting transfers between devices: 50.9 us -> 28.3 us  [swap(): lax.ppermute(array_in, axis_name, [(at, at ^ flip) for at in range(size)])]
    ppermute x35 -> x26, waiting for transfers between devices: 44.6 us -> 58.3 us  [swap(): lax.ppermute(array_in, axis_name, [(at, at ^ flip) for at in range(size)])]
    unnamed x74 -> x24, local copies, waits for them, and re-layouts: 23.4 us -> 11.3 us
    slice x3 -> x0, local copies, waits for them, and re-layouts: 2.06 us -> none  [the longest x1 0.73 us: on_device(): grad_inner[:, :units]]
    another operation x5 -> x4, other arithmetic: 4.47 us -> 2.84 us
    pallas_call x18 -> x26, Pallas kernels: 51.6 us -> 51.5 us  [run(): pl.pallas_call(kernel, out_shape=tuple(out_shape), in_specs=specs + [pl.B...]
  transfers between devices with their start and end apart: 35 -> 26, of which waited for: 15 -> 11; matrix products, arithmetic and copies ran while one was open for 7% -> 3% of each run, Pallas kernels for 12% -> 19%
where the time goes in v1:
time: 163 us; the launch traced here: 162 us
  waiting for transfers between devices  58.3 us (36%)
  Pallas kernels  51.5 us (32%)
  starting transfers between devices  28.3 us (17%)
  local copies, waits for them, and re-layouts  17.3 us (11%)
  other arithmetic  5.51 us (3%)
    ppermute x26, waiting for transfers between devices, swap(): lax.ppermute(array_in, axis_name, [(at, at ^ flip) for at in range(size)])  58.3 us
    pallas_call x26, Pallas kernels, run(): pl.pallas_call(kernel, out_shape=tuple(out_shape), in_specs=specs + [pl.B...  51.5 us
    ppermute x26, starting transfers between devices, swap(): lax.ppermute(array_in, axis_name, [(at, at ^ flip) for at in range(size)])  28.3 us
    unnamed x24, local copies, waits for them, and re-layouts  11.3 us
  transfers between devices with their start and end apart: 26, of which 11 were waited for; matrix products, arithmetic and copies ran while one was open for 3% of the time, Pallas kernels for 19%

profile of v1, /device:TPU:0, one launch (start us, length us, event | category | flops | bytes accessed | tf_op | source)
XLA Modules:
  0.0 161.9 jit_solution(6273832060798365661)
XLA Ops:
  0.7 0.8 convert.31
  3.6 1.0 pad_maximum_fusion.refs_6_.refs_0_.refs_1_
  4.7 5.1 %collective-permute-start.2 = (bf16[144,768]{1,0:T(8,128)(2,1)S(1)}, bf16[144,768]{1,0:T(8,128)(2,1)S(1)}, u32[]{:S(2)}, u32[]{:S(2)}) collective-permute-start(bf16[144,768]{1,0:T(8,128)(2,1)S(1)} %pad_maximum_fusion.refs_6_.refs_0_.refs_1_), channel_id=1, source_target_pairs={{0,3},{1,2},{2,1},{3,0},{4,7},{5,6},{6,5},{7,4},{8,11},{9,10},{10,... | collective-permute-start | bytes 663560 | tf_op jit(solution)/shard_map/ppermute | solution.py:563
  13.2 0.7 pad_add_fusion
  14.0 1.0 pad.40.refs_14_
  15.1 0.8 broadcast_add_fusion
  15.9 2.3 %copy-done = bf16[768,3072]{1,0:T(8,128)(2,1)S(1)} copy-done((bf16[768,3072]{1,0:T(8,128)(2,1)S(1)}, bf16[768,3072]{1,0:T(8,128)(2,1)}, u32[]{:S(2)}) %copy-start) | copy-done | bytes 4718616
  18.3 2.3 %copy-done.1 = bf16[3072,768]{1,0:T(8,128)(2,1)S(1)} copy-done((bf16[3072,768]{1,0:T(8,128)(2,1)S(1)}, bf16[3072,768]{1,0:T(8,128)(2,1)}, u32[]{:S(2)}) %copy-start.1) | copy-done | bytes 4718616
  20.6 1.3 copy-done.4
  21.9 1.3 copy-done.5
  23.1 1.3 copy-done.6
  24.4 1.6 %fetch.1 = (bf16[768,768]{1,0:T(8,128)(2,1)S(1)}, bf16[768,768]{1,0:T(8,128)(2,1)S(1)}, bf16[768,768]{1,0:T(8,128)(2,1)S(1)}, bf16[768,768]{1,0:T(8,128)(2,1)S(1...) custom-call(bf16[768,768]{1,0:T(8,128)(2,1)S(1)} %copy-done.3, bf16[768,768]{1,0:T(8,128)(2,1)S(1)} %copy-done.4, ...), custom_call_target="tpu_custom_call" | custom-call | tf_op jit(solution)/shard_map/fetch/pallas_call | solution.py:68
  26.2 2.4 %collective-permute-done.1.refs_2_ = bf16[144,768]{1,0:T(8,128)(2,1)S(1)} collective-permute-done((bf16[144,768]{1,0:T(8,128)(2,1)S(1)}, bf16[144,768]{1,0:T(8,128)(2,1)S(1)}, u32[]{:S(2)}, u32[]{:S(2)}) %collective-permute-start.1) | collective-permute-done | bytes 221216 | tf_op jit(solution)/shard_map/ppermute | solution.py:563
  28.6 15.1 %forward.1 = (bf16[144,768]{1,0:T(8,128)(2,1)S(1)}, bf16[144,768]{1,0:T(8,128)(2,1)S(1)}, bf16[640,768]{1,0:T(8,128)(2,1)S(1)}, bf16[640,768]{1,0:T(8,128)(2,1)S...) custom-call(bf16[144,768]{1,0:T(8,128)(2,1)S(1)} %pad_maximum_fusion, ...), custom_call_target="tpu_custom_call" | custom-call | tf_op jit(solution)/shard_map/forward/pallas_call | solution.py:68
  43.7 4.0 %feed_back.1 = (bf16[144,3072]{1,0:T(8,128)(2,1)S(1)}, f32[144,768]{1,0:T(8,128)S(1)}, bf16[144,768]{1,0:T(8,128)(2,1)S(1)}, f32[2,768]{1,0:T(2,128)S(1)}, bf16[144,768]{1,0:T(8,128)(2,1)S(1)}) custom-call(bf16[144,768]{1,0:T(8,128)(2,1)S(1)} %get-tuple-element.111.refs_0_, f32[144,768]{1,0:T(8,128)S(1)} %get-tuple-element.112.refs_1_, ...), custom_call_target="tpu_custom_call" | custom-call | tf_op jit(solution)/shard_map/feed_back/pallas_call | solution.py:68
  48.5 2.0 %inner_terms.1 = (bf16[4,96,1920]{2,1,0:T(8,128)(2,1)S(1)}, bf16[4,96,1920]{2,1,0:T(8,128)(2,1)S(1)}, bf16[4,96,1920]{2,1,0:T(8,128)(2,1)S(1)}, bf16[4,96,1920]{2,1,0:T(8,128)(2,1)S(1)}) custom-call(bf16[144,768]{1,0:T(8,128)(2,1)S(1)} %get-tuple-element.124.refs_0_, bf16[144,3072]{1,0:T(8,128)(2,1)S(1)} %get-tuple-element.125.refs_1_, ...), custom_call_target="tpu_custom_call" | custom-call | tf_op jit(solution)/shard_map/inner_terms/pallas_call | solution.py:68
  51.1 1.5 collective-permute-start.6
  53.1 6.1 %attn_back.1 = (bf16[144,256]{1,0:T(8,128)(2,1)S(1)}, bf16[256,640]{1,0:T(8,128)(2,1)S(1)}, bf16[256,640]{1,0:T(8,128)(2,1)S(1)}, f32[16,128]{1,0:T(8,128)S(1)}) custom-call(bf16[144,768]{1,0:T(8,128)(2,1)S(1)} %get-tuple-element.118.refs_0_, bf16[12,144,640]{2,1,0:T(8,128)(2,1)S(1)} %get-tuple-element.119.refs_1_, ...), custom_call_target="tpu_custom_call" | custom-call | tf_op jit(solution)/shard_map/attn_back/pallas_call | solution.py:68
  59.2 3.9 %collective-permute-done.6.refs_3_.refs_1_ = bf16[2,384,256]{2,1,0:T(8,128)(2,1)S(1)} collective-permute-done((bf16[2,384,256]{2,1,0:T(8,128)(2,1)S(1)}, bf16[2,384,256]{2,1,0:T(8,128)(2,1)S(1)}, u32[]{:S(2)}, u32[]{:S(2)}) %collective-permute-start.6) | collective-permute-done | bytes 393248 | tf_op jit(solution)/shard_map/ppermute | solution.py:563
  63.2 1.6 collective-permute-start.7
  65.0 5.8 %attn_more.1 = (bf16[144,256]{1,0:T(8,128)(2,1)S(1)}, bf16[256,640]{1,0:T(8,128)(2,1)S(1)}, bf16[256,640]{1,0:T(8,128)(2,1)S(1)}, f32[16,128]{1,0:T(8,128)S(1)}) custom-call(bf16[144,768]{1,0:T(8,128)(2,1)S(1)} %get-tuple-element.118.refs_0_, bf16[12,144,640]{2,1,0:T(8,128)(2,1)S(1)} %get-tuple-element.119.refs_1_, ...), custom_call_target="tpu_custom_call" | custom-call | tf_op jit(solution)/shard_map/attn_more/pallas_call | solution.py:68
  70.8 6.4 %attn_rest.1 = (bf16[144,256]{1,0:T(8,128)(2,1)S(1)}, bf16[256,640]{1,0:T(8,128)(2,1)S(1)}, bf16[256,640]{1,0:T(8,128)(2,1)S(1)}, f32[16,128]{1,0:T(8,128)}, f32[48,128]{1,0:T(8,128)S(1)}) custom-call(bf16[144,768]{1,0:T(8,128)(2,1)S(1)} %get-tuple-element.118.refs_0_, bf16[12,144,640]{2,1,0:T(8,128)(2,1)S(1)} %get-tuple-element.119.refs_1_, ...), custom_call_target="tpu_custom_call" | custom-call | tf_op jit(solution)/shard_map/attn_rest/pallas_call | solution.py:68
  77.2 1.8 %collective-permute-done.8.refs_2_ = bf16[2,384,512]{2,1,0:T(8,128)(2,1)S(1)} collective-permute-done((bf16[2,384,512]{2,1,0:T(8,128)(2,1)S(1)}, bf16[2,384,512]{2,1,0:T(8,128)(2,1)S(1)}, u32[]{:S(2)}, u32[]{:S(2)}) %collective-permute-start.8) | collective-permute-done | bytes 786464 | tf_op jit(solution)/shard_map/ppermute | solution.py:563
  79.2 0.9 collective-permute-done.7.refs_1_
  80.2 2.7 %attn_terms.1 = (bf16[4,96,2304]{2,1,0:T(8,128)(2,1)S(1)}, bf16[4,96,2432]{2,1,0:T(8,128)(2,1)S(1)}) custom-call(f32[48,128]{1,0:T(8,128)S(1)} %get-tuple-element.150.refs_3_.refs_0_.refs_1_, bf16[144,768]{1,0:T(8,128)(2,1)S(1)} %pad_maximum_fusion.refs_6_.refs_0_.refs_1_, bf16[640,768]{1,0:T(8,128)(2,1)S(1)} %get-tuple-element.151.refs_2_, ...), custom_call_target="tpu_custom_call" | custom-call | tf_op jit(solution)/shard_map/attn_terms/pallas_call | solution.py:68
  83.0 1.6 collective-permute-start.11
  84.6 1.5 collective-permute-start.10
  86.1 3.0 %rows_back.1 = (f32[144,768]{1,0:T(8,128)S(1)}, bf16[2,144,768]{2,1,0:T(8,128)(2,1)S(1)}, bf16[1,144,768]{2,1,0:T(8,128)(2,1)S(1)}) custom-call(f32[144,768]{1,0:T(8,128)S(1)} %get-tuple-element.117.refs_0_, bf16[768,768]{1,0:T(8,128)(2,1)S(1)} %get-tuple-element.106.refs_6_.refs_1_, bf16[768,768]{1,0:T(8,128)(2,1)S(1)} %get-tuple-element.104.refs_4_.refs_2_, ...), custom_call_target="tpu_custom_call" | custom-call | tf_op jit(solution)/shard_map/rows_back/pallas_call | solution.py:68
  90.1 12.3 %collective-permute-done.11.refs_1_ = bf16[2,96,1920]{2,1,0:T(8,128)(2,1)S(1)} collective-permute-done((bf16[2,96,1920]{2,1,0:T(8,128)(2,1)S(1)}, bf16[2,96,1920]{2,1,0:T(8,128)(2,1)S(1)}, u32[]{:S(2)}, u32[]{:S(2)}) %collective-permute-start.11) | collective-permute-done | bytes 737312 | tf_op jit(solution)/shard_map/ppermute | solution.py:563
  102.4 1.6 %collective-permute-start.15 = (bf16[1,96,1920]{2,1,0:T(8,128)(2,1)S(1)}, bf16[1,96,1920]{2,1,0:T(8,128)(2,1)S(1)}, u32[]{:S(2)}, u32[]{:S(2)}) collective-permute-start(bf16[1,96,1920]{2,1,0:T(8,128)(2,1)S(1)} %get-tuple-element.169), channel_id=1, source_target_pairs={{0,16},{4,20},{8,24},{12,28},{16,0},{20,4},{24,8},{28,12},{1,17},{... | collective-permute-start | bytes 1105928 | tf_op jit(solution)/shard_map/ppermute | solution.py:563
  104.1 1.5 collective-permute-start.18
  106.1 1.5 collective-permute-start.20
  107.7 2.6 %collective-permute-done.14 = bf16[1,96,1920]{2,1,0:T(8,128)(2,1)S(1)} collective-permute-done((bf16[1,96,1920]{2,1,0:T(8,128)(2,1)S(1)}, bf16[1,96,1920]{2,1,0:T(8,128)(2,1)S(1)}, u32[]{:S(2)}, u32[]{:S(2)}) %collective-permute-start.14) | collective-permute-done | bytes 368672 | tf_op jit(solution)/shard_map/ppermute | solution.py:563
  110.3 3.8 %collective-permute-done.15 = bf16[1,96,1920]{2,1,0:T(8,128)(2,1)S(1)} collective-permute-done((bf16[1,96,1920]{2,1,0:T(8,128)(2,1)S(1)}, bf16[1,96,1920]{2,1,0:T(8,128)(2,1)S(1)}, u32[]{:S(2)}, u32[]{:S(2)}) %collective-permute-start.15) | collective-permute-done | bytes 368672 | tf_op jit(solution)/shard_map/ppermute | solution.py:563
  114.2 2.0 %collective-permute-start.17 = (bf16[2,96,768]{2,1,0:T(8,128)(2,1)S(1)}, bf16[2,96,768]{2,1,0:T(8,128)(2,1)S(1)}, u32[]{:S(2)}, u32[]{:S(2)}) collective-permute-start(bf16[2,96,768]{2,1,0:T(8,128)(2,1)S(1)} %get-tuple-element.172), channel_id=1, source_target_pairs={{0,1},{1,0},{2,3},{3,2},{4,5},{5,4},{6,7},{7,6},{8,9},{9,8},{10,11... | collective-permute-start | bytes 884744 | tf_op jit(solution)/shard_map/ppermute | solution.py:563
  116.2 4.0 %collective-permute-done.18 = bf16[1,96,2432]{2,1,0:T(8,128)(2,1)S(1)} collective-permute-done((bf16[1,96,2432]{2,1,0:T(8,128)(2,1)S(1)}, bf16[1,96,2432]{2,1,0:T(8,128)(2,1)S(1)}, u32[]{:S(2)}, u32[]{:S(2)}) %collective-permute-start.18) | collective-permute-done | bytes 466976 | tf_op jit(solution)/shard_map/ppermute | solution.py:563
  120.3 12.0 %collective-permute-done.19 = bf16[1,96,2432]{2,1,0:T(8,128)(2,1)S(1)} collective-permute-done((bf16[1,96,2432]{2,1,0:T(8,128)(2,1)S(1)}, bf16[1,96,2432]{2,1,0:T(8,128)(2,1)S(1)}, u32[]{:S(2)}, u32[]{:S(2)}) %collective-permute-start.19) | collective-permute-done | bytes 466976 | tf_op jit(solution)/shard_map/ppermute | solution.py:563
  132.7 2.9 %collective-permute-start.25 = (bf16[1,96,768]{2,1,0:T(8,128)(2,1)S(1)}, bf16[1,96,768]{2,1,0:T(8,128)(2,1)S(1)}, u32[]{:S(2)}, u32[]{:S(2)}) collective-permute-start(bf16[1,96,768]{2,1,0:T(8,128)(2,1)S(1)} %get-tuple-element.185), channel_id=1, source_target_pairs={{0,2},{1,3},{2,0},{3,1},{4,6},{5,7},{6,4},{7,5},{8,10},{9,11},{10,... | collective-permute-start | bytes 442376 | tf_op jit(solution)/shard_map/ppermute | solution.py:563
  135.8 2.8 %collective-permute-start.22 = (bf16[1,24,2816]{2,1,0:T(8,128)(2,1)S(1)}, bf16[1,24,2816]{2,1,0:T(8,128)(2,1)S(1)}, u32[]{:S(2)}, u32[]{:S(2)}) collective-permute-start(bf16[1,24,2816]{2,1,0:T(8,128)(2,1)S(1)} %get-tuple-element.182), channel_id=1, source_target_pairs={{0,2},{1,3},{2,0},{3,1},{4,6},{5,7},{6,4},{7,5},{8,10},{9,11},{10,... | collective-permute-start | bytes 405512 | tf_op jit(solution)/shard_map/ppermute | solution.py:563
  138.7 1.4 collective-permute-start.23
  140.0 0.7 rows_result.1.refs_2_
  140.7 14.0 %collective-permute-done.25.refs_1_ = bf16[1,96,768]{2,1,0:T(8,128)(2,1)S(1)} collective-permute-done((bf16[1,96,768]{2,1,0:T(8,128)(2,1)S(1)}, bf16[1,96,768]{2,1,0:T(8,128)(2,1)S(1)}, u32[]{:S(2)}, u32[]{:S(2)}) %collective-permute-start.25) | collective-permute-done | bytes 147488 | tf_op jit(solution)/shard_map/ppermute | solution.py:563
  154.8 0.9 copy-done.7
  155.7 0.7 outer_result.1.refs_2_
  156.5 1.0 copy-done.2
  157.4 0.8 inner_result.1
  158.2 1.0 copy-done.8
  159.2 0.7 attn_result.1
  (82 shorter events, 12.9 us)
Async XLA Ops:
  0.6 15.3 %copy-start.3 = (bf16[768,768]{1,0:T(8,128)(2,1)S(1)}, bf16[768,768]{1,0:T(8,128)(2,1)}, u32[]{:S(2)}) copy-start(bf16[768,768]{1,0:T(8,128)(2,1)} %refs_0_.1) | copy-start | bytes 3538948
  4.7 21.5 %collective-permute-start.2 = (bf16[144,768]{1,0:T(8,128)(2,1)S(1)}, bf16[144,768]{1,0:T(8,128)(2,1)S(1)}, u32[]{:S(2)}, u32[]{:S(2)}) collective-permute-start(bf16[144,768]{1,0:T(8,128)(2,1)S(1)} %pad_maximum_fusion.refs_6_.refs_0_.refs_1_), channel_id=1, source_target_pairs={{0,3},{1,2},{2,1},{3,0},{4,7},{5,6},{6,5},{7,4},{8,11},{9,10},{10,... | collective-permute-start | bytes 663560 | tf_op jit(solution)/shard_map/ppermute | solution.py:563
  9.8 18.8 %collective-permute-start.1 = (bf16[144,768]{1,0:T(8,128)(2,1)S(1)}, bf16[144,768]{1,0:T(8,128)(2,1)S(1)}, u32[]{:S(2)}, u32[]{:S(2)}) collective-permute-start(bf16[144,768]{1,0:T(8,128)(2,1)S(1)} %pad_maximum_fusion.refs_6_.refs_0_.refs_1_), channel_id=1, source_target_pairs={{0,2},{1,3},{2,0},{3,1},{4,6},{5,7},{6,4},{7,5},{8,10},{9,11},{10,... | collective-permute-start | bytes 663560 | tf_op jit(solution)/shard_map/ppermute | solution.py:563
  9.8 18.8 %collective-permute-start = (bf16[144,768]{1,0:T(8,128)(2,1)S(1)}, bf16[144,768]{1,0:T(8,128)(2,1)S(1)}, u32[]{:S(2)}, u32[]{:S(2)}) collective-permute-start(bf16[144,768]{1,0:T(8,128)(2,1)S(1)} %pad_maximum_fusion.refs_6_.refs_0_.refs_1_), channel_id=1, source_target_pairs={{0,1},{1,0},{2,3},{3,2},{4,5},{5,4},{6,7},{7,6},{8,9},{9,8},{10,11... | collective-permute-start | bytes 663560 | tf_op jit(solution)/shard_map/ppermute | solution.py:563
  15.9 2.3 %copy-start = (bf16[768,3072]{1,0:T(8,128)(2,1)S(1)}, bf16[768,3072]{1,0:T(8,128)(2,1)}, u32[]{:S(2)}) copy-start(bf16[768,3072]{1,0:T(8,128)(2,1)} %refs_4_.1) | copy-start | bytes 14155780
  18.3 2.3 %copy-start.1 = (bf16[3072,768]{1,0:T(8,128)(2,1)S(1)}, bf16[3072,768]{1,0:T(8,128)(2,1)}, u32[]{:S(2)}) copy-start(bf16[3072,768]{1,0:T(8,128)(2,1)} %refs_5_.1) | copy-start | bytes 14155780
  20.6 1.3 copy-start.4
  21.9 1.3 copy-start.5
  23.1 1.3 copy-start.6
  24.4 1.7 %copy-start.9 = (f32[12,32]{1,0:T(8,128)S(1)}, f32[12,32]{1,0:T(8,128)}, u32[]{:S(2)}) copy-start(f32[12,32]{1,0:T(8,128)} %param.31) | copy-start | bytes 4612
  24.4 1.7 %copy-start.10 = (f32[12,32]{1,0:T(8,128)S(1)}, f32[12,32]{1,0:T(8,128)}, u32[]{:S(2)}) copy-start(f32[12,32]{1,0:T(8,128)} %param.33) | copy-start | bytes 4612
  24.4 1.7 %copy-start.11 = (f32[12,32]{1,0:T(8,128)S(1)}, f32[12,32]{1,0:T(8,128)}, u32[]{:S(2)}) copy-start(f32[12,32]{1,0:T(8,128)} %param.32) | copy-start | bytes 4612
  43.7 4.5 %collective-permute-start.3 = (bf16[4,384,768]{2,1,0:T(8,128)(2,1)S(1)}, bf16[4,384,768]{2,1,0:T(8,128)(2,1)S(1)}, u32[]{:S(2)}, u32[]{:S(2)}) collective-permute-start(bf16[4,384,768]{2,1,0:T(8,128)(2,1)S(1)} %get-tuple-element.128), channel_id=1, source_target_pairs={{0,4},{4,0},{8,12},{12,8},{16,20},{20,16},{24,28},{28,24},{1,5},{5... | collective-permute-start | bytes 7077896 | tf_op jit(solution)/shard_map/ppermute | solution.py:563
  50.5 12.5 %collective-permute-start.5 = (bf16[4,96,1920]{2,1,0:T(8,128)(2,1)S(1)}, bf16[4,96,1920]{2,1,0:T(8,128)(2,1)S(1)}, u32[]{:S(2)}, u32[]{:S(2)}) collective-permute-start(bf16[4,96,1920]{2,1,0:T(8,128)(2,1)S(1)} %get-tuple-element.136), channel_id=1, source_target_pairs={{0,4},{4,0},{8,12},{12,8},{16,20},{20,16},{24,28},{28,24},{1,5},{5... | collective-permute-start | bytes 4423688 | tf_op jit(solution)/shard_map/ppermute | solution.py:563
  50.7 14.1 %collective-permute-start.4 = (bf16[4,96,1920]{2,1,0:T(8,128)(2,1)S(1)}, bf16[4,96,1920]{2,1,0:T(8,128)(2,1)S(1)}, u32[]{:S(2)}, u32[]{:S(2)}) collective-permute-start(bf16[4,96,1920]{2,1,0:T(8,128)(2,1)S(1)} %get-tuple-element.134), channel_id=1, source_target_pairs={{0,4},{4,0},{8,12},{12,8},{16,20},{20,16},{24,28},{28,24},{1,5},{5... | collective-permute-start | bytes 4423688 | tf_op jit(solution)/shard_map/ppermute | solution.py:563
  51.1 12.0 %collective-permute-start.6 = (bf16[2,384,256]{2,1,0:T(8,128)(2,1)S(1)}, bf16[2,384,256]{2,1,0:T(8,128)(2,1)S(1)}, u32[]{:S(2)}, u32[]{:S(2)}) collective-permute-start(bf16[2,384,256]{2,1,0:T(8,128)(2,1)S(1)} %get-tuple-element.138), channel_id=1, source_target_pairs={{0,8},{4,12},{8,0},{12,4},{16,24},{20,28},{24,16},{28,20},{1,9},{5... | collective-permute-start | bytes 1179656 | tf_op jit(solution)/shard_map/ppermute | solution.py:563
  52.6 26.5 %collective-permute-start.8 = (bf16[2,384,512]{2,1,0:T(8,128)(2,1)S(1)}, bf16[2,384,512]{2,1,0:T(8,128)(2,1)S(1)}, u32[]{:S(2)}, u32[]{:S(2)}) collective-permute-start(bf16[2,384,512]{2,1,0:T(8,128)(2,1)S(1)} %get-tuple-element.153), channel_id=1, source_target_pairs={{0,8},{4,12},{8,0},{12,4},{16,24},{20,28},{24,16},{28,20},{1,9},{5... | collective-permute-start | bytes 2359304 | tf_op jit(solution)/shard_map/ppermute | solution.py:563
  63.2 16.9 %collective-permute-start.7 = (bf16[2,96,1920]{2,1,0:T(8,128)(2,1)S(1)}, bf16[2,96,1920]{2,1,0:T(8,128)(2,1)S(1)}, u32[]{:S(2)}, u32[]{:S(2)}) collective-permute-start(bf16[2,96,1920]{2,1,0:T(8,128)(2,1)S(1)} %get-tuple-element.152), channel_id=1, source_target_pairs={{0,16},{4,20},{8,24},{12,28},{16,0},{20,4},{24,8},{28,12},{1,17},{... | collective-permute-start | bytes 2211848 | tf_op jit(solution)/shard_map/ppermute | solution.py:563
  82.9 6.9 %collective-permute-start.12 = (bf16[4,96,2432]{2,1,0:T(8,128)(2,1)S(1)}, bf16[4,96,2432]{2,1,0:T(8,128)(2,1)S(1)}, u32[]{:S(2)}, u32[]{:S(2)}) collective-permute-start(bf16[4,96,2432]{2,1,0:T(8,128)(2,1)S(1)} %get-tuple-element.162), channel_id=1, source_target_pairs={{0,4},{4,0},{8,12},{12,8},{16,20},{20,16},{24,28},{28,24},{1,5},{5... | collective-permute-start | bytes 5603336 | tf_op jit(solution)/shard_map/ppermute | solution.py:563
  83.0 19.4 %collective-permute-start.11 = (bf16[2,96,1920]{2,1,0:T(8,128)(2,1)S(1)}, bf16[2,96,1920]{2,1,0:T(8,128)(2,1)S(1)}, u32[]{:S(2)}, u32[]{:S(2)}) collective-permute-start(bf16[2,96,1920]{2,1,0:T(8,128)(2,1)S(1)} %get-tuple-element.161), channel_id=1, source_target_pairs={{0,8},{4,12},{8,0},{12,4},{16,24},{20,28},{24,16},{28,20},{1,9},{5... | collective-permute-start | bytes 2211848 | tf_op jit(solution)/shard_map/ppermute | solution.py:563
  84.6 21.0 %collective-permute-start.10 = (bf16[1,384,768]{2,1,0:T(8,128)(2,1)S(1)}, bf16[1,384,768]{2,1,0:T(8,128)(2,1)S(1)}, u32[]{:S(2)}, u32[]{:S(2)}) collective-permute-start(bf16[1,384,768]{2,1,0:T(8,128)(2,1)S(1)} %get-tuple-element.160), channel_id=1, source_target_pairs={{0,16},{4,20},{8,24},{12,28},{16,0},{20,4},{24,8},{28,12},{1,17},{... | collective-permute-start | bytes 1769480 | tf_op jit(solution)/shard_map/ppermute | solution.py:563
  89.1 16.9 %collective-permute-start.9 = (bf16[2,144,768]{2,1,0:T(8,128)(2,1)S(1)}, bf16[2,144,768]{2,1,0:T(8,128)(2,1)S(1)}, u32[]{:S(2)}, u32[]{:S(2)}) collective-permute-start(bf16[2,144,768]{2,1,0:T(8,128)(2,1)S(1)} %get-tuple-element.159), channel_id=1, source_target_pairs={{0,1},{1,0},{2,3},{3,2},{4,5},{5,4},{6,7},{7,6},{8,9},{9,8},{10,11... | collective-permute-start | bytes 1327112 | tf_op jit(solution)/shard_map/ppermute | solution.py:563
  89.2 21.1 %collective-permute-start.14 = (bf16[1,96,1920]{2,1,0:T(8,128)(2,1)S(1)}, bf16[1,96,1920]{2,1,0:T(8,128)(2,1)S(1)}, u32[]{:S(2)}, u32[]{:S(2)}) collective-permute-start(bf16[1,96,1920]{2,1,0:T(8,128)(2,1)S(1)} %get-tuple-element.168), channel_id=1, source_target_pairs={{0,8},{4,12},{8,0},{12,4},{16,24},{20,28},{24,16},{28,20},{1,9},{5... | collective-permute-start | bytes 1105928 | tf_op jit(solution)/shard_map/ppermute | solution.py:563
  102.4 11.6 %collective-permute-start.15 = (bf16[1,96,1920]{2,1,0:T(8,128)(2,1)S(1)}, bf16[1,96,1920]{2,1,0:T(8,128)(2,1)S(1)}, u32[]{:S(2)}, u32[]{:S(2)}) collective-permute-start(bf16[1,96,1920]{2,1,0:T(8,128)(2,1)S(1)} %get-tuple-element.169), channel_id=1, source_target_pairs={{0,16},{4,20},{8,24},{12,28},{16,0},{20,4},{24,8},{28,12},{1,17},{... | collective-permute-start | bytes 1105928 | tf_op jit(solution)/shard_map/ppermute | solution.py:563
  104.1 16.2 %collective-permute-start.18 = (bf16[1,96,2432]{2,1,0:T(8,128)(2,1)S(1)}, bf16[1,96,2432]{2,1,0:T(8,128)(2,1)S(1)}, u32[]{:S(2)}, u32[]{:S(2)}) collective-permute-start(bf16[1,96,2432]{2,1,0:T(8,128)(2,1)S(1)} %get-tuple-element.174), channel_id=1, source_target_pairs={{0,8},{4,12},{8,0},{12,4},{16,24},{20,28},{24,16},{28,20},{1,9},{5... | collective-permute-start | bytes 1400840 | tf_op jit(solution)/shard_map/ppermute | solution.py:563
  105.5 26.7 %collective-permute-start.19 = (bf16[1,96,2432]{2,1,0:T(8,128)(2,1)S(1)}, bf16[1,96,2432]{2,1,0:T(8,128)(2,1)S(1)}, u32[]{:S(2)}, u32[]{:S(2)}) collective-permute-start(bf16[1,96,2432]{2,1,0:T(8,128)(2,1)S(1)} %get-tuple-element.175), channel_id=1, source_target_pairs={{0,16},{4,20},{8,24},{12,28},{16,0},{20,4},{24,8},{28,12},{1,17},{... | collective-permute-start | bytes 1400840 | tf_op jit(solution)/shard_map/ppermute | solution.py:563
  106.1 26.2 %collective-permute-start.20 = (bf16[1,96,2432]{2,1,0:T(8,128)(2,1)S(1)}, bf16[1,96,2432]{2,1,0:T(8,128)(2,1)S(1)}, u32[]{:S(2)}, u32[]{:S(2)}) collective-permute-start(bf16[1,96,2432]{2,1,0:T(8,128)(2,1)S(1)} %get-tuple-element.176), channel_id=1, source_target_pairs={{0,24},{4,28},{8,16},{12,20},{16,8},{20,12},{24,0},{28,4},{1,25},{... | collective-permute-start | bytes 1400840 | tf_op jit(solution)/shard_map/ppermute | solution.py:563
  114.1 18.4 %collective-permute-start.16 = (bf16[2,24,3840]{2,1,0:T(8,128)(2,1)S(1)}, bf16[2,24,3840]{2,1,0:T(8,128)(2,1)S(1)}, u32[]{:S(2)}, u32[]{:S(2)}) collective-permute-start(bf16[2,24,3840]{2,1,0:T(8,128)(2,1)S(1)} %get-tuple-element.171), channel_id=1, source_target_pairs={{0,1},{1,0},{2,3},{3,2},{4,5},{5,4},{6,7},{7,6},{8,9},{9,8},{10,11... | collective-permute-start | bytes 1105928 | tf_op jit(solution)/shard_map/ppermute | solution.py:563
  114.2 18.3 %collective-permute-start.17 = (bf16[2,96,768]{2,1,0:T(8,128)(2,1)S(1)}, bf16[2,96,768]{2,1,0:T(8,128)(2,1)S(1)}, u32[]{:S(2)}, u32[]{:S(2)}) collective-permute-start(bf16[2,96,768]{2,1,0:T(8,128)(2,1)S(1)} %get-tuple-element.172), channel_id=1, source_target_pairs={{0,1},{1,0},{2,3},{3,2},{4,5},{5,4},{6,7},{7,6},{8,9},{9,8},{10,11... | collective-permute-start | bytes 884744 | tf_op jit(solution)/shard_map/ppermute | solution.py:563
  120.3 18.4 %collective-permute-start.13 = (bf16[144,768]{1,0:T(8,128)(2,1)S(1)}, bf16[144,768]{1,0:T(8,128)(2,1)S(1)}, u32[]{:S(2)}, u32[]{:S(2)}) collective-permute-start(bf16[144,768]{1,0:T(8,128)(2,1)S(1)} %get-tuple-element.167), channel_id=1, source_target_pairs={{0,2},{1,3},{2,0},{3,1},{4,6},{5,7},{6,4},{7,5},{8,10},{9,11},{10,... | collective-permute-start | bytes 663560 | tf_op jit(solution)/shard_map/ppermute | solution.py:563
  132.6 23.8 %collective-permute-start.24 = (bf16[1,24,3840]{2,1,0:T(8,128)(2,1)S(1)}, bf16[1,24,3840]{2,1,0:T(8,128)(2,1)S(1)}, u32[]{:S(2)}, u32[]{:S(2)}) collective-permute-start(bf16[1,24,3840]{2,1,0:T(8,128)(2,1)S(1)} %get-tuple-element.184), channel_id=1, source_target_pairs={{0,2},{1,3},{2,0},{3,1},{4,6},{5,7},{6,4},{7,5},{8,10},{9,11},{10,... | collective-permute-start | bytes 552968 | tf_op jit(solution)/shard_map/ppermute | solution.py:563
  132.7 22.1 %collective-permute-start.25 = (bf16[1,96,768]{2,1,0:T(8,128)(2,1)S(1)}, bf16[1,96,768]{2,1,0:T(8,128)(2,1)S(1)}, u32[]{:S(2)}, u32[]{:S(2)}) collective-permute-start(bf16[1,96,768]{2,1,0:T(8,128)(2,1)S(1)} %get-tuple-element.185), channel_id=1, source_target_pairs={{0,2},{1,3},{2,0},{3,1},{4,6},{5,7},{6,4},{7,5},{8,10},{9,11},{10,... | collective-permute-start | bytes 442376 | tf_op jit(solution)/shard_map/ppermute | solution.py:563
  135.6 22.6 %collective-permute-start.21 = (bf16[1,24,2816]{2,1,0:T(8,128)(2,1)S(1)}, bf16[1,24,2816]{2,1,0:T(8,128)(2,1)S(1)}, u32[]{:S(2)}, u32[]{:S(2)}) collective-permute-start(bf16[1,24,2816]{2,1,0:T(8,128)(2,1)S(1)} %get-tuple-element.181), channel_id=1, source_target_pairs={{0,1},{1,0},{2,3},{3,2},{4,5},{5,4},{6,7},{7,6},{8,9},{9,8},{10,11... | collective-permute-start | bytes 405512 | tf_op jit(solution)/shard_map/ppermute | solution.py:563
  135.8 22.4 %collective-permute-start.22 = (bf16[1,24,2816]{2,1,0:T(8,128)(2,1)S(1)}, bf16[1,24,2816]{2,1,0:T(8,128)(2,1)S(1)}, u32[]{:S(2)}, u32[]{:S(2)}) collective-permute-start(bf16[1,24,2816]{2,1,0:T(8,128)(2,1)S(1)} %get-tuple-element.182), channel_id=1, source_target_pairs={{0,2},{1,3},{2,0},{3,1},{4,6},{5,7},{6,4},{7,5},{8,10},{9,11},{10,... | collective-permute-start | bytes 405512 | tf_op jit(solution)/shard_map/ppermute | solution.py:563
  138.7 19.5 %collective-permute-start.23 = (bf16[1,24,2816]{2,1,0:T(8,128)(2,1)S(1)}, bf16[1,24,2816]{2,1,0:T(8,128)(2,1)S(1)}, u32[]{:S(2)}, u32[]{:S(2)}) collective-permute-start(bf16[1,24,2816]{2,1,0:T(8,128)(2,1)S(1)} %get-tuple-element.183), channel_id=1, source_target_pairs={{0,3},{1,2},{2,1},{3,0},{4,7},{5,6},{6,5},{7,4},{8,11},{9,10},{10,... | collective-permute-start | bytes 405512 | tf_op jit(solution)/shard_map/ppermute | solution.py:563
  154.8 0.9 copy-start.7
  156.5 1.0 copy-start.2
  158.2 1.0 copy-start.8

commit v2 on v1

--- a/solution.py
+++ b/solution.py
@@ -311,7 +311,7 @@
 
 
 def attn_back(
-    d_heads, probs, query, keys_all, values_all, query_at, key_at, first_pair, pairs
+    d_heads, probs, query, keys_all, values_all, query_at, key_at, first_pair, pairs, spare=0
 ):
     rows, width = d_heads.shape
     columns = pairs * LANES
@@ -320,8 +320,8 @@
 
     def kernel(*refs):
         d_ref, p_ref, q_ref, k_ref, v_ref, q_at, k_at = refs[:7]
-        dq_ref, dk_ref, dv_ref, tables = refs[7:11]
-        heads_t, q_t, line_idx, key_hots, line_hots, row_hots, line_rows, rolls = refs[11:]
+        dkv_ref, tables = refs[7:9]
+        heads_t, q_t, line_idx, key_hots, line_hots, row_hots, line_rows, rolls = refs[9:]
         base = first_pair * LANES
         heads_t[...] = d_ref[:, base : base + columns].astype(F32).T.astype(BF)
         q_t[...] = q_ref[:, base : base + columns].astype(F32).T.astype(BF)
@@ -365,8 +365,9 @@
                 d_score = p_one * (d_probs - row_dot)
                 low_score = d_score.astype(BF)
                 back.append(dot_nn(low_score, k_pair))
-                dk_ref[own, :] = dot_nn(q_t[own, :], low_score).astype(BF)
-                dv_ref[own, :] = dot_nn(heads_t[own, :], low_probs).astype(BF)
+                below = pl.ds(pl.multiple_of(columns + at * LANES + 64 * half, 64), 64)
+                dkv_ref[own, :] = dot_nn(q_t[own, :], low_score).astype(BF)
+                dkv_ref[below, :] = dot_nn(heads_t[own, :], low_probs).astype(BF)
                 at_keys = dot_nt(low_score, key_hots[...])
                 in_region = all_sum(at_keys[:, LANES:] * region_hot)
                 boxes = at_keys[:, :LANES]
@@ -397,7 +398,7 @@
                 row = row + jnp.where(one_lane == REL - 1, whole - before - within, 0.0)
                 row = row + jnp.where(one_lane == 3 * REL, in_region, 0.0)
                 tables[pl.ds(head, 1), :] = row
-            dq_ref[:, col] = (jnp.where(lane < 64, back[0], back[1]) * 0.125).astype(BF)
+            dkv_ref[2 * columns : 2 * columns + rows, col] = (jnp.where(lane < 64, back[0], back[1]) * 0.125).astype(BF)
             return carry
 
         lax.fori_loop(0, pairs, pair, 0)
@@ -437,9 +438,7 @@
         (d_heads, probs, query, keys_all, values_all, query_at, key_at),
         [vmem()] * 7,
         (
-            like((rows, columns), BF),
-            like((columns, keys), BF),
-            like((columns, keys), BF),
+            like((2 * columns + rows + spare, keys), BF),
             like((16, LANES), F32),
         ),
         [
@@ -479,39 +478,33 @@
 
 def rows_back(d_first, parts, weights, shards):
     rows, width = d_first.shape
-
-    def kernel(*refs):
-        first, wq, wk, wv = refs[:4]
-        part_refs = refs[4 : 4 + 3 * len(parts)]
-        own, send, keep = refs[4 + 3 * len(parts) :]
+    count = width // len(parts)
+
+    def kernel(first, wq, wk, wv, *refs):
+        part_refs, (own, send, keep) = refs[: len(parts)], refs[len(parts) :]
         for at in range(shards - 1, -1, -1):
-            cut = slice(at * rows, (at + 1) * rows)
-            total, place = None, 0
-            for group in range(len(parts)):
-                _, dk, dv = part_refs[3 * group : 3 * group + 3]
-                col = slice(place, place + dk.shape[0])
-                value = dot_nn(wk[:, col], dk[:, cut]) + dot_nn(wv[:, col], dv[:, cut])
+            cut, total = slice(at * rows, (at + 1) * rows), None
+            for group, part in enumerate(part_refs):
+                col = slice(group * count, (group + 1) * count)
+                value = dot_nn(wk[:, col], part[:count, cut])
+                value = value + dot_nn(wv[:, col], part[count : 2 * count, cut])
                 total = value if total is None else total + value
-                place += dk.shape[0]
             if at % 2:
                 send[at // 2] = total.T.astype(BF)
-                continue
-            if at:
+            elif at:
                 keep[at // 2 - 1] = total.T.astype(BF)
-                continue
-            result, place = first[...] + total.T, 0
-            for group in range(len(parts)):
-                dq = part_refs[3 * group]
-                col = slice(place, place + dq.shape[1])
-                result = result + dot_nt(dq[...], wq[:, col])
-                place += dq.shape[1]
-            own[...] = result
-
-    flat = [array for part in parts for array in part]
+            else:
+                result = first[...] + total.T
+                for group, part in enumerate(part_refs):
+                    d_query = part[2 * count : 2 * count + rows, :count]
+                    col = slice(group * count, (group + 1) * count)
+                    result = result + dot_nt(d_query, wq[:, col])
+                own[...] = result
+
     return Stage(
         kernel,
-        (d_first, *weights, *flat),
-        [vmem()] * (4 + len(flat)),
+        (d_first, *weights, *parts),
+        [vmem()] * (4 + len(parts)),
         (
             like((rows, width), F32),
             like((shards // 2, rows, width), BF),
@@ -535,7 +528,12 @@
     return Stage(kernel, (own, got), [vmem()] * 2, (like((row_count, own.shape[1]), BF),))
 
 
-def pack(sums, tables):
+def two_halves(value):
+    high, low = two_parts(value)
+    return jnp.concatenate([high.astype(F32), low.astype(F32)], 0)
+
+
+def pack(sums, tables, spare):
     width = sums[0].shape[1]
     height = sum(item.shape[0] for item in sums) * width // LANES
 
@@ -547,12 +545,16 @@
                     out[place : place + 1] = ref[row : row + 1, cut : cut + LANES]
                     place += 1
         total = refs[len(sums)][...]
-        for ref in refs[len(sums) + 1 : -1]:
+        for ref in refs[len(sums) + 1 : -2]:
             total = total + ref[...]
         out[place : place + total.shape[0]] = total
         out[place + total.shape[0] :] = jnp.zeros_like(out[place + total.shape[0] :])
-
-    operands = (*sums, *tables)
+        high, low = two_parts(out[...])
+        below = refs[-2].shape[0] - high.shape[0]
+        refs[-2][below:, :LANES] = high
+        refs[-2][below:, LANES : 2 * LANES] = low
+
+    operands = (*sums, *tables, spare)
     return Stage(
         kernel, operands, [vmem()] * len(operands), (like((-(-(height + tables[0].shape[0]) // 16) * 16, LANES), F32),)
     )
@@ -565,11 +567,6 @@
 
 def tok_shards(array_in):
     return [array_in] + [swap(array_in, "tok", step) for step in range(1, lax.axis_size("tok"))]
-
-
-def two_halves(value):
-    high, low = two_parts(value)
-    return jnp.concatenate([high.astype(F32), low.astype(F32)], 0)
 
 
 def whole_value(halves):
@@ -830,78 +827,117 @@
         while len(self.path) > left:
             self.halve(after, rider)
 
-    def result(self, columns, after=()):
-        kept, got = self.kept[0], self.got[0]
-
-        def kernel(kept_ref, got_ref, *outs):
-            low = 0
+    def result(self, columns, after=(), side=None):
+        held, rows = len(self.kept), self.kept[0].shape[1]
+        sides = [] if side is None else [side]
+        extra = 0 if side is None else side.shape[1]
+
+        def kernel(*refs):
+            ins, outs = refs[: -len(columns)], refs[-len(columns) :]
+            kept, got, low = ins[:held], ins[held : held + len(self.got)], 0
             for out, width in zip(outs, columns):
-                cut = slice(low, low + width)
-                out[...] = kept_ref[0, :, cut] + got_ref[0, :, cut].astype(F32)
-                low += width
+                own = width - (extra if out is outs[-1] else 0)
+                out[:, :own] = add_columns(kept, got, (0,), low, low + own, F32)
+                low += own
+            if sides:
+                outs[-1][:, columns[-1] - extra :] = ins[-1][...]
 
         stage = Stage(
             kernel,
-            (kept, got),
-            [vmem()] * 2,
-            [like((kept.shape[1], width), F32) for width in columns],
+            (*self.kept, *self.got, *sides),
+            [vmem()] * (held + len(self.got) + len(sides)),
+            [like((rows, width), F32) for width in columns],
         )
         return run([stage], f"{self.name}_result", 4, after)
 
 
 class Direct:
-    def __init__(self, terms, load, name):
-        self.kept, sends = terms
-        self.first = self.kept
-        self.got = [swap(piece, "page", 1) for piece in sends]
-        self.load, self.name = load, name
-
-    def step(self, after):
-        items, rows, cols = self.kept.shape
-        toks = lax.axis_size("tok")
-        sent = [like((1, rows, cols + LANES), BF)] * (items - 1)
-
-        def kernel(kept, load, *refs):
-            got, (own, load_out, *outs) = refs[: len(self.got)], refs[len(self.got) :]
-            value = whole_value(two_halves(load[...]))
-            value = value + whole_value(got[-1][0, :, -LANES:].astype(F32))
+    def __init__(self, tokens_pair, parts_pair, load, side, rows, name, after):
+        pages, toks = lax.axis_size("page"), lax.axis_size("tok")
+        items, keys = pages // 2, tokens_pair[0].shape[0]
+        share = tokens_pair[0].shape[1] // pages
+        cols = 3 * tokens_pair[0].shape[1]
+        count = cols // 3 // len(parts_pair)
+        extra = side.kept[0].shape[2]
+        self.name = name
+
+        def kernel(mine, other, load_ref, side_kept, side_got, *refs):
+            part_refs, refs = refs[: 2 * len(parts_pair)], refs[2 * len(parts_pair) :]
+            own, load_out, side_own = refs[:3]
+            outs, (turned, picked) = refs[3 : 2 + items], refs[2 + items :]
+            page = lax.axis_index("page")
+            for which, ref in enumerate((mine, other)):
+                turned[...] = ref[...].astype(F32).T.astype(BF).reshape(pages, share, keys)
+                for at in range(items):
+                    picked[which, at * share : (at + 1) * share] = turned[page ^ (2 * at)]
+            for group in range(len(parts_pair)):
+                for kind in range(3):
+                    total = None
+                    for which in range(2):
+                        part = part_refs[2 * group + which]
+                        if kind == 0:
+                            d_query = part[2 * count : 2 * count + rows, :count]
+                            value = dot_nn(picked[which, :, :rows], d_query)
+                        else:
+                            used = slice((kind - 1) * count, kind * count)
+                            value = dot_nt(picked[which], part[used, :])
+                        total = value if total is None else total + value
+                    place = kind * (cols // 3) + group * count
+                    col = slice(place, place + count)
+                    own[:, col] = total[:share]
+                    for at in range(1, items):
+                        outs[at - 1][0, :, col] = total[at * share : (at + 1) * share].astype(BF)
+            below = part_refs[-1]
+            height = load_ref.shape[0]
+            value = below[-height:, :LANES].astype(F32) + below[-height:, LANES : 2 * LANES].astype(
+                F32
+            )
+            value = whole_value(two_halves(load_ref[...])) + value
             load_out[...] = value
-            for at in range(items):
-                low = 0
-                for piece in got:
-                    width = min(piece.shape[2], cols - low)
-                    cut = slice(low, low + width)
-                    if at:
-                        outs[at - 1][0, :, cut] = kept[at, :, cut] + piece[at, :, :width]
-                    else:
-                        own[:, cut] = kept[at, :, cut].astype(F32) + piece[at, :, :width].astype(F32)
-                    low += width
-            for out in outs:
-                put_load(out, 0, value)
-
-        operands = (self.kept, self.load, *self.got)
+            side_own[...] = side_kept[0].astype(F32) + side_got[0].astype(F32)
+            for at in range(1, items):
+                outs[at - 1][0, :, cols : cols + extra] = side_kept[at] + side_got[at]
+                put_load(outs[at - 1], 0, value)
+
+        flat = [part for pair in parts_pair for part in pair]
+        operands = (*tokens_pair, load, side.kept[0], side.got[0], *flat)
         stage = Stage(
             kernel,
             operands,
             [vmem()] * len(operands),
-            [like((rows, cols), F32), like(self.load.shape, F32), *sent],
+            [
+                like((share, cols), F32),
+                like(load.shape, F32),
+                like((share, extra), F32),
+                *[like((1, share, cols + extra + LANES), BF)] * (items - 1),
+            ],
+            [
+                pltpu.VMEM((pages, share, keys), BF),
+                pltpu.VMEM((2, items * share, keys), BF),
+            ],
         )
-        own, self.load, *sends = run([stage], f"{self.name}_step1", 6, after)
-        self.last = own
-        self.kept = own.reshape(toks, rows // toks, cols)
+        own, self.load, self.side_own, *sends = run([stage], f"{name}_terms", 10, after)
+        self.first = own
+        self.kept = own.reshape(toks, share // toks, cols)
         self.got = [
-            swap(piece, "page", 2 * (at + 1)).reshape(toks, rows // toks, cols + LANES)
+            swap(piece, "page", 2 * (at + 1)).reshape(toks, share // toks, cols + extra + LANES)
             for at, piece in enumerate(sends)
         ]
 
     def along(self, after):
         toks, rows, cols = self.kept.shape
         blocks = 2 * self.load.shape[0] // rows
-
-        def kernel(kept, load, one, two, three, own, load_out, *outs):
+        extra = self.side_own.shape[1]
+
+        def kernel(kept, load, side_own, one, two, three, own, load_out, side_out, *outs):
             tok = lax.axis_index("tok")
+            for at in range(toks):
+                total = side_own[at * rows : (at + 1) * rows]
+                for piece in (one, two, three):
+                    total = total + piece[at, :, cols : cols + extra].astype(F32)
+                side_out[at * rows : (at + 1) * rows] = total
             halves = [
-                whole_value(piece[:, :, cols:].astype(F32).reshape(toks * rows, LANES))
+                whole_value(piece[:, :, cols + extra :].astype(F32).reshape(toks * rows, LANES))
                 for piece in (one, two, three)
             ]
             mine = whole_value(two_halves(load[...]))
@@ -919,12 +955,18 @@
 
         stage = Stage(
             kernel,
-            (self.kept, self.load, *self.got),
-            [vmem()] * 5,
-            [like((rows, cols), F32), like(self.load.shape, F32)]
+            (self.kept, self.load, self.side_own, *self.got),
+            [vmem()] * 6,
+            [
+                like((rows, cols), F32),
+                like(self.load.shape, F32),
+                like((toks * rows, extra), F32),
+            ]
             + [like((1, rows, cols + blocks * LANES), BF)] * (toks - 1),
         )
-        self.kept, self.load, *sends = run([stage], f"{self.name}_step2", 6, after)
+        self.kept, self.load, self.side_sum, *sends = run(
+            [stage], f"{self.name}_step2", 6, after
+        )
         self.last = self.kept
         self.got = [swap(piece, "tok", at + 1) for at, piece in enumerate(sends)]
 
@@ -960,18 +1002,16 @@
 
 
 class Halved:
-    def __init__(self, terms, load, name):
-        self.sum = Reduction(terms, name)
+    def __init__(self, terms, load, name, side):
+        self.sum, self.side = Reduction(terms, name), side
         self.first = self.sum.kept[0]
         self.rider = Rider(load, list(self.sum.path))
 
-    def step(self, after):
-        self.sum.step(after, self.rider)
-        self.last = self.sum.last
-
     def along(self, after):
         self.sum.until(0, after, self.rider)
-        self.last = self.sum.last
+        self.side.until(0, (self.sum.last,))
+        self.last = self.side.last
+        self.side_sum = self.side.kept[0][0] + self.side.got[0][0].astype(F32)
 
     def result(self, columns, after):
         outs = self.sum.result(columns, after)
@@ -1057,20 +1097,25 @@
         vectors,
         padded(cotangent),
     )
+    unit = width // 6
     terms, outs = with_terms(
         [first, second],
-        [[(second.results[4], second.results[7], "nn")]],
+        [
+            [(second.results[4], Cut(second.results[7], 0, 4 * unit), "nn")],
+            [(second.results[4], Cut(second.results[7], 4 * unit, width), "nn")],
+        ],
         "forward",
         10,
     )
     mix, query, keys_all, values_all, tokens_all, probs, key_at = outs[:7]
     block, hidden, n_one, r_one, active, slope, d_second, d_outer, sums_two = outs[7:]
     outer = Reduction(terms[0], "outer")
+    zed = Reduction(terms[1], "zed", tok_first=True)
     back = feed_back(d_outer, d_second, slope, n_one, r_one, w_inner, w_outer, w_out, vectors)
     d_inner, d_first, d_attn, sums_one, d_heads = run([back], "feed_back", 8, (outer.kept[0],))
-    unit = width // 6
-    outer.step((d_attn,), cuts=[2 * unit, 4 * unit])
-    main = 15 * unit
+    outer.step((d_attn,), cuts=[2 * unit, 2 * unit])
+    zed.halve((outer.last,))
+    main = 16 * unit
     terms, _ = with_terms(
         [],
         [
@@ -1079,73 +1124,83 @@
         ],
         "inner_terms",
         10,
-        (d_attn, outer.last),
+        (d_attn, zed.last),
     )
     inner = Reduction(terms[0], "inner", turn=True)
     out = Reduction(terms[1], "out")
+    whole_tiles = lax.axis_size("page") == 8 and width // lax.axis_size("page") % 16 == 0
     third = width // LANES // 3
 
-    def heads_back(at):
+    def heads_back(at, spare=0):
         return attn_back(
-            d_heads, probs, query, keys_all, values_all, query_at, key_at, at * third, third
+            d_heads, probs, query, keys_all, values_all, query_at, key_at, at * third, third, spare
         )
 
-    *part_one, tables_one = run([heads_back(0)], "attn_back", 10, (out.kept[0],))
-    inner.step((tables_one, *outer.got[:1]), cuts=[15 * unit])
-    out.step((inner.last,), cuts=[15 * unit])
-    *part_two, tables_two = run(
+    def beside(array):
+        return [swap(array, "page", 1)] if whole_tiles else []
+
+    other_tokens = beside(tokens_all)
+
+    part_one, tables_one = run([heads_back(0)], "attn_back", 10, (out.kept[0], ))
+    zed.halve((tables_one, *outer.got[:1]))
+    inner.step((zed.last,), cuts=[16 * unit])
+    out.step((inner.last,), cuts=[14 * unit])
+    others = beside(part_one)
+    part_two, tables_two = run(
         [heads_back(1)], "attn_more", 10, (out.last,)
     )
-    stage = heads_back(2)
-    parts = [part_one, part_two, stage.results[:3]]
-    whole_tiles = lax.axis_size("page") == 8 and width // lax.axis_size("page") % 16 == 0
-    *last_part, _, small = run(
-        [stage, pack((sums_one, sums_two), (tables_one, tables_two, stage.results[3]))],
+    others += beside(part_two)
+    stage = heads_back(2, 48)
+    last_part, _, small = run(
+        [stage, pack((sums_one, sums_two), (tables_one, tables_two, stage.results[1]), stage.results[0])],
         "attn_rest",
         10,
         (tables_two,),
     )
-    parts[2] = last_part
+    parts = [part_one, part_two, last_part]
+    others += beside(last_part)
 
     def attn_sum(after):
-        terms, _ = with_terms(
-            [],
-            [
-                [(padded_tokens, part[0], "nn") for part in parts]
-                + [(tokens_all, part[1], "nt") for part in parts]
-                + [(tokens_all, part[2], "nt") for part in parts]
-            ],
-            "attn_terms",
-            10,
-            after,
-            load=small if whole_tiles else None,
-            cuts=[9],
+        if whole_tiles:
+            return Direct(
+                (tokens_all, *other_tokens),
+                list(zip(parts, others)),
+                small,
+                zed,
+                rows,
+                "attn",
+                after,
+            )
+        count = width // len(parts)
+        groups = (
+            [(padded_tokens, part[2 * count :][:rows, :count], "nn") for part in parts]
+            + [(tokens_all, Cut(part, 0, count), "nt") for part in parts]
+            + [(tokens_all, Cut(part, count, 2 * count), "nt") for part in parts]
         )
-        return (Direct if whole_tiles else Halved)(terms[0], small, "attn")
+        return Halved(plain_terms(groups), small, "attn", zed)
 
     outer.step((small,))
-    inner.step((outer.last,))
-    attn = attn_sum((inner.last, ))
+    inner.step((outer.last, *others[0:1]))
     d_own, rows_sent, rows_kept = run(
-        [rows_back(d_first, parts, (w_query, w_key, w_value), shards)], "rows_back", 10, (attn.first,)
+        [rows_back(d_first, parts, (w_query, w_key, w_value), shards)], "rows_back", 10, (inner.last,)
     )
     rows_got = swap(rows_sent, "tok", 1)
-    attn.step((d_own,))
-    out.step((attn.last,))
-    outer.step((out.last,))
+    out.step((d_own, *others[1:2]))
+    attn = attn_sum((out.last, *outer.got[:3], *inner.got[:2]))
     d_own, rows_sent = run(
-        [rows_step(d_own, rows_kept, rows_got)], "rows_step", 4, (outer.last,)
+        [rows_step(d_own, rows_kept, rows_got)], "rows_step", 4, (attn.first,)
     )
     rows_got = swap(rows_sent, "tok", 2)
     inner.join(out)
     inner.step((d_own,))
-    attn.along((inner.last,))
-    outer.step((attn.last,))
-    inner.step((outer.last,))
-    (d_tokens,) = run([rows_result(d_own, rows_got, row_count)], "rows_result", 4, (inner.last,))
-    (grad_outer,) = outer.result([width], (d_tokens,))
-    grad_inner, grad_out = inner.result([w_inner.shape[1], width], (grad_outer,))
-    grad_attn, small = attn.result([width] * 3, (grad_inner,))
+    outer.step((inner.last,))
+    (d_tokens,) = run([rows_result(d_own, rows_got, row_count)], "rows_result", 4, (outer.last,))
+    inner.step((d_tokens,))
+    outer.step((inner.last,))
+    attn.along((outer.last,))
+    grad_inner, grad_out = inner.result([w_inner.shape[1], width], (attn.last,))
+    (grad_outer,) = outer.result([width], (grad_inner,), attn.side_sum)
+    grad_attn, small = attn.result([width] * 3, (grad_outer,))
     vector_rows = width // LANES
     vector_sums = small[: 4 * vector_rows].reshape(4, width)
     tables = small[4 * vector_rows :][: table_line.shape[0]]

time: 163 us -> 153 us (0.939)
  waiting for transfers between devices: 58.3 us -> 47.4 us
    ppermute x26 -> x32, waiting for transfers between devices: 58.3 us -> 47.4 us  [swap(): lax.ppermute(array_in, axis_name, [(at, at ^ flip) for at in range(size)])]
    ppermute x26 -> x32, starting transfers between devices: 28.3 us -> 29.2 us  [swap(): lax.ppermute(array_in, axis_name, [(at, at ^ flip) for at in range(size)])]
    pallas_call x26 -> x27, Pallas kernels: 51.5 us -> 51.6 us  [run(): pl.pallas_call(kernel, out_shape=tuple(out_shape), in_specs=specs + [pl.B...]
  transfers between devices with their start and end apart: 26 -> 32, of which waited for: 11 -> 12; matrix products, arithmetic and copies ran while one was open for 3% -> 4% of each run, Pallas kernels for 19% -> 22%
where the time goes in v2:
time: 153 us; the launch traced here: 152 us
  Pallas kernels  51.6 us (34%)
  waiting for transfers between devices  47.4 us (31%)
  starting transfers between devices  29.2 us (19%)
  local copies, waits for them, and re-layouts  17.3 us (11%)
  other arithmetic  5.51 us (4%)
    pallas_call x27, Pallas kernels, run(): pl.pallas_call(kernel, out_shape=tuple(out_shape), in_specs=specs + [pl.B...  51.6 us
    ppermute x32, waiting for transfers between devices, swap(): lax.ppermute(array_in, axis_name, [(at, at ^ flip) for at in range(size)])  47.4 us
    ppermute x32, starting transfers between devices, swap(): lax.ppermute(array_in, axis_name, [(at, at ^ flip) for at in range(size)])  29.2 us
    unnamed x24, local copies, waits for them, and re-layouts  11.3 us
  transfers between devices with their start and end apart: 32, of which 12 were waited for; matrix products, arithmetic and copies ran while one was open for 4% of the time, Pallas kernels for 22%

profile of v2, /device:TPU:0, one launch (start us, length us, event | category | flops | bytes accessed | tf_op | source)
XLA Modules:
  0.0 151.9 jit_solution(10777493378278505455)
XLA Ops:
  0.7 0.8 convert.31
  3.6 1.0 pad_maximum_fusion.refs_6_.refs_0_
  4.7 5.1 %collective-permute-start.2 = (bf16[144,768]{1,0:T(8,128)(2,1)S(1)}, bf16[144,768]{1,0:T(8,128)(2,1)S(1)}, u32[]{:S(2)}, u32[]{:S(2)}) collective-permute-start(bf16[144,768]{1,0:T(8,128)(2,1)S(1)} %pad_maximum_fusion.refs_6_.refs_0_), channel_id=1, source_target_pairs={{0,3},{1,2},{2,1},{3,0},{4,7},{5,6},{6,5},{7,4},{8,11},{9,10},{10,... | collective-permute-start | bytes 663560 | tf_op jit(solution)/shard_map/ppermute | solution.py:565
  14.0 1.0 pad.40.refs_14_
  15.1 0.8 broadcast_add_fusion
  15.9 2.3 %copy-done = bf16[768,3072]{1,0:T(8,128)(2,1)S(1)} copy-done((bf16[768,3072]{1,0:T(8,128)(2,1)S(1)}, bf16[768,3072]{1,0:T(8,128)(2,1)}, u32[]{:S(2)}) %copy-start) | copy-done | bytes 4718616
  18.3 2.3 %copy-done.1 = bf16[3072,768]{1,0:T(8,128)(2,1)S(1)} copy-done((bf16[3072,768]{1,0:T(8,128)(2,1)S(1)}, bf16[3072,768]{1,0:T(8,128)(2,1)}, u32[]{:S(2)}) %copy-start.1) | copy-done | bytes 4718616
  20.6 1.3 copy-done.3
  21.9 1.3 copy-done.4
  23.1 1.3 copy-done.5
  24.4 1.6 %fetch.1 = (bf16[768,768]{1,0:T(8,128)(2,1)S(1)}, bf16[768,768]{1,0:T(8,128)(2,1)S(1)}, bf16[768,768]{1,0:T(8,128)(2,1)S(1)}, bf16[768,768]{1,0:T(8,128)(2,1)S(1...) custom-call(bf16[768,768]{1,0:T(8,128)(2,1)S(1)} %copy-done.2, bf16[768,768]{1,0:T(8,128)(2,1)S(1)} %copy-done.3, ...), custom_call_target="tpu_custom_call" | custom-call | tf_op jit(solution)/shard_map/fetch/pallas_call | solution.py:68
  26.2 2.4 %collective-permute-done.1.refs_2_ = bf16[144,768]{1,0:T(8,128)(2,1)S(1)} collective-permute-done((bf16[144,768]{1,0:T(8,128)(2,1)S(1)}, bf16[144,768]{1,0:T(8,128)(2,1)S(1)}, u32[]{:S(2)}, u32[]{:S(2)}) %collective-permute-start.1) | collective-permute-done | bytes 221216 | tf_op jit(solution)/shard_map/ppermute | solution.py:565
  28.6 15.4 %forward.1 = (bf16[144,768]{1,0:T(8,128)(2,1)S(1)}, bf16[144,768]{1,0:T(8,128)(2,1)S(1)}, bf16[640,768]{1,0:T(8,128)(2,1)S(1)}, bf16[640,768]{1,0:T(8,128)(2,1)S...) custom-call(bf16[144,768]{1,0:T(8,128)(2,1)S(1)} %pad_maximum_fusion, ...), custom_call_target="tpu_custom_call" | custom-call | tf_op jit(solution)/shard_map/forward/pallas_call | solution.py:68
  44.5 4.0 %feed_back.1 = (bf16[144,3072]{1,0:T(8,128)(2,1)S(1)}, f32[144,768]{1,0:T(8,128)S(1)}, bf16[144,768]{1,0:T(8,128)(2,1)S(1)}, f32[2,768]{1,0:T(2,128)S(1)}, bf16[144,768]{1,0:T(8,128)(2,1)S(1)}) custom-call(bf16[144,768]{1,0:T(8,128)(2,1)S(1)} %get-tuple-element.111.refs_0_, f32[144,768]{1,0:T(8,128)S(1)} %get-tuple-element.112.refs_1_, ...), custom_call_target="tpu_custom_call" | custom-call | tf_op jit(solution)/shard_map/feed_back/pallas_call | solution.py:68
  48.9 1.9 %inner_terms.1 = (bf16[4,96,2048]{2,1,0:T(8,128)(2,1)S(1)}, bf16[4,96,2048]{2,1,0:T(8,128)(2,1)S(1)}, bf16[4,96,1792]{2,1,0:T(8,128)(2,1)S(1)}, bf16[4,96,1792]{2,1,0:T(8,128)(2,1)S(1)}) custom-call(bf16[144,768]{1,0:T(8,128)(2,1)S(1)} %get-tuple-element.124.refs_0_, bf16[144,3072]{1,0:T(8,128)(2,1)S(1)} %get-tuple-element.125.refs_1_, ...), custom_call_target="tpu_custom_call" | custom-call | tf_op jit(solution)/shard_map/inner_terms/pallas_call | solution.py:68
  51.3 1.5 collective-permute-start.8
  52.9 6.0 %attn_back.1 = (bf16[656,640]{1,0:T(8,128)(2,1)S(1)}, f32[16,128]{1,0:T(8,128)S(1)}) custom-call(bf16[144,768]{1,0:T(8,128)(2,1)S(1)} %get-tuple-element.118.refs_0_, bf16[12,144,640]{2,1,0:T(8,128)(2,1)S(1)} %get-tuple-element.119.refs_1_, bf16[144,768]{1,0:T(8,128)(2,1)S(1)} %get-tuple-element.120.refs_2_, ...), custom_call_target="tpu_custom_call" | custom-call | tf_op jit(solution)/shard_map/attn_back/pallas_call | solution.py:68
  58.9 3.6 %collective-permute-done.8.refs_3_.refs_1_ = bf16[2,384,256]{2,1,0:T(8,128)(2,1)S(1)} collective-permute-done((bf16[2,384,256]{2,1,0:T(8,128)(2,1)S(1)}, bf16[2,384,256]{2,1,0:T(8,128)(2,1)S(1)}, u32[]{:S(2)}, u32[]{:S(2)}) %collective-permute-start.8) | collective-permute-done | bytes 393248 | tf_op jit(solution)/shard_map/ppermute | solution.py:565
  62.4 1.5 collective-permute-start.10
  64.2 1.6 %collective-permute-start.9 = (bf16[2,96,2048]{2,1,0:T(8,128)(2,1)S(1)}, bf16[2,96,2048]{2,1,0:T(8,128)(2,1)S(1)}, u32[]{:S(2)}, u32[]{:S(2)}) collective-permute-start(bf16[2,96,2048]{2,1,0:T(8,128)(2,1)S(1)} %get-tuple-element.149), channel_id=1, source_target_pairs={{0,16},{4,20},{8,24},{12,28},{16,0},{20,4},{24,8},{28,12},{1,17},{... | collective-permute-start | bytes 2359304 | tf_op jit(solution)/shard_map/ppermute | solution.py:565
  65.9 5.8 %attn_more.1 = (bf16[656,640]{1,0:T(8,128)(2,1)S(1)}, f32[16,128]{1,0:T(8,128)S(1)}) custom-call(bf16[144,768]{1,0:T(8,128)(2,1)S(1)} %get-tuple-element.118.refs_0_, bf16[12,144,640]{2,1,0:T(8,128)(2,1)S(1)} %get-tuple-element.119.refs_1_, bf16[144,768]{1,0:T(8,128)(2,1)S(1)} %get-tuple-element.120.refs_2_, ...), custom_call_target="tpu_custom_call" | custom-call | tf_op jit(solution)/shard_map/attn_more/pallas_call | solution.py:68
  71.9 0.8 collective-permute-done.10.refs_2_
  72.7 1.5 collective-permute-start.17
  74.2 6.4 %attn_rest.1 = (bf16[704,640]{1,0:T(8,128)(2,1)S(1)}, f32[16,128]{1,0:T(8,128)}, f32[48,128]{1,0:T(8,128)S(1)}) custom-call(bf16[144,768]{1,0:T(8,128)(2,1)S(1)} %get-tuple-element.118.refs_0_, bf16[12,144,640]{2,1,0:T(8,128)(2,1)S(1)} %get-tuple-element.119.refs_1_, bf16[144,768]{1,0:T(8,128)(2,1)S(1)} %get-tuple-element.120.refs_2_, ...), custom_call_target="tpu_custom_call" | custom-call | tf_op jit(solution)/shard_map/attn_rest/pallas_call | solution.py:68
  80.6 3.6 %collective-permute-done.9.refs_1_ = bf16[2,96,2048]{2,1,0:T(8,128)(2,1)S(1)} collective-permute-done((bf16[2,96,2048]{2,1,0:T(8,128)(2,1)S(1)}, bf16[2,96,2048]{2,1,0:T(8,128)(2,1)S(1)}, u32[]{:S(2)}, u32[]{:S(2)}) %collective-permute-start.9) | collective-permute-done | bytes 786464 | tf_op jit(solution)/shard_map/ppermute | solution.py:565
  84.2 1.0 collective-permute-start.14
  85.4 1.6 %collective-permute-start.18 = (bf16[1,384,512]{2,1,0:T(8,128)(2,1)S(1)}, bf16[1,384,512]{2,1,0:T(8,128)(2,1)S(1)}, u32[]{:S(2)}, u32[]{:S(2)}) collective-permute-start(bf16[1,384,512]{2,1,0:T(8,128)(2,1)S(1)} %get-tuple-element.161), channel_id=1, source_target_pairs={{0,16},{4,20},{8,24},{12,28},{16,0},{20,4},{24,8},{28,12},{1,17},{... | collective-permute-start | bytes 1179656 | tf_op jit(solution)/shard_map/ppermute | solution.py:565
  87.0 2.6 %collective-permute-done.17.refs_1_ = bf16[2,96,1792]{2,1,0:T(8,128)(2,1)S(1)} collective-permute-done((bf16[2,96,1792]{2,1,0:T(8,128)(2,1)S(1)}, bf16[2,96,1792]{2,1,0:T(8,128)(2,1)S(1)}, u32[]{:S(2)}, u32[]{:S(2)}) %collective-permute-start.17) | collective-permute-done | bytes 688160 | tf_op jit(solution)/shard_map/ppermute | solution.py:565
  90.1 3.0 %rows_back.1 = (f32[144,768]{1,0:T(8,128)S(1)}, bf16[2,144,768]{2,1,0:T(8,128)(2,1)S(1)}, bf16[1,144,768]{2,1,0:T(8,128)(2,1)S(1)}) custom-call(f32[144,768]{1,0:T(8,128)S(1)} %get-tuple-element.117.refs_0_, bf16[768,768]{1,0:T(8,128)(2,1)S(1)} %get-tuple-element.106.refs_6_.refs_1_, bf16[768,768]{1,0:T(8,128)(2,1)S(1)} %get-tuple-element.104.refs_4_.refs_2_, ...), custom_call_target="tpu_custom_call" | custom-call | tf_op jit(solution)/shard_map/rows_back/pallas_call | solution.py:68
  93.3 2.5 %collective-permute-done.14.refs_4_ = bf16[4,96,256]{2,1,0:T(8,128)(2,1)S(1)} collective-permute-done((bf16[4,96,256]{2,1,0:T(8,128)(2,1)S(1)}, bf16[4,96,256]{2,1,0:T(8,128)(2,1)S(1)}, u32[]{:S(2)}, u32[]{:S(2)}) %collective-permute-start.14) | collective-permute-done | bytes 196640 | tf_op jit(solution)/shard_map/ppermute | solution.py:565
  95.8 1.5 %collective-permute-start.21 = (bf16[1,96,1792]{2,1,0:T(8,128)(2,1)S(1)}, bf16[1,96,1792]{2,1,0:T(8,128)(2,1)S(1)}, u32[]{:S(2)}, u32[]{:S(2)}) collective-permute-start(bf16[1,96,1792]{2,1,0:T(8,128)(2,1)S(1)} %get-tuple-element.166), channel_id=1, source_target_pairs={{0,16},{4,20},{8,24},{12,28},{16,0},{20,4},{24,8},{28,12},{1,17},{... | collective-permute-start | bytes 1032200 | tf_op jit(solution)/shard_map/ppermute | solution.py:565
  97.3 1.9 %collective-permute-done.19.refs_13_ = bf16[1,96,2048]{2,1,0:T(8,128)(2,1)S(1)} collective-permute-done((bf16[1,96,2048]{2,1,0:T(8,128)(2,1)S(1)}, bf16[1,96,2048]{2,1,0:T(8,128)(2,1)S(1)}, u32[]{:S(2)}, u32[]{:S(2)}) %collective-permute-start.19) | collective-permute-done | bytes 393248 | tf_op jit(solution)/shard_map/ppermute | solution.py:565
  99.2 2.9 %attn_terms.1 = (f32[96,2304]{1,0:T(8,128)S(1)}, f32[48,128]{1,0:T(8,128)S(1)}, f32[96,256]{1,0:T(8,128)S(1)}, bf16[1,96,2688]{2,1,0:T(8,128)(2,1)S(1)}, bf16[1,...) custom-call(bf16[640,768]{1,0:T(8,128)(2,1)S(1)} %get-tuple-element.157.refs_0_, ...), custom_call_target="tpu_custom_call" | custom-call | tf_op jit(solution)/shard_map/attn_terms/pallas_call | solution.py:68
  102.8 2.9 %collective-permute-start.24 = (bf16[1,96,2688]{2,1,0:T(8,128)(2,1)S(1)}, bf16[1,96,2688]{2,1,0:T(8,128)(2,1)S(1)}, u32[]{:S(2)}, u32[]{:S(2)}) collective-permute-start(bf16[1,96,2688]{2,1,0:T(8,128)(2,1)S(1)} %get-tuple-element.173), channel_id=1, source_target_pairs={{0,24},{4,28},{8,16},{12,20},{16,8},{20,12},{24,0},{28,4},{1,25},{... | collective-permute-start | bytes 1548296 | tf_op jit(solution)/shard_map/ppermute | solution.py:565
  105.8 1.4 collective-permute-start.20
  107.3 1.8 %collective-permute-start.26 = (bf16[2,24,3840]{2,1,0:T(8,128)(2,1)S(1)}, bf16[2,24,3840]{2,1,0:T(8,128)(2,1)S(1)}, u32[]{:S(2)}, u32[]{:S(2)}) collective-permute-start(bf16[2,24,3840]{2,1,0:T(8,128)(2,1)S(1)} %get-tuple-element.175), channel_id=1, source_target_pairs={{0,1},{1,0},{2,3},{3,2},{4,5},{5,4},{6,7},{7,6},{8,9},{9,8},{10,11... | collective-permute-start | bytes 1105928 | tf_op jit(solution)/shard_map/ppermute | solution.py:565
  109.1 7.2 %collective-permute-done.20.refs_1_ = bf16[144,768]{1,0:T(8,128)(2,1)S(1)} collective-permute-done((bf16[144,768]{1,0:T(8,128)(2,1)S(1)}, bf16[144,768]{1,0:T(8,128)(2,1)S(1)}, u32[]{:S(2)}, u32[]{:S(2)}) %collective-permute-start.20) | collective-permute-done | bytes 221216 | tf_op jit(solution)/shard_map/ppermute | solution.py:565
  117.0 5.2 %collective-permute-done.26.refs_1_ = bf16[2,24,3840]{2,1,0:T(8,128)(2,1)S(1)} collective-permute-done((bf16[2,24,3840]{2,1,0:T(8,128)(2,1)S(1)}, bf16[2,24,3840]{2,1,0:T(8,128)(2,1)S(1)}, u32[]{:S(2)}, u32[]{:S(2)}) %collective-permute-start.26) | collective-permute-done | bytes 368672 | tf_op jit(solution)/shard_map/ppermute | solution.py:565
  122.2 0.9 copy-done.7
  123.3 2.3 %collective-permute-done.25.refs_1_ = bf16[2,96,512]{2,1,0:T(8,128)(2,1)S(1)} collective-permute-done((bf16[2,96,512]{2,1,0:T(8,128)(2,1)S(1)}, bf16[2,96,512]{2,1,0:T(8,128)(2,1)S(1)}, u32[]{:S(2)}, u32[]{:S(2)}) %collective-permute-start.25) | collective-permute-done | bytes 196640 | tf_op jit(solution)/shard_map/ppermute | solution.py:565
  125.6 2.2 %collective-permute-done.23 = bf16[1,96,2688]{2,1,0:T(8,128)(2,1)S(1)} collective-permute-done((bf16[1,96,2688]{2,1,0:T(8,128)(2,1)S(1)}, bf16[1,96,2688]{2,1,0:T(8,128)(2,1)S(1)}, u32[]{:S(2)}, u32[]{:S(2)}) %collective-permute-start.23) | collective-permute-done | bytes 516128 | tf_op jit(solution)/shard_map/ppermute | solution.py:565
  128.1 2.6 %collective-permute-start.28 = (bf16[1,24,2816]{2,1,0:T(8,128)(2,1)S(1)}, bf16[1,24,2816]{2,1,0:T(8,128)(2,1)S(1)}, u32[]{:S(2)}, u32[]{:S(2)}) collective-permute-start(bf16[1,24,2816]{2,1,0:T(8,128)(2,1)S(1)} %get-tuple-element.181), channel_id=1, source_target_pairs={{0,2},{1,3},{2,0},{3,1},{4,6},{5,7},{6,4},{7,5},{8,10},{9,11},{10,... | collective-permute-start | bytes 405512 | tf_op jit(solution)/shard_map/ppermute | solution.py:565
  130.7 1.8 %collective-permute-start.29 = (bf16[1,24,2816]{2,1,0:T(8,128)(2,1)S(1)}, bf16[1,24,2816]{2,1,0:T(8,128)(2,1)S(1)}, u32[]{:S(2)}, u32[]{:S(2)}) collective-permute-start(bf16[1,24,2816]{2,1,0:T(8,128)(2,1)S(1)} %get-tuple-element.182), channel_id=1, source_target_pairs={{0,3},{1,2},{2,1},{3,0},{4,7},{5,6},{6,5},{7,4},{8,11},{9,10},{10,... | collective-permute-start | bytes 405512 | tf_op jit(solution)/shard_map/ppermute | solution.py:565
  132.5 0.8 inner_result.1
  133.3 13.3 %collective-permute-done.30.refs_1_ = bf16[1,96,512]{2,1,0:T(8,128)(2,1)S(1)} collective-permute-done((bf16[1,96,512]{2,1,0:T(8,128)(2,1)S(1)}, bf16[1,96,512]{2,1,0:T(8,128)(2,1)S(1)}, u32[]{:S(2)}, u32[]{:S(2)}) %collective-permute-start.30) | collective-permute-done | bytes 98336 | tf_op jit(solution)/shard_map/ppermute | solution.py:565
  146.6 1.0 copy-done.8
  147.5 0.7 outer_result.1.refs_5_
  148.3 1.0 copy-done.6
  (95 shorter events, 14.3 us)
Async XLA Ops:
  0.6 15.3 %copy-start.2 = (bf16[768,768]{1,0:T(8,128)(2,1)S(1)}, bf16[768,768]{1,0:T(8,128)(2,1)}, u32[]{:S(2)}) copy-start(bf16[768,768]{1,0:T(8,128)(2,1)} %refs_0_.1) | copy-start | bytes 3538948
  4.7 21.5 %collective-permute-start.2 = (bf16[144,768]{1,0:T(8,128)(2,1)S(1)}, bf16[144,768]{1,0:T(8,128)(2,1)S(1)}, u32[]{:S(2)}, u32[]{:S(2)}) collective-permute-start(bf16[144,768]{1,0:T(8,128)(2,1)S(1)} %pad_maximum_fusion.refs_6_.refs_0_), channel_id=1, source_target_pairs={{0,3},{1,2},{2,1},{3,0},{4,7},{5,6},{6,5},{7,4},{8,11},{9,10},{10,... | collective-permute-start | bytes 663560 | tf_op jit(solution)/shard_map/ppermute | solution.py:565
  9.8 18.8 %collective-permute-start.1 = (bf16[144,768]{1,0:T(8,128)(2,1)S(1)}, bf16[144,768]{1,0:T(8,128)(2,1)S(1)}, u32[]{:S(2)}, u32[]{:S(2)}) collective-permute-start(bf16[144,768]{1,0:T(8,128)(2,1)S(1)} %pad_maximum_fusion.refs_6_.refs_0_), channel_id=1, source_target_pairs={{0,2},{1,3},{2,0},{3,1},{4,6},{5,7},{6,4},{7,5},{8,10},{9,11},{10,... | collective-permute-start | bytes 663560 | tf_op jit(solution)/shard_map/ppermute | solution.py:565
  9.8 18.8 %collective-permute-start = (bf16[144,768]{1,0:T(8,128)(2,1)S(1)}, bf16[144,768]{1,0:T(8,128)(2,1)S(1)}, u32[]{:S(2)}, u32[]{:S(2)}) collective-permute-start(bf16[144,768]{1,0:T(8,128)(2,1)S(1)} %pad_maximum_fusion.refs_6_.refs_0_), channel_id=1, source_target_pairs={{0,1},{1,0},{2,3},{3,2},{4,5},{5,4},{6,7},{7,6},{8,9},{9,8},{10,11... | collective-permute-start | bytes 663560 | tf_op jit(solution)/shard_map/ppermute | solution.py:565
  15.9 2.3 %copy-start = (bf16[768,3072]{1,0:T(8,128)(2,1)S(1)}, bf16[768,3072]{1,0:T(8,128)(2,1)}, u32[]{:S(2)}) copy-start(bf16[768,3072]{1,0:T(8,128)(2,1)} %refs_4_.1) | copy-start | bytes 14155780
  18.3 2.3 %copy-start.1 = (bf16[3072,768]{1,0:T(8,128)(2,1)S(1)}, bf16[3072,768]{1,0:T(8,128)(2,1)}, u32[]{:S(2)}) copy-start(bf16[3072,768]{1,0:T(8,128)(2,1)} %refs_5_.1) | copy-start | bytes 14155780
  20.6 1.3 copy-start.3
  21.9 1.3 copy-start.4
  23.1 1.3 copy-start.5
  24.4 1.7 %copy-start.9 = (f32[12,32]{1,0:T(8,128)S(1)}, f32[12,32]{1,0:T(8,128)}, u32[]{:S(2)}) copy-start(f32[12,32]{1,0:T(8,128)} %param.31) | copy-start | bytes 4612
  24.4 1.7 %copy-start.10 = (f32[12,32]{1,0:T(8,128)S(1)}, f32[12,32]{1,0:T(8,128)}, u32[]{:S(2)}) copy-start(f32[12,32]{1,0:T(8,128)} %param.33) | copy-start | bytes 4612
  24.4 1.7 %copy-start.11 = (f32[12,32]{1,0:T(8,128)S(1)}, f32[12,32]{1,0:T(8,128)}, u32[]{:S(2)}) copy-start(f32[12,32]{1,0:T(8,128)} %param.32) | copy-start | bytes 4612
  44.0 4.5 %collective-permute-start.4 = (bf16[4,384,512]{2,1,0:T(8,128)(2,1)S(1)}, bf16[4,384,512]{2,1,0:T(8,128)(2,1)S(1)}, u32[]{:S(2)}, u32[]{:S(2)}) collective-permute-start(bf16[4,384,512]{2,1,0:T(8,128)(2,1)S(1)} %get-tuple-element.130), channel_id=1, source_target_pairs={{0,4},{4,0},{8,12},{12,8},{16,20},{20,16},{24,28},{28,24},{1,5},{5... | collective-permute-start | bytes 4718600 | tf_op jit(solution)/shard_map/ppermute | solution.py:565
  44.0 4.7 %collective-permute-start.3 = (bf16[4,384,256]{2,1,0:T(8,128)(2,1)S(1)}, bf16[4,384,256]{2,1,0:T(8,128)(2,1)S(1)}, u32[]{:S(2)}, u32[]{:S(2)}) collective-permute-start(bf16[4,384,256]{2,1,0:T(8,128)(2,1)S(1)} %get-tuple-element.129), channel_id=1, source_target_pairs={{0,4},{4,0},{8,12},{12,8},{16,20},{20,16},{24,28},{28,24},{1,5},{5... | collective-permute-start | bytes 2359304 | tf_op jit(solution)/shard_map/ppermute | solution.py:565
  50.8 13.2 %collective-permute-start.6 = (bf16[4,96,2048]{2,1,0:T(8,128)(2,1)S(1)}, bf16[4,96,2048]{2,1,0:T(8,128)(2,1)S(1)}, u32[]{:S(2)}, u32[]{:S(2)}) collective-permute-start(bf16[4,96,2048]{2,1,0:T(8,128)(2,1)S(1)} %get-tuple-element.137), channel_id=1, source_target_pairs={{0,4},{4,0},{8,12},{12,8},{16,20},{20,16},{24,28},{28,24},{1,5},{5... | collective-permute-start | bytes 4718600 | tf_op jit(solution)/shard_map/ppermute | solution.py:565
  50.9 14.9 %collective-permute-start.5 = (bf16[4,96,1792]{2,1,0:T(8,128)(2,1)S(1)}, bf16[4,96,1792]{2,1,0:T(8,128)(2,1)S(1)}, u32[]{:S(2)}, u32[]{:S(2)}) collective-permute-start(bf16[4,96,1792]{2,1,0:T(8,128)(2,1)S(1)} %get-tuple-element.135), channel_id=1, source_target_pairs={{0,4},{4,0},{8,12},{12,8},{16,20},{20,16},{24,28},{28,24},{1,5},{5... | collective-permute-start | bytes 4128776 | tf_op jit(solution)/shard_map/ppermute | solution.py:565
  51.3 11.1 %collective-permute-start.8 = (bf16[2,384,256]{2,1,0:T(8,128)(2,1)S(1)}, bf16[2,384,256]{2,1,0:T(8,128)(2,1)S(1)}, u32[]{:S(2)}, u32[]{:S(2)}) collective-permute-start(bf16[2,384,256]{2,1,0:T(8,128)(2,1)S(1)} %get-tuple-element.140), channel_id=1, source_target_pairs={{0,8},{4,12},{8,0},{12,4},{16,24},{20,28},{24,16},{28,20},{1,9},{5... | collective-permute-start | bytes 1179656 | tf_op jit(solution)/shard_map/ppermute | solution.py:565
  52.8 11.1 %collective-permute-start.7 = (bf16[8,96,256]{2,1,0:T(8,128)(2,1)S(1)}, bf16[8,96,256]{2,1,0:T(8,128)(2,1)S(1)}, u32[]{:S(2)}, u32[]{:S(2)}) collective-permute-start(bf16[8,96,256]{2,1,0:T(8,128)(2,1)S(1)} %get-tuple-element.138), channel_id=1, source_target_pairs={{0,1},{1,0},{2,3},{3,2},{4,5},{5,4},{6,7},{7,6},{8,9},{9,8},{10,11... | collective-permute-start | bytes 1179656 | tf_op jit(solution)/shard_map/ppermute | solution.py:565
  58.9 21.7 %collective-permute-start.11 = (bf16[656,640]{1,0:T(8,128)(2,1)S(1)}, bf16[656,640]{1,0:T(8,128)(2,1)S(1)}, u32[]{:S(2)}, u32[]{:S(2)}) collective-permute-start(bf16[656,640]{1,0:T(8,128)(2,1)S(1)} %get-tuple-element.134.refs_4_.refs_5_), channel_id=1, source_target_pairs={{0,4},{4,0},{8,12},{12,8},{16,20},{20,16},{24,28},{28,24},{1,5},{5... | collective-permute-start | bytes 2519048 | tf_op jit(solution)/shard_map/ppermute | solution.py:565
  62.4 10.3 %collective-permute-start.10 = (bf16[2,384,256]{2,1,0:T(8,128)(2,1)S(1)}, bf16[2,384,256]{2,1,0:T(8,128)(2,1)S(1)}, u32[]{:S(2)}, u32[]{:S(2)}) collective-permute-start(bf16[2,384,256]{2,1,0:T(8,128)(2,1)S(1)} %get-tuple-element.150), channel_id=1, source_target_pairs={{0,8},{4,12},{8,0},{12,4},{16,24},{20,28},{24,16},{28,20},{1,9},{5... | collective-permute-start | bytes 1179656 | tf_op jit(solution)/shard_map/ppermute | solution.py:565
  63.9 21.4 %collective-permute-start.13 = (bf16[640,768]{1,0:T(8,128)(2,1)S(1)}, bf16[640,768]{1,0:T(8,128)(2,1)S(1)}, u32[]{:S(2)}, u32[]{:S(2)}) collective-permute-start(bf16[640,768]{1,0:T(8,128)(2,1)S(1)} %get-tuple-element.157.refs_0_), channel_id=1, source_target_pairs={{0,4},{4,0},{8,12},{12,8},{16,20},{20,16},{24,28},{28,24},{1,5},{5... | collective-permute-start | bytes 2949128 | tf_op jit(solution)/shard_map/ppermute | solution.py:565
  64.2 20.0 %collective-permute-start.9 = (bf16[2,96,2048]{2,1,0:T(8,128)(2,1)S(1)}, bf16[2,96,2048]{2,1,0:T(8,128)(2,1)S(1)}, u32[]{:S(2)}, u32[]{:S(2)}) collective-permute-start(bf16[2,96,2048]{2,1,0:T(8,128)(2,1)S(1)} %get-tuple-element.149), channel_id=1, source_target_pairs={{0,16},{4,20},{8,24},{12,28},{16,0},{20,4},{24,8},{28,12},{1,17},{... | collective-permute-start | bytes 2359304 | tf_op jit(solution)/shard_map/ppermute | solution.py:565
  71.7 21.4 %collective-permute-start.15 = (bf16[656,640]{1,0:T(8,128)(2,1)S(1)}, bf16[656,640]{1,0:T(8,128)(2,1)S(1)}, u32[]{:S(2)}, u32[]{:S(2)}) collective-permute-start(bf16[656,640]{1,0:T(8,128)(2,1)S(1)} %get-tuple-element.144.refs_5_.refs_7_), channel_id=1, source_target_pairs={{0,4},{4,0},{8,12},{12,8},{16,20},{20,16},{24,28},{28,24},{1,5},{5... | collective-permute-start | bytes 2519048 | tf_op jit(solution)/shard_map/ppermute | solution.py:565
  72.7 16.9 %collective-permute-start.17 = (bf16[2,96,1792]{2,1,0:T(8,128)(2,1)S(1)}, bf16[2,96,1792]{2,1,0:T(8,128)(2,1)S(1)}, u32[]{:S(2)}, u32[]{:S(2)}) collective-permute-start(bf16[2,96,1792]{2,1,0:T(8,128)(2,1)S(1)} %get-tuple-element.159), channel_id=1, source_target_pairs={{0,8},{4,12},{8,0},{12,4},{16,24},{20,28},{24,16},{28,20},{1,9},{5... | collective-permute-start | bytes 2064392 | tf_op jit(solution)/shard_map/ppermute | solution.py:565
  80.6 16.7 %collective-permute-start.16 = (bf16[704,640]{1,0:T(8,128)(2,1)S(1)}, bf16[704,640]{1,0:T(8,128)(2,1)S(1)}, u32[]{:S(2)}, u32[]{:S(2)}) collective-permute-start(bf16[704,640]{1,0:T(8,128)(2,1)S(1)} %get-tuple-element.148.refs_6_.refs_9_), channel_id=1, source_target_pairs={{0,4},{4,0},{8,12},{12,8},{16,20},{20,16},{24,28},{28,24},{1,5},{5... | collective-permute-start | bytes 2703368 | tf_op jit(solution)/shard_map/ppermute | solution.py:565
  84.2 11.6 %collective-permute-start.14 = (bf16[4,96,256]{2,1,0:T(8,128)(2,1)S(1)}, bf16[4,96,256]{2,1,0:T(8,128)(2,1)S(1)}, u32[]{:S(2)}, u32[]{:S(2)}) collective-permute-start(bf16[4,96,256]{2,1,0:T(8,128)(2,1)S(1)} %get-tuple-element.158), channel_id=1, source_target_pairs={{0,2},{1,3},{2,0},{3,1},{4,6},{5,7},{6,4},{7,5},{8,10},{9,11},{10,... | collective-permute-start | bytes 589832 | tf_op jit(solution)/shard_map/ppermute | solution.py:565
  85.4 11.9 %collective-permute-start.18 = (bf16[1,384,512]{2,1,0:T(8,128)(2,1)S(1)}, bf16[1,384,512]{2,1,0:T(8,128)(2,1)S(1)}, u32[]{:S(2)}, u32[]{:S(2)}) collective-permute-start(bf16[1,384,512]{2,1,0:T(8,128)(2,1)S(1)} %get-tuple-element.161), channel_id=1, source_target_pairs={{0,16},{4,20},{8,24},{12,28},{16,0},{20,4},{24,8},{28,12},{1,17},{... | collective-permute-start | bytes 1179656 | tf_op jit(solution)/shard_map/ppermute | solution.py:565
  89.6 9.6 %collective-permute-start.19 = (bf16[1,96,2048]{2,1,0:T(8,128)(2,1)S(1)}, bf16[1,96,2048]{2,1,0:T(8,128)(2,1)S(1)}, u32[]{:S(2)}, u32[]{:S(2)}) collective-permute-start(bf16[1,96,2048]{2,1,0:T(8,128)(2,1)S(1)} %get-tuple-element.162), channel_id=1, source_target_pairs={{0,8},{4,12},{8,0},{12,4},{16,24},{20,28},{24,16},{28,20},{1,9},{5... | collective-permute-start | bytes 1179656 | tf_op jit(solution)/shard_map/ppermute | solution.py:565
  93.1 12.6 %collective-permute-start.12 = (bf16[2,144,768]{2,1,0:T(8,128)(2,1)S(1)}, bf16[2,144,768]{2,1,0:T(8,128)(2,1)S(1)}, u32[]{:S(2)}, u32[]{:S(2)}) collective-permute-start(bf16[2,144,768]{2,1,0:T(8,128)(2,1)S(1)} %get-tuple-element.156), channel_id=1, source_target_pairs={{0,1},{1,0},{2,3},{3,2},{4,5},{5,4},{6,7},{7,6},{8,9},{9,8},{10,11... | collective-permute-start | bytes 1327112 | tf_op jit(solution)/shard_map/ppermute | solution.py:565
  95.8 11.5 %collective-permute-start.21 = (bf16[1,96,1792]{2,1,0:T(8,128)(2,1)S(1)}, bf16[1,96,1792]{2,1,0:T(8,128)(2,1)S(1)}, u32[]{:S(2)}, u32[]{:S(2)}) collective-permute-start(bf16[1,96,1792]{2,1,0:T(8,128)(2,1)S(1)} %get-tuple-element.166), channel_id=1, source_target_pairs={{0,16},{4,20},{8,24},{12,28},{16,0},{20,4},{24,8},{28,12},{1,17},{... | collective-permute-start | bytes 1032200 | tf_op jit(solution)/shard_map/ppermute | solution.py:565
  102.1 23.5 %collective-permute-start.22 = (bf16[1,96,2688]{2,1,0:T(8,128)(2,1)S(1)}, bf16[1,96,2688]{2,1,0:T(8,128)(2,1)S(1)}, u32[]{:S(2)}, u32[]{:S(2)}) collective-permute-start(bf16[1,96,2688]{2,1,0:T(8,128)(2,1)S(1)} %get-tuple-element.171), channel_id=1, source_target_pairs={{0,8},{4,12},{8,0},{12,4},{16,24},{20,28},{24,16},{28,20},{1,9},{5... | collective-permute-start | bytes 1548296 | tf_op jit(solution)/shard_map/ppermute | solution.py:565
  102.5 25.3 %collective-permute-start.23 = (bf16[1,96,2688]{2,1,0:T(8,128)(2,1)S(1)}, bf16[1,96,2688]{2,1,0:T(8,128)(2,1)S(1)}, u32[]{:S(2)}, u32[]{:S(2)}) collective-permute-start(bf16[1,96,2688]{2,1,0:T(8,128)(2,1)S(1)} %get-tuple-element.172), channel_id=1, source_target_pairs={{0,16},{4,20},{8,24},{12,28},{16,0},{20,4},{24,8},{28,12},{1,17},{... | collective-permute-start | bytes 1548296 | tf_op jit(solution)/shard_map/ppermute | solution.py:565
  102.8 25.0 %collective-permute-start.24 = (bf16[1,96,2688]{2,1,0:T(8,128)(2,1)S(1)}, bf16[1,96,2688]{2,1,0:T(8,128)(2,1)S(1)}, u32[]{:S(2)}, u32[]{:S(2)}) collective-permute-start(bf16[1,96,2688]{2,1,0:T(8,128)(2,1)S(1)} %get-tuple-element.173), channel_id=1, source_target_pairs={{0,24},{4,28},{8,16},{12,20},{16,8},{20,12},{24,0},{28,4},{1,25},{... | collective-permute-start | bytes 1548296 | tf_op jit(solution)/shard_map/ppermute | solution.py:565
  105.8 10.5 %collective-permute-start.20 = (bf16[144,768]{1,0:T(8,128)(2,1)S(1)}, bf16[144,768]{1,0:T(8,128)(2,1)S(1)}, u32[]{:S(2)}, u32[]{:S(2)}) collective-permute-start(bf16[144,768]{1,0:T(8,128)(2,1)S(1)} %get-tuple-element.165), channel_id=1, source_target_pairs={{0,2},{1,3},{2,0},{3,1},{4,6},{5,7},{6,4},{7,5},{8,10},{9,11},{10,... | collective-permute-start | bytes 663560 | tf_op jit(solution)/shard_map/ppermute | solution.py:565
  107.3 14.9 %collective-permute-start.26 = (bf16[2,24,3840]{2,1,0:T(8,128)(2,1)S(1)}, bf16[2,24,3840]{2,1,0:T(8,128)(2,1)S(1)}, u32[]{:S(2)}, u32[]{:S(2)}) collective-permute-start(bf16[2,24,3840]{2,1,0:T(8,128)(2,1)S(1)} %get-tuple-element.175), channel_id=1, source_target_pairs={{0,1},{1,0},{2,3},{3,2},{4,5},{5,4},{6,7},{7,6},{8,9},{9,8},{10,11... | collective-permute-start | bytes 1105928 | tf_op jit(solution)/shard_map/ppermute | solution.py:565
  116.3 9.3 %collective-permute-start.25 = (bf16[2,96,512]{2,1,0:T(8,128)(2,1)S(1)}, bf16[2,96,512]{2,1,0:T(8,128)(2,1)S(1)}, u32[]{:S(2)}, u32[]{:S(2)}) collective-permute-start(bf16[2,96,512]{2,1,0:T(8,128)(2,1)S(1)} %get-tuple-element.174), channel_id=1, source_target_pairs={{0,1},{1,0},{2,3},{3,2},{4,5},{5,4},{6,7},{7,6},{8,9},{9,8},{10,11... | collective-permute-start | bytes 589832 | tf_op jit(solution)/shard_map/ppermute | solution.py:565
  122.2 0.9 copy-start.7
  123.2 9.3 %collective-permute-start.31 = (bf16[1,24,3840]{2,1,0:T(8,128)(2,1)S(1)}, bf16[1,24,3840]{2,1,0:T(8,128)(2,1)S(1)}, u32[]{:S(2)}, u32[]{:S(2)}) collective-permute-start(bf16[1,24,3840]{2,1,0:T(8,128)(2,1)S(1)} %get-tuple-element.185), channel_id=1, source_target_pairs={{0,2},{1,3},{2,0},{3,1},{4,6},{5,7},{6,4},{7,5},{8,10},{9,11},{10,... | collective-permute-start | bytes 552968 | tf_op jit(solution)/shard_map/ppermute | solution.py:565
  128.0 20.2 %collective-permute-start.27 = (bf16[1,24,2816]{2,1,0:T(8,128)(2,1)S(1)}, bf16[1,24,2816]{2,1,0:T(8,128)(2,1)S(1)}, u32[]{:S(2)}, u32[]{:S(2)}) collective-permute-start(bf16[1,24,2816]{2,1,0:T(8,128)(2,1)S(1)} %get-tuple-element.180), channel_id=1, source_target_pairs={{0,1},{1,0},{2,3},{3,2},{4,5},{5,4},{6,7},{7,6},{8,9},{9,8},{10,11... | collective-permute-start | bytes 405512 | tf_op jit(solution)/shard_map/ppermute | solution.py:565
  128.1 20.2 %collective-permute-start.28 = (bf16[1,24,2816]{2,1,0:T(8,128)(2,1)S(1)}, bf16[1,24,2816]{2,1,0:T(8,128)(2,1)S(1)}, u32[]{:S(2)}, u32[]{:S(2)}) collective-permute-start(bf16[1,24,2816]{2,1,0:T(8,128)(2,1)S(1)} %get-tuple-element.181), channel_id=1, source_target_pairs={{0,2},{1,3},{2,0},{3,1},{4,6},{5,7},{6,4},{7,5},{8,10},{9,11},{10,... | collective-permute-start | bytes 405512 | tf_op jit(solution)/shard_map/ppermute | solution.py:565
  130.7 17.6 %collective-permute-start.29 = (bf16[1,24,2816]{2,1,0:T(8,128)(2,1)S(1)}, bf16[1,24,2816]{2,1,0:T(8,128)(2,1)S(1)}, u32[]{:S(2)}, u32[]{:S(2)}) collective-permute-start(bf16[1,24,2816]{2,1,0:T(8,128)(2,1)S(1)} %get-tuple-element.182), channel_id=1, source_target_pairs={{0,3},{1,2},{2,1},{3,0},{4,7},{5,6},{6,5},{7,4},{8,11},{9,10},{10,... | collective-permute-start | bytes 405512 | tf_op jit(solution)/shard_map/ppermute | solution.py:565
  132.5 14.1 %collective-permute-start.30 = (bf16[1,96,512]{2,1,0:T(8,128)(2,1)S(1)}, bf16[1,96,512]{2,1,0:T(8,128)(2,1)S(1)}, u32[]{:S(2)}, u32[]{:S(2)}) collective-permute-start(bf16[1,96,512]{2,1,0:T(8,128)(2,1)S(1)} %get-tuple-element.183), channel_id=1, source_target_pairs={{0,2},{1,3},{2,0},{3,1},{4,6},{5,7},{6,4},{7,5},{8,10},{9,11},{10,... | collective-permute-start | bytes 294920 | tf_op jit(solution)/shard_map/ppermute | solution.py:565
  146.6 1.0 copy-start.8
  148.3 1.0 copy-start.6

commit v3 on v2

--- a/solution.py
+++ b/solution.py
@@ -109,7 +109,58 @@
     return jnp.where(key_at[4:5, :] > 0, bucket + same, 2 * REL)
 
 
-def attn_forward(token_shards, row_count, weights, line_table, box_table, query_at):
+def with_places(tokens, places, rows):
+    count, width = tokens.shape
+
+    def kernel(tok, region, line, horiz, vert, out, work):
+        work[:count] = tok[...].astype(F32)
+        work[count:] = jnp.zeros((rows - count, width), F32)
+        lines = (
+            (rows - 2, 0, region[...]),
+            (rows - 2, 256, line[...] >> 5),
+            (rows - 2, 512, line[...] & 31),
+            (rows - 1, 0, horiz[...]),
+            (rows - 1, 256, vert[...]),
+        )
+        for row, lane, value in lines:
+            work[row : row + 1, lane : lane + count] = value.astype(F32).reshape(1, count)
+        out[...] = work[...].astype(BF)
+
+    return Stage(
+        kernel,
+        (tokens, *places),
+        [vmem()] * 5,
+        (like((rows, width), BF),),
+        [pltpu.VMEM((rows, width), F32)],
+    )
+
+
+def first_rows(token_shards, weights):
+    rows, width = token_shards[0].shape
+    shards = len(token_shards)
+
+    def kernel(*refs):
+        tok_refs, (wk, wv, wq, q_ref, k_ref, v_ref, x_ref) = refs[:shards], refs[shards:]
+        for at in range(shards):
+            x_ref[at * rows : (at + 1) * rows] = tok_refs[at][...]
+        q_ref[...] = (dot_nn(tok_refs[0][...], wq[...]) * 0.125).astype(BF)
+        k_ref[...] = dot_nn(x_ref[...], wk[...]).astype(BF)
+        v_ref[...] = dot_nn(x_ref[...], wv[...]).astype(BF)
+
+    return Stage(
+        kernel,
+        (*token_shards, *weights),
+        [vmem()] * (shards + 3),
+        (
+            like((rows, width), BF),
+            like((shards * rows, width), BF),
+            like((shards * rows, width), BF),
+        ),
+        [pltpu.VMEM((shards * rows, width), BF)],
+    )
+
+
+def attn_forward(token_shards, row_count, ready, weights, line_table, box_table, query_at):
     rows, width = token_shards[0].shape
     head_count = line_table.shape[0]
     shards = len(token_shards)
@@ -117,9 +168,9 @@
 
     def kernel(*refs):
         tok_refs = refs[:shards]
-        wk, wv, wq, line_ref, box_ref, q_at = refs[shards : shards + 6]
-        mix_ref, q_ref, k_ref, v_ref, x_ref, p_ref, k_at = refs[shards + 6 : shards + 13]
-        line_idx, box_idx, hots = refs[shards + 13 :]
+        q_in, k_in, v_in, wk, wv, line_ref, box_ref, q_at = refs[shards : shards + 8]
+        mix_ref, q_ref, k_ref, v_ref, x_ref, p_ref, k_at = refs[shards + 8 : shards + 15]
+        line_idx, box_idx, hots = refs[shards + 15 :]
         places = [jnp.zeros((16, keys), F32)] * 3
         for at in range(shards):
             info = tok_refs[at][rows - 16 :, :].astype(F32)
@@ -141,9 +192,12 @@
             x_ref[at * rows : (at + 1) * rows] = tok_refs[at][...]
         if keys > shards * rows:
             x_ref[shards * rows :] = jnp.zeros((keys - shards * rows, width), BF)
-        k_ref[...] = dot_nn(x_ref[...], wk[...]).astype(BF)
-        v_ref[...] = dot_nn(x_ref[...], wv[...]).astype(BF)
-        q_ref[...] = (dot_nn(tok_refs[0][...], wq[...]) * 0.125).astype(BF)
+        done = k_in.shape[0]
+        q_ref[...] = q_in[...]
+        k_ref[:done] = k_in[...]
+        v_ref[:done] = v_in[...]
+        k_ref[done:] = dot_nn(x_ref[done:], wk[...]).astype(BF)
+        v_ref[done:] = dot_nn(x_ref[done:], wv[...]).astype(BF)
         line_idx[...] = line_index(q_at, k_at)
         lane = lax.broadcasted_iota(I32, (rows, LANES), 1)
         place = jnp.where(lane < BOXES, q_at[:, 2:3], q_at[:, 3:4])
@@ -185,8 +239,8 @@
 
     return Stage(
         kernel,
-        (*token_shards, *weights, line_table, box_table, query_at),
-        [vmem()] * (shards + 6),
+        (*token_shards, *ready, *weights, line_table, box_table, query_at),
+        [vmem()] * (shards + 8),
         (
             like((rows, width), BF),
             like((rows, width), BF),
@@ -230,12 +284,13 @@
 
     hidden_units = w_inner.shape[1]
 
-    def kernel(mix_ref, tok, wo, wi, wu, vec, cot, *outs):
-        block, hid, n_one, r_one, act, slope, d_sec, d_out, sums, total = outs
+    def kernel(mix_ref, tok, wo, wi, wu, cot, *refs):
+        vec = [ref[...].reshape(1, width) for ref in refs[:4]]
+        block, hid, n_one, r_one, act, slope, d_sec, d_out, sums, total = refs[4:]
         n, r = normal(tok[...].astype(F32) + dot_nn(mix_ref[...], wo[...]))
         n_one[...] = n
         r_one[...] = jnp.broadcast_to(r, r_one.shape)
-        hidden = n * vec[0:1, :] + vec[1:2, :]
+        hidden = n * vec[0] + vec[1]
         hid[...] = hidden.astype(BF)
         total[...] = hidden
         for cut in range(0, hidden_units, FF_CUT):
@@ -247,18 +302,20 @@
             slope[:, cut : cut + FF_CUT] = upper + inner * bell
             total[...] += dot_nn(active, wu[cut : cut + FF_CUT, :])
         n, r = normal(total[...])
-        block[...] = (n * vec[2:3, :] + vec[3:4, :])[:row_count].astype(BF)
-        grad = cot[...].astype(F32)
+        block[...] = (n * vec[2] + vec[3])[:row_count].astype(BF)
+        total[:row_count] = cot[...].astype(F32)
+        total[row_count:] = jnp.zeros((rows - row_count, width), F32)
+        grad = total[...]
         sums[0:1, :] = jnp.sum(grad * n, axis=0, keepdims=True)
         sums[1:2, :] = jnp.sum(grad, axis=0, keepdims=True)
-        second = normal_back(grad * vec[2:3, :], n, r)
+        second = normal_back(grad * vec[2], n, r)
         d_sec[...] = second
         d_out[...] = second.astype(BF)
 
     return Stage(
         kernel,
-        (mix, tokens, w_out, w_inner, w_outer, vectors, cotangent),
-        [vmem()] * 7,
+        (mix, tokens, w_out, w_inner, w_outer, cotangent, *vectors),
+        [vmem()] * 10,
         (
             like((row_count, width), BF),
             like((rows, width), BF),
@@ -274,7 +331,7 @@
     )
 
 
-def feed_back(d_outer, d_second, slope, n_one, r_one, w_inner, w_outer, w_out, vectors):
+def feed_back(d_outer, d_second, slope, n_one, r_one, w_inner, w_outer, w_out, gain_one):
     rows, width = d_outer.shape
     hidden_units = w_inner.shape[1]
 
@@ -291,14 +348,14 @@
         n = n_ref[...]
         sums[0:1, :] = jnp.sum(d_hidden * n, axis=0, keepdims=True)
         sums[1:2, :] = jnp.sum(d_hidden, axis=0, keepdims=True)
-        first = normal_back(d_hidden * vec[0:1, :], n, r_ref[:, 0:1])
+        first = normal_back(d_hidden * vec[...].reshape(1, width), n, r_ref[:, 0:1])
         d_first[...] = first
         d_attn[...] = first.astype(BF)
         d_heads[...] = dot_nt(d_attn[...], wo[...]).astype(BF)
 
     return Stage(
         kernel,
-        (d_outer, d_second, slope, n_one, r_one, w_inner, w_outer, w_out, vectors),
+        (d_outer, d_second, slope, n_one, r_one, w_inner, w_outer, w_out, gain_one),
         [vmem()] * 9,
         (
             like((rows, hidden_units), BF),
@@ -1045,20 +1102,8 @@
     shards = lax.axis_size("tok")
     rows = -(-(row_count + 2) // 16) * 16
 
-    def padded(array_in):
-        return jnp.pad(array_in, ((0, rows - row_count), (0, 0)))
-
-    def spread(*lines):
-        return jnp.concatenate(
-            [jnp.pad(line, (0, 256 - row_count)) for line in lines]
-            + [jnp.zeros(width - 256 * len(lines), I32)]
-        )
-
-    info = jnp.stack(
-        [spread(region_ids, line_pos // 32, line_pos % 32), spread(box_horiz, box_vert)]
-    ).astype(BF)
-    padded_tokens = jnp.concatenate(
-        [tokens, jnp.zeros((rows - row_count - 2, width), BF), info], 0
+    (padded_tokens,) = run(
+        [with_places(tokens, (region_ids, line_pos, box_horiz, box_vert), rows)], "places", 4
     )
     token_shards = tok_shards(padded_tokens)
     places = jnp.stack([region_ids, line_pos, box_horiz, box_vert], 1)
@@ -1074,15 +1119,19 @@
     box_table = jnp.pad(
         jnp.concatenate([table_horiz, table_vert], 1), ((0, 0), (0, LANES - 2 * REL))
     )
-    vectors = jnp.stack([gain_one, shift_one, gain_two, shift_two], 0)
+    vectors = (gain_one, shift_one, gain_two, shift_two)
 
     w_query, w_key, w_value, w_out, w_inner, w_outer = run(
         [fetch((w_query, w_key, w_value, w_out, w_inner, w_outer))], "fetch", 1, (padded_tokens,)
+    )
+    ready = run(
+        [first_rows(token_shards[:2], (w_key, w_value, w_query))], "first_rows", 6
     )
     first = attn_forward(
         token_shards,
         row_count,
-        (w_key, w_value, w_query),
+        ready,
+        (w_key, w_value),
         line_table,
         box_table,
         query_at,
@@ -1095,7 +1144,7 @@
         w_inner,
         w_outer,
         vectors,
-        padded(cotangent),
+        cotangent,
     )
     unit = width // 6
     terms, outs = with_terms(
@@ -1111,7 +1160,7 @@
     block, hidden, n_one, r_one, active, slope, d_second, d_outer, sums_two = outs[7:]
     outer = Reduction(terms[0], "outer")
     zed = Reduction(terms[1], "zed", tok_first=True)
-    back = feed_back(d_outer, d_second, slope, n_one, r_one, w_inner, w_outer, w_out, vectors)
+    back = feed_back(d_outer, d_second, slope, n_one, r_one, w_inner, w_outer, w_out, gain_one)
     d_inner, d_first, d_attn, sums_one, d_heads = run([back], "feed_back", 8, (outer.kept[0],))
     outer.step((d_attn,), cuts=[2 * unit, 2 * unit])
     zed.halve((outer.last,))

time: 153 us -> 152 us (level)
  other arithmetic: 5.51 us -> 1.59 us
    unnamed x24 -> x44, local copies, waits for them, and re-layouts: 11.3 us -> 16.3 us
    another operation x5 -> x0, other arithmetic: 2.85 us -> none
    another operation x6 -> x0, local copies, waits for them, and re-layouts: 2.77 us -> none  [the longest x4 2.76 us: on_device(): vectors = jnp.stack([gain_one, shift_one, gain_two, shift_two], 0)]
    pallas_call x27 -> x29, Pallas kernels: 51.6 us -> 52.1 us  [run(): pl.pallas_call(kernel, out_shape=tuple(out_shape), in_specs=specs + [pl.B...]
  transfers between devices with their start and end apart: 32 -> 32, of which waited for: 12 -> 13; matrix products, arithmetic and copies ran while one was open for 4% -> 1% of each run, Pallas kernels for 22% -> 23%
where the time goes in v3:
time: 152 us; the launch traced here: 151 us
  Pallas kernels  52.1 us (34%)
  waiting for transfers between devices  48.7 us (32%)
  starting transfers between devices  29.1 us (19%)
  local copies, waits for them, and re-layouts  18.4 us (12%)
  other arithmetic  1.59 us (1%)
    pallas_call x29, Pallas kernels, run(): pl.pallas_call(kernel, out_shape=tuple(out_shape), in_specs=specs + [pl.B...  52.1 us
    ppermute x32, waiting for transfers between devices, swap(): lax.ppermute(array_in, axis_name, [(at, at ^ flip) for at in range(size)])  48.7 us
    ppermute x32, starting transfers between devices, swap(): lax.ppermute(array_in, axis_name, [(at, at ^ flip) for at in range(size)])  29.1 us
    unnamed x44, local copies, waits for them, and re-layouts  16.3 us
  transfers between devices with their start and end apart: 32, of which 13 were waited for; matrix products, arithmetic and copies ran while one was open for 1% of the time, Pallas kernels for 23%

profile of v3, /device:TPU:0, one launch (start us, length us, event | category | flops | bytes accessed | tf_op | source)
XLA Modules:
  0.0 151.0 jit_solution(13966276483006897437)
XLA Ops:
  0.7 0.9 copy-done.9
  4.3 5.1 %collective-permute-start.2 = (bf16[144,768]{1,0:T(8,128)(2,1)S(1)}, bf16[144,768]{1,0:T(8,128)(2,1)S(1)}, u32[]{:S(2)}, u32[]{:S(2)}) collective-permute-start(bf16[144,768]{1,0:T(8,128)(2,1)S(1)} %places.1.refs_6_.refs_0_), channel_id=1, source_target_pairs={{0,3},{1,2},{2,1},{3,0},{4,7},{5,6},{6,5},{7,4},{8,11},{9,10},{10,... | collective-permute-start | bytes 663560 | tf_op jit(solution)/shard_map/ppermute | solution.py:622
  11.0 0.8 broadcast_add_fusion
  11.8 2.3 %copy-done = bf16[768,3072]{1,0:T(8,128)(2,1)S(1)} copy-done((bf16[768,3072]{1,0:T(8,128)(2,1)S(1)}, bf16[768,3072]{1,0:T(8,128)(2,1)}, u32[]{:S(2)}) %copy-start) | copy-done | bytes 4718616
  14.2 2.3 %copy-done.1 = bf16[3072,768]{1,0:T(8,128)(2,1)S(1)} copy-done((bf16[3072,768]{1,0:T(8,128)(2,1)S(1)}, bf16[3072,768]{1,0:T(8,128)(2,1)}, u32[]{:S(2)}) %copy-start.1) | copy-done | bytes 4718616
  16.5 1.3 copy-done.2
  17.8 1.3 copy-done.3
  19.0 1.3 copy-done.4
  20.3 1.3 copy-done.5
  21.6 1.6 %fetch.1 = (bf16[768,768]{1,0:T(8,128)(2,1)S(1)}, bf16[768,768]{1,0:T(8,128)(2,1)S(1)}, bf16[768,768]{1,0:T(8,128)(2,1)S(1)}, bf16[768,768]{1,0:T(8,128)(2,1)S(1...) custom-call(bf16[768,768]{1,0:T(8,128)(2,1)S(1)} %copy-done.2, bf16[768,768]{1,0:T(8,128)(2,1)S(1)} %copy-done.3, ...), custom_call_target="tpu_custom_call" | custom-call | tf_op jit(solution)/shard_map/fetch/pallas_call | solution.py:68
  23.7 1.1 first_rows.1
  24.8 3.4 %collective-permute-done.1.refs_2_ = bf16[144,768]{1,0:T(8,128)(2,1)S(1)} collective-permute-done((bf16[144,768]{1,0:T(8,128)(2,1)S(1)}, bf16[144,768]{1,0:T(8,128)(2,1)S(1)}, u32[]{:S(2)}, u32[]{:S(2)}) %collective-permute-start.1) | collective-permute-done | bytes 221216 | tf_op jit(solution)/shard_map/ppermute | solution.py:622
  28.3 14.8 %forward.1 = (bf16[144,768]{1,0:T(8,128)(2,1)S(1)}, bf16[144,768]{1,0:T(8,128)(2,1)S(1)}, bf16[640,768]{1,0:T(8,128)(2,1)S(1)}, bf16[640,768]{1,0:T(8,128)(2,1)S...) custom-call(bf16[144,768]{1,0:T(8,128)(2,1)S(1)} %places.1.refs_6_.r, ...), custom_call_target="tpu_custom_call" | custom-call | tf_op jit(solution)/shard_map/forward/pallas_call | solution.py:68
  43.6 4.0 %feed_back.1 = (bf16[144,3072]{1,0:T(8,128)(2,1)S(1)}, f32[144,768]{1,0:T(8,128)S(1)}, bf16[144,768]{1,0:T(8,128)(2,1)S(1)}, f32[2,768]{1,0:T(2,128)S(1)}, bf16[144,768]{1,0:T(8,128)(2,1)S(1)}) custom-call(bf16[144,768]{1,0:T(8,128)(2,1)S(1)} %get-tuple-element.117.refs_0_, f32[144,768]{1,0:T(8,128)S(1)} %get-tuple-element.118.refs_1_, ...), custom_call_target="tpu_custom_call" | custom-call | tf_op jit(solution)/shard_map/feed_back/pallas_call | solution.py:68
  47.9 1.9 %inner_terms.1 = (bf16[4,96,2048]{2,1,0:T(8,128)(2,1)S(1)}, bf16[4,96,2048]{2,1,0:T(8,128)(2,1)S(1)}, bf16[4,96,1792]{2,1,0:T(8,128)(2,1)S(1)}, bf16[4,96,1792]{2,1,0:T(8,128)(2,1)S(1)}) custom-call(bf16[144,768]{1,0:T(8,128)(2,1)S(1)} %get-tuple-element.130.refs_0_, bf16[144,3072]{1,0:T(8,128)(2,1)S(1)} %get-tuple-element.131.refs_1_, ...), custom_call_target="tpu_custom_call" | custom-call | tf_op jit(solution)/shard_map/inner_terms/pallas_call | solution.py:68
  50.4 1.5 collective-permute-start.8
  51.9 6.0 %attn_back.1 = (bf16[656,640]{1,0:T(8,128)(2,1)S(1)}, f32[16,128]{1,0:T(8,128)S(1)}) custom-call(bf16[144,768]{1,0:T(8,128)(2,1)S(1)} %get-tuple-element.124.refs_0_, bf16[12,144,640]{2,1,0:T(8,128)(2,1)S(1)} %get-tuple-element.125.refs_1_, bf16[144,768]{1,0:T(8,128)(2,1)S(1)} %get-tuple-element.126.refs_2_, ...), custom_call_target="tpu_custom_call" | custom-call | tf_op jit(solution)/shard_map/attn_back/pallas_call | solution.py:68
  57.9 3.6 %collective-permute-done.8.refs_3_.refs_1_ = bf16[2,384,256]{2,1,0:T(8,128)(2,1)S(1)} collective-permute-done((bf16[2,384,256]{2,1,0:T(8,128)(2,1)S(1)}, bf16[2,384,256]{2,1,0:T(8,128)(2,1)S(1)}, u32[]{:S(2)}, u32[]{:S(2)}) %collective-permute-start.8) | collective-permute-done | bytes 393248 | tf_op jit(solution)/shard_map/ppermute | solution.py:622
  61.5 1.5 collective-permute-start.10
  63.2 1.6 %collective-permute-start.9 = (bf16[2,96,2048]{2,1,0:T(8,128)(2,1)S(1)}, bf16[2,96,2048]{2,1,0:T(8,128)(2,1)S(1)}, u32[]{:S(2)}, u32[]{:S(2)}) collective-permute-start(bf16[2,96,2048]{2,1,0:T(8,128)(2,1)S(1)} %get-tuple-element.155), channel_id=1, source_target_pairs={{0,16},{4,20},{8,24},{12,28},{16,0},{20,4},{24,8},{28,12},{1,17},{... | collective-permute-start | bytes 2359304 | tf_op jit(solution)/shard_map/ppermute | solution.py:622
  65.0 5.8 %attn_more.1 = (bf16[656,640]{1,0:T(8,128)(2,1)S(1)}, f32[16,128]{1,0:T(8,128)S(1)}) custom-call(bf16[144,768]{1,0:T(8,128)(2,1)S(1)} %get-tuple-element.124.refs_0_, bf16[12,144,640]{2,1,0:T(8,128)(2,1)S(1)} %get-tuple-element.125.refs_1_, bf16[144,768]{1,0:T(8,128)(2,1)S(1)} %get-tuple-element.126.refs_2_, ...), custom_call_target="tpu_custom_call" | custom-call | tf_op jit(solution)/shard_map/attn_more/pallas_call | solution.py:68
  71.7 1.5 collective-permute-start.17
  73.2 6.4 %attn_rest.1 = (bf16[704,640]{1,0:T(8,128)(2,1)S(1)}, f32[16,128]{1,0:T(8,128)}, f32[48,128]{1,0:T(8,128)S(1)}) custom-call(bf16[144,768]{1,0:T(8,128)(2,1)S(1)} %get-tuple-element.124.refs_0_, bf16[12,144,640]{2,1,0:T(8,128)(2,1)S(1)} %get-tuple-element.125.refs_1_, bf16[144,768]{1,0:T(8,128)(2,1)S(1)} %get-tuple-element.126.refs_2_, ...), custom_call_target="tpu_custom_call" | custom-call | tf_op jit(solution)/shard_map/attn_rest/pallas_call | solution.py:68
  79.7 3.6 %collective-permute-done.9.refs_1_ = bf16[2,96,2048]{2,1,0:T(8,128)(2,1)S(1)} collective-permute-done((bf16[2,96,2048]{2,1,0:T(8,128)(2,1)S(1)}, bf16[2,96,2048]{2,1,0:T(8,128)(2,1)S(1)}, u32[]{:S(2)}, u32[]{:S(2)}) %collective-permute-start.9) | collective-permute-done | bytes 786464 | tf_op jit(solution)/shard_map/ppermute | solution.py:622
  83.2 1.0 collective-permute-start.14
  84.4 1.6 %collective-permute-start.18 = (bf16[1,384,512]{2,1,0:T(8,128)(2,1)S(1)}, bf16[1,384,512]{2,1,0:T(8,128)(2,1)S(1)}, u32[]{:S(2)}, u32[]{:S(2)}) collective-permute-start(bf16[1,384,512]{2,1,0:T(8,128)(2,1)S(1)} %get-tuple-element.167), channel_id=1, source_target_pairs={{0,16},{4,20},{8,24},{12,28},{16,0},{20,4},{24,8},{28,12},{1,17},{... | collective-permute-start | bytes 1179656 | tf_op jit(solution)/shard_map/ppermute | solution.py:622
  86.0 2.6 %collective-permute-done.17.refs_1_ = bf16[2,96,1792]{2,1,0:T(8,128)(2,1)S(1)} collective-permute-done((bf16[2,96,1792]{2,1,0:T(8,128)(2,1)S(1)}, bf16[2,96,1792]{2,1,0:T(8,128)(2,1)S(1)}, u32[]{:S(2)}, u32[]{:S(2)}) %collective-permute-start.17) | collective-permute-done | bytes 688160 | tf_op jit(solution)/shard_map/ppermute | solution.py:622
  89.2 3.0 %rows_back.1 = (f32[144,768]{1,0:T(8,128)S(1)}, bf16[2,144,768]{2,1,0:T(8,128)(2,1)S(1)}, bf16[1,144,768]{2,1,0:T(8,128)(2,1)S(1)}) custom-call(f32[144,768]{1,0:T(8,128)S(1)} %get-tuple-element.123.refs_0_, bf16[768,768]{1,0:T(8,128)(2,1)S(1)} %get-tuple-element.109.refs_4_.refs_1_, bf16[768,768]{1,0:T(8,128)(2,1)S(1)} %get-tuple-element.107.refs_2_.refs_7_, ...), custom_call_target="tpu_custom_call" | custom-call | tf_op jit(solution)/shard_map/rows_back/pallas_call | solution.py:68
  92.4 2.4 %collective-permute-done.14.refs_4_ = bf16[4,96,256]{2,1,0:T(8,128)(2,1)S(1)} collective-permute-done((bf16[4,96,256]{2,1,0:T(8,128)(2,1)S(1)}, bf16[4,96,256]{2,1,0:T(8,128)(2,1)S(1)}, u32[]{:S(2)}, u32[]{:S(2)}) %collective-permute-start.14) | collective-permute-done | bytes 196640 | tf_op jit(solution)/shard_map/ppermute | solution.py:622
  94.8 1.5 %collective-permute-start.21 = (bf16[1,96,1792]{2,1,0:T(8,128)(2,1)S(1)}, bf16[1,96,1792]{2,1,0:T(8,128)(2,1)S(1)}, u32[]{:S(2)}, u32[]{:S(2)}) collective-permute-start(bf16[1,96,1792]{2,1,0:T(8,128)(2,1)S(1)} %get-tuple-element.172), channel_id=1, source_target_pairs={{0,16},{4,20},{8,24},{12,28},{16,0},{20,4},{24,8},{28,12},{1,17},{... | collective-permute-start | bytes 1032200 | tf_op jit(solution)/shard_map/ppermute | solution.py:622
  96.3 2.0 %collective-permute-done.19.refs_13_ = bf16[1,96,2048]{2,1,0:T(8,128)(2,1)S(1)} collective-permute-done((bf16[1,96,2048]{2,1,0:T(8,128)(2,1)S(1)}, bf16[1,96,2048]{2,1,0:T(8,128)(2,1)S(1)}, u32[]{:S(2)}, u32[]{:S(2)}) %collective-permute-start.19) | collective-permute-done | bytes 393248 | tf_op jit(solution)/shard_map/ppermute | solution.py:622
  98.3 2.9 %attn_terms.1 = (f32[96,2304]{1,0:T(8,128)S(1)}, f32[48,128]{1,0:T(8,128)S(1)}, f32[96,256]{1,0:T(8,128)S(1)}, bf16[1,96,2688]{2,1,0:T(8,128)(2,1)S(1)}, bf16[1,...) custom-call(bf16[640,768]{1,0:T(8,128)(2,1)S(1)} %get-tuple-element.163.refs_0_, ...), custom_call_target="tpu_custom_call" | custom-call | tf_op jit(solution)/shard_map/attn_terms/pallas_call | solution.py:68
  101.8 3.0 %collective-permute-start.24 = (bf16[1,96,2688]{2,1,0:T(8,128)(2,1)S(1)}, bf16[1,96,2688]{2,1,0:T(8,128)(2,1)S(1)}, u32[]{:S(2)}, u32[]{:S(2)}) collective-permute-start(bf16[1,96,2688]{2,1,0:T(8,128)(2,1)S(1)} %get-tuple-element.179), channel_id=1, source_target_pairs={{0,24},{4,28},{8,16},{12,20},{16,8},{20,12},{24,0},{28,4},{1,25},{... | collective-permute-start | bytes 1548296 | tf_op jit(solution)/shard_map/ppermute | solution.py:622
  104.9 1.4 collective-permute-start.20
  106.4 1.8 %collective-permute-start.26 = (bf16[2,24,3840]{2,1,0:T(8,128)(2,1)S(1)}, bf16[2,24,3840]{2,1,0:T(8,128)(2,1)S(1)}, u32[]{:S(2)}, u32[]{:S(2)}) collective-permute-start(bf16[2,24,3840]{2,1,0:T(8,128)(2,1)S(1)} %get-tuple-element.181), channel_id=1, source_target_pairs={{0,1},{1,0},{2,3},{3,2},{4,5},{5,4},{6,7},{7,6},{8,9},{9,8},{10,11... | collective-permute-start | bytes 1105928 | tf_op jit(solution)/shard_map/ppermute | solution.py:622
  108.2 7.1 %collective-permute-done.20.refs_1_ = bf16[144,768]{1,0:T(8,128)(2,1)S(1)} collective-permute-done((bf16[144,768]{1,0:T(8,128)(2,1)S(1)}, bf16[144,768]{1,0:T(8,128)(2,1)S(1)}, u32[]{:S(2)}, u32[]{:S(2)}) %collective-permute-start.20) | collective-permute-done | bytes 221216 | tf_op jit(solution)/shard_map/ppermute | solution.py:622
  115.3 0.7 rows_result.1.refs_2_
  116.1 5.2 %collective-permute-done.26.refs_1_ = bf16[2,24,3840]{2,1,0:T(8,128)(2,1)S(1)} collective-permute-done((bf16[2,24,3840]{2,1,0:T(8,128)(2,1)S(1)}, bf16[2,24,3840]{2,1,0:T(8,128)(2,1)S(1)}, u32[]{:S(2)}, u32[]{:S(2)}) %collective-permute-start.26) | collective-permute-done | bytes 368672 | tf_op jit(solution)/shard_map/ppermute | solution.py:622
  121.3 0.9 copy-done.7
  122.3 2.2 %collective-permute-done.25.refs_1_ = bf16[2,96,512]{2,1,0:T(8,128)(2,1)S(1)} collective-permute-done((bf16[2,96,512]{2,1,0:T(8,128)(2,1)S(1)}, bf16[2,96,512]{2,1,0:T(8,128)(2,1)S(1)}, u32[]{:S(2)}, u32[]{:S(2)}) %collective-permute-start.25) | collective-permute-done | bytes 196640 | tf_op jit(solution)/shard_map/ppermute | solution.py:622
  124.6 2.2 %collective-permute-done.23 = bf16[1,96,2688]{2,1,0:T(8,128)(2,1)S(1)} collective-permute-done((bf16[1,96,2688]{2,1,0:T(8,128)(2,1)S(1)}, bf16[1,96,2688]{2,1,0:T(8,128)(2,1)S(1)}, u32[]{:S(2)}, u32[]{:S(2)}) %collective-permute-start.23) | collective-permute-done | bytes 516128 | tf_op jit(solution)/shard_map/ppermute | solution.py:622
  127.2 2.6 %collective-permute-start.28 = (bf16[1,24,2816]{2,1,0:T(8,128)(2,1)S(1)}, bf16[1,24,2816]{2,1,0:T(8,128)(2,1)S(1)}, u32[]{:S(2)}, u32[]{:S(2)}) collective-permute-start(bf16[1,24,2816]{2,1,0:T(8,128)(2,1)S(1)} %get-tuple-element.187), channel_id=1, source_target_pairs={{0,2},{1,3},{2,0},{3,1},{4,6},{5,7},{6,4},{7,5},{8,10},{9,11},{10,... | collective-permute-start | bytes 405512 | tf_op jit(solution)/shard_map/ppermute | solution.py:622
  129.8 1.8 %collective-permute-start.29 = (bf16[1,24,2816]{2,1,0:T(8,128)(2,1)S(1)}, bf16[1,24,2816]{2,1,0:T(8,128)(2,1)S(1)}, u32[]{:S(2)}, u32[]{:S(2)}) collective-permute-start(bf16[1,24,2816]{2,1,0:T(8,128)(2,1)S(1)} %get-tuple-element.188), channel_id=1, source_target_pairs={{0,3},{1,2},{2,1},{3,0},{4,7},{5,6},{6,5},{7,4},{8,11},{9,10},{10,... | collective-permute-start | bytes 405512 | tf_op jit(solution)/shard_map/ppermute | solution.py:622
  131.5 0.8 inner_result.1
  132.3 13.3 %collective-permute-done.30.refs_1_ = bf16[1,96,512]{2,1,0:T(8,128)(2,1)S(1)} collective-permute-done((bf16[1,96,512]{2,1,0:T(8,128)(2,1)S(1)}, bf16[1,96,512]{2,1,0:T(8,128)(2,1)S(1)}, u32[]{:S(2)}, u32[]{:S(2)}) %collective-permute-start.30) | collective-permute-done | bytes 98336 | tf_op jit(solution)/shard_map/ppermute | solution.py:622
  145.6 1.0 copy-done.8
  146.5 0.7 outer_result.1.refs_5_
  147.3 1.0 copy-done.6
  (99 shorter events, 12.4 us)
Async XLA Ops:
  4.3 20.5 %collective-permute-start.2 = (bf16[144,768]{1,0:T(8,128)(2,1)S(1)}, bf16[144,768]{1,0:T(8,128)(2,1)S(1)}, u32[]{:S(2)}, u32[]{:S(2)}) collective-permute-start(bf16[144,768]{1,0:T(8,128)(2,1)S(1)} %places.1.refs_6_.refs_0_), channel_id=1, source_target_pairs={{0,3},{1,2},{2,1},{3,0},{4,7},{5,6},{6,5},{7,4},{8,11},{9,10},{10,... | collective-permute-start | bytes 663560 | tf_op jit(solution)/shard_map/ppermute | solution.py:622
  9.4 18.8 %collective-permute-start.1 = (bf16[144,768]{1,0:T(8,128)(2,1)S(1)}, bf16[144,768]{1,0:T(8,128)(2,1)S(1)}, u32[]{:S(2)}, u32[]{:S(2)}) collective-permute-start(bf16[144,768]{1,0:T(8,128)(2,1)S(1)} %places.1.refs_6_.refs_0_), channel_id=1, source_target_pairs={{0,2},{1,3},{2,0},{3,1},{4,6},{5,7},{6,4},{7,5},{8,10},{9,11},{10,... | collective-permute-start | bytes 663560 | tf_op jit(solution)/shard_map/ppermute | solution.py:622
  9.4 14.3 %collective-permute-start = (bf16[144,768]{1,0:T(8,128)(2,1)S(1)}, bf16[144,768]{1,0:T(8,128)(2,1)S(1)}, u32[]{:S(2)}, u32[]{:S(2)}) collective-permute-start(bf16[144,768]{1,0:T(8,128)(2,1)S(1)} %places.1.refs_6_.refs_0_), channel_id=1, source_target_pairs={{0,1},{1,0},{2,3},{3,2},{4,5},{5,4},{6,7},{7,6},{8,9},{9,8},{10,11... | collective-permute-start | bytes 663560 | tf_op jit(solution)/shard_map/ppermute | solution.py:622
  11.8 2.3 %copy-start = (bf16[768,3072]{1,0:T(8,128)(2,1)S(1)}, bf16[768,3072]{1,0:T(8,128)(2,1)}, u32[]{:S(2)}) copy-start(bf16[768,3072]{1,0:T(8,128)(2,1)} %refs_4_.3) | copy-start | bytes 14155780
  14.2 2.3 %copy-start.1 = (bf16[3072,768]{1,0:T(8,128)(2,1)S(1)}, bf16[3072,768]{1,0:T(8,128)(2,1)}, u32[]{:S(2)}) copy-start(bf16[3072,768]{1,0:T(8,128)(2,1)} %refs_5_.1) | copy-start | bytes 14155780
  16.5 1.3 copy-start.2
  17.8 1.3 copy-start.3
  19.0 1.3 copy-start.4
  20.3 1.3 copy-start.5
  21.6 1.7 %copy-start.19 = (f32[12,32]{1,0:T(8,128)S(1)}, f32[12,32]{1,0:T(8,128)}, u32[]{:S(2)}) copy-start(f32[12,32]{1,0:T(8,128)} %param.31) | copy-start | bytes 4612
  21.6 1.7 %copy-start.20 = (f32[12,32]{1,0:T(8,128)S(1)}, f32[12,32]{1,0:T(8,128)}, u32[]{:S(2)}) copy-start(f32[12,32]{1,0:T(8,128)} %param.33) | copy-start | bytes 4612
  21.6 1.7 %copy-start.21 = (f32[12,32]{1,0:T(8,128)S(1)}, f32[12,32]{1,0:T(8,128)}, u32[]{:S(2)}) copy-start(f32[12,32]{1,0:T(8,128)} %param.32) | copy-start | bytes 4612
  23.7 4.5 %copy-start.10 = (bf16[140,768]{1,0:T(8,128)(2,1)S(1)}, bf16[140,768]{1,0:T(8,128)(2,1)}, u32[]{:S(2)}) copy-start(bf16[140,768]{1,0:T(8,128)(2,1)} %refs_15_.1) | copy-start | bytes 645124
  23.7 4.5 %copy-start.11 = (f32[768]{0:T(1024)S(1)}, f32[768]{0:T(1024)}, u32[]{:S(2)}) copy-start(f32[768]{0:T(1024)} %refs_8_.1) | copy-start | bytes 9220
  23.7 4.5 %copy-start.16 = (f32[768]{0:T(1024)S(1)}, f32[768]{0:T(1024)}, u32[]{:S(2)}) copy-start(f32[768]{0:T(1024)} %refs_17_.1) | copy-start | bytes 9220
  23.7 4.5 %copy-start.17 = (f32[768]{0:T(1024)S(1)}, f32[768]{0:T(1024)}, u32[]{:S(2)}) copy-start(f32[768]{0:T(1024)} %refs_18_.1) | copy-start | bytes 9220
  23.7 4.6 %copy-start.18 = (f32[768]{0:T(1024)S(1)}, f32[768]{0:T(1024)}, u32[]{:S(2)}) copy-start(f32[768]{0:T(1024)} %refs_19_.1) | copy-start | bytes 9220
  43.1 4.5 %collective-permute-start.4 = (bf16[4,384,512]{2,1,0:T(8,128)(2,1)S(1)}, bf16[4,384,512]{2,1,0:T(8,128)(2,1)S(1)}, u32[]{:S(2)}, u32[]{:S(2)}) collective-permute-start(bf16[4,384,512]{2,1,0:T(8,128)(2,1)S(1)} %get-tuple-element.136), channel_id=1, source_target_pairs={{0,4},{4,0},{8,12},{12,8},{16,20},{20,16},{24,28},{28,24},{1,5},{5... | collective-permute-start | bytes 4718600 | tf_op jit(solution)/shard_map/ppermute | solution.py:622
  43.1 4.8 %collective-permute-start.3 = (bf16[4,384,256]{2,1,0:T(8,128)(2,1)S(1)}, bf16[4,384,256]{2,1,0:T(8,128)(2,1)S(1)}, u32[]{:S(2)}, u32[]{:S(2)}) collective-permute-start(bf16[4,384,256]{2,1,0:T(8,128)(2,1)S(1)} %get-tuple-element.135), channel_id=1, source_target_pairs={{0,4},{4,0},{8,12},{12,8},{16,20},{20,16},{24,28},{28,24},{1,5},{5... | collective-permute-start | bytes 2359304 | tf_op jit(solution)/shard_map/ppermute | solution.py:622
  49.8 13.2 %collective-permute-start.6 = (bf16[4,96,2048]{2,1,0:T(8,128)(2,1)S(1)}, bf16[4,96,2048]{2,1,0:T(8,128)(2,1)S(1)}, u32[]{:S(2)}, u32[]{:S(2)}) collective-permute-start(bf16[4,96,2048]{2,1,0:T(8,128)(2,1)S(1)} %get-tuple-element.143), channel_id=1, source_target_pairs={{0,4},{4,0},{8,12},{12,8},{16,20},{20,16},{24,28},{28,24},{1,5},{5... | collective-permute-start | bytes 4718600 | tf_op jit(solution)/shard_map/ppermute | solution.py:622
  49.9 14.9 %collective-permute-start.5 = (bf16[4,96,1792]{2,1,0:T(8,128)(2,1)S(1)}, bf16[4,96,1792]{2,1,0:T(8,128)(2,1)S(1)}, u32[]{:S(2)}, u32[]{:S(2)}) collective-permute-start(bf16[4,96,1792]{2,1,0:T(8,128)(2,1)S(1)} %get-tuple-element.141), channel_id=1, source_target_pairs={{0,4},{4,0},{8,12},{12,8},{16,20},{20,16},{24,28},{28,24},{1,5},{5... | collective-permute-start | bytes 4128776 | tf_op jit(solution)/shard_map/ppermute | solution.py:622
  50.4 11.1 %collective-permute-start.8 = (bf16[2,384,256]{2,1,0:T(8,128)(2,1)S(1)}, bf16[2,384,256]{2,1,0:T(8,128)(2,1)S(1)}, u32[]{:S(2)}, u32[]{:S(2)}) collective-permute-start(bf16[2,384,256]{2,1,0:T(8,128)(2,1)S(1)} %get-tuple-element.146), channel_id=1, source_target_pairs={{0,8},{4,12},{8,0},{12,4},{16,24},{20,28},{24,16},{28,20},{1,9},{5... | collective-permute-start | bytes 1179656 | tf_op jit(solution)/shard_map/ppermute | solution.py:622
  51.9 11.1 %collective-permute-start.7 = (bf16[8,96,256]{2,1,0:T(8,128)(2,1)S(1)}, bf16[8,96,256]{2,1,0:T(8,128)(2,1)S(1)}, u32[]{:S(2)}, u32[]{:S(2)}) collective-permute-start(bf16[8,96,256]{2,1,0:T(8,128)(2,1)S(1)} %get-tuple-element.144), channel_id=1, source_target_pairs={{0,1},{1,0},{2,3},{3,2},{4,5},{5,4},{6,7},{7,6},{8,9},{9,8},{10,11... | collective-permute-start | bytes 1179656 | tf_op jit(solution)/shard_map/ppermute | solution.py:622
  57.9 21.7 %collective-permute-start.11 = (bf16[656,640]{1,0:T(8,128)(2,1)S(1)}, bf16[656,640]{1,0:T(8,128)(2,1)S(1)}, u32[]{:S(2)}, u32[]{:S(2)}) collective-permute-start(bf16[656,640]{1,0:T(8,128)(2,1)S(1)} %get-tuple-element.140.refs_4_.refs_5_), channel_id=1, source_target_pairs={{0,4},{4,0},{8,12},{12,8},{16,20},{20,16},{24,28},{28,24},{1,5},{5... | collective-permute-start | bytes 2519048 | tf_op jit(solution)/shard_map/ppermute | solution.py:622
  61.5 10.3 %collective-permute-start.10 = (bf16[2,384,256]{2,1,0:T(8,128)(2,1)S(1)}, bf16[2,384,256]{2,1,0:T(8,128)(2,1)S(1)}, u32[]{:S(2)}, u32[]{:S(2)}) collective-permute-start(bf16[2,384,256]{2,1,0:T(8,128)(2,1)S(1)} %get-tuple-element.156), channel_id=1, source_target_pairs={{0,8},{4,12},{8,0},{12,4},{16,24},{20,28},{24,16},{28,20},{1,9},{5... | collective-permute-start | bytes 1179656 | tf_op jit(solution)/shard_map/ppermute | solution.py:622
  63.0 21.5 %collective-permute-start.13 = (bf16[640,768]{1,0:T(8,128)(2,1)S(1)}, bf16[640,768]{1,0:T(8,128)(2,1)S(1)}, u32[]{:S(2)}, u32[]{:S(2)}) collective-permute-start(bf16[640,768]{1,0:T(8,128)(2,1)S(1)} %get-tuple-element.163.refs_0_), channel_id=1, source_target_pairs={{0,4},{4,0},{8,12},{12,8},{16,20},{20,16},{24,28},{28,24},{1,5},{5... | collective-permute-start | bytes 2949128 | tf_op jit(solution)/shard_map/ppermute | solution.py:622
  63.2 20.0 %collective-permute-start.9 = (bf16[2,96,2048]{2,1,0:T(8,128)(2,1)S(1)}, bf16[2,96,2048]{2,1,0:T(8,128)(2,1)S(1)}, u32[]{:S(2)}, u32[]{:S(2)}) collective-permute-start(bf16[2,96,2048]{2,1,0:T(8,128)(2,1)S(1)} %get-tuple-element.155), channel_id=1, source_target_pairs={{0,16},{4,20},{8,24},{12,28},{16,0},{20,4},{24,8},{28,12},{1,17},{... | collective-permute-start | bytes 2359304 | tf_op jit(solution)/shard_map/ppermute | solution.py:622
  70.8 21.4 %collective-permute-start.15 = (bf16[656,640]{1,0:T(8,128)(2,1)S(1)}, bf16[656,640]{1,0:T(8,128)(2,1)S(1)}, u32[]{:S(2)}, u32[]{:S(2)}) collective-permute-start(bf16[656,640]{1,0:T(8,128)(2,1)S(1)} %get-tuple-element.150.refs_5_.refs_7_), channel_id=1, source_target_pairs={{0,4},{4,0},{8,12},{12,8},{16,20},{20,16},{24,28},{28,24},{1,5},{5... | collective-permute-start | bytes 2519048 | tf_op jit(solution)/shard_map/ppermute | solution.py:622
  71.7 16.9 %collective-permute-start.17 = (bf16[2,96,1792]{2,1,0:T(8,128)(2,1)S(1)}, bf16[2,96,1792]{2,1,0:T(8,128)(2,1)S(1)}, u32[]{:S(2)}, u32[]{:S(2)}) collective-permute-start(bf16[2,96,1792]{2,1,0:T(8,128)(2,1)S(1)} %get-tuple-element.165), channel_id=1, source_target_pairs={{0,8},{4,12},{8,0},{12,4},{16,24},{20,28},{24,16},{28,20},{1,9},{5... | collective-permute-start | bytes 2064392 | tf_op jit(solution)/shard_map/ppermute | solution.py:622
  79.6 16.7 %collective-permute-start.16 = (bf16[704,640]{1,0:T(8,128)(2,1)S(1)}, bf16[704,640]{1,0:T(8,128)(2,1)S(1)}, u32[]{:S(2)}, u32[]{:S(2)}) collective-permute-start(bf16[704,640]{1,0:T(8,128)(2,1)S(1)} %get-tuple-element.154.refs_6_.refs_9_), channel_id=1, source_target_pairs={{0,4},{4,0},{8,12},{12,8},{16,20},{20,16},{24,28},{28,24},{1,5},{5... | collective-permute-start | bytes 2703368 | tf_op jit(solution)/shard_map/ppermute | solution.py:622
  83.2 11.6 %collective-permute-start.14 = (bf16[4,96,256]{2,1,0:T(8,128)(2,1)S(1)}, bf16[4,96,256]{2,1,0:T(8,128)(2,1)S(1)}, u32[]{:S(2)}, u32[]{:S(2)}) collective-permute-start(bf16[4,96,256]{2,1,0:T(8,128)(2,1)S(1)} %get-tuple-element.164), channel_id=1, source_target_pairs={{0,2},{1,3},{2,0},{3,1},{4,6},{5,7},{6,4},{7,5},{8,10},{9,11},{10,... | collective-permute-start | bytes 589832 | tf_op jit(solution)/shard_map/ppermute | solution.py:622
  84.4 11.9 %collective-permute-start.18 = (bf16[1,384,512]{2,1,0:T(8,128)(2,1)S(1)}, bf16[1,384,512]{2,1,0:T(8,128)(2,1)S(1)}, u32[]{:S(2)}, u32[]{:S(2)}) collective-permute-start(bf16[1,384,512]{2,1,0:T(8,128)(2,1)S(1)} %get-tuple-element.167), channel_id=1, source_target_pairs={{0,16},{4,20},{8,24},{12,28},{16,0},{20,4},{24,8},{28,12},{1,17},{... | collective-permute-start | bytes 1179656 | tf_op jit(solution)/shard_map/ppermute | solution.py:622
  88.7 9.7 %collective-permute-start.19 = (bf16[1,96,2048]{2,1,0:T(8,128)(2,1)S(1)}, bf16[1,96,2048]{2,1,0:T(8,128)(2,1)S(1)}, u32[]{:S(2)}, u32[]{:S(2)}) collective-permute-start(bf16[1,96,2048]{2,1,0:T(8,128)(2,1)S(1)} %get-tuple-element.168), channel_id=1, source_target_pairs={{0,8},{4,12},{8,0},{12,4},{16,24},{20,28},{24,16},{28,20},{1,9},{5... | collective-permute-start | bytes 1179656 | tf_op jit(solution)/shard_map/ppermute | solution.py:622
  92.2 12.6 %collective-permute-start.12 = (bf16[2,144,768]{2,1,0:T(8,128)(2,1)S(1)}, bf16[2,144,768]{2,1,0:T(8,128)(2,1)S(1)}, u32[]{:S(2)}, u32[]{:S(2)}) collective-permute-start(bf16[2,144,768]{2,1,0:T(8,128)(2,1)S(1)} %get-tuple-element.162), channel_id=1, source_target_pairs={{0,1},{1,0},{2,3},{3,2},{4,5},{5,4},{6,7},{7,6},{8,9},{9,8},{10,11... | collective-permute-start | bytes 1327112 | tf_op jit(solution)/shard_map/ppermute | solution.py:622
  94.8 11.5 %collective-permute-start.21 = (bf16[1,96,1792]{2,1,0:T(8,128)(2,1)S(1)}, bf16[1,96,1792]{2,1,0:T(8,128)(2,1)S(1)}, u32[]{:S(2)}, u32[]{:S(2)}) collective-permute-start(bf16[1,96,1792]{2,1,0:T(8,128)(2,1)S(1)} %get-tuple-element.172), channel_id=1, source_target_pairs={{0,16},{4,20},{8,24},{12,28},{16,0},{20,4},{24,8},{28,12},{1,17},{... | collective-permute-start | bytes 1032200 | tf_op jit(solution)/shard_map/ppermute | solution.py:622
  101.3 23.3 %collective-permute-start.22 = (bf16[1,96,2688]{2,1,0:T(8,128)(2,1)S(1)}, bf16[1,96,2688]{2,1,0:T(8,128)(2,1)S(1)}, u32[]{:S(2)}, u32[]{:S(2)}) collective-permute-start(bf16[1,96,2688]{2,1,0:T(8,128)(2,1)S(1)} %get-tuple-element.177), channel_id=1, source_target_pairs={{0,8},{4,12},{8,0},{12,4},{16,24},{20,28},{24,16},{28,20},{1,9},{5... | collective-permute-start | bytes 1548296 | tf_op jit(solution)/shard_map/ppermute | solution.py:622
  101.6 25.2 %collective-permute-start.23 = (bf16[1,96,2688]{2,1,0:T(8,128)(2,1)S(1)}, bf16[1,96,2688]{2,1,0:T(8,128)(2,1)S(1)}, u32[]{:S(2)}, u32[]{:S(2)}) collective-permute-start(bf16[1,96,2688]{2,1,0:T(8,128)(2,1)S(1)} %get-tuple-element.178), channel_id=1, source_target_pairs={{0,16},{4,20},{8,24},{12,28},{16,0},{20,4},{24,8},{28,12},{1,17},{... | collective-permute-start | bytes 1548296 | tf_op jit(solution)/shard_map/ppermute | solution.py:622
  101.8 25.0 %collective-permute-start.24 = (bf16[1,96,2688]{2,1,0:T(8,128)(2,1)S(1)}, bf16[1,96,2688]{2,1,0:T(8,128)(2,1)S(1)}, u32[]{:S(2)}, u32[]{:S(2)}) collective-permute-start(bf16[1,96,2688]{2,1,0:T(8,128)(2,1)S(1)} %get-tuple-element.179), channel_id=1, source_target_pairs={{0,24},{4,28},{8,16},{12,20},{16,8},{20,12},{24,0},{28,4},{1,25},{... | collective-permute-start | bytes 1548296 | tf_op jit(solution)/shard_map/ppermute | solution.py:622
  104.9 10.4 %collective-permute-start.20 = (bf16[144,768]{1,0:T(8,128)(2,1)S(1)}, bf16[144,768]{1,0:T(8,128)(2,1)S(1)}, u32[]{:S(2)}, u32[]{:S(2)}) collective-permute-start(bf16[144,768]{1,0:T(8,128)(2,1)S(1)} %get-tuple-element.171), channel_id=1, source_target_pairs={{0,2},{1,3},{2,0},{3,1},{4,6},{5,7},{6,4},{7,5},{8,10},{9,11},{10,... | collective-permute-start | bytes 663560 | tf_op jit(solution)/shard_map/ppermute | solution.py:622
  106.4 14.8 %collective-permute-start.26 = (bf16[2,24,3840]{2,1,0:T(8,128)(2,1)S(1)}, bf16[2,24,3840]{2,1,0:T(8,128)(2,1)S(1)}, u32[]{:S(2)}, u32[]{:S(2)}) collective-permute-start(bf16[2,24,3840]{2,1,0:T(8,128)(2,1)S(1)} %get-tuple-element.181), channel_id=1, source_target_pairs={{0,1},{1,0},{2,3},{3,2},{4,5},{5,4},{6,7},{7,6},{8,9},{9,8},{10,11... | collective-permute-start | bytes 1105928 | tf_op jit(solution)/shard_map/ppermute | solution.py:622
  115.3 9.2 %collective-permute-start.25 = (bf16[2,96,512]{2,1,0:T(8,128)(2,1)S(1)}, bf16[2,96,512]{2,1,0:T(8,128)(2,1)S(1)}, u32[]{:S(2)}, u32[]{:S(2)}) collective-permute-start(bf16[2,96,512]{2,1,0:T(8,128)(2,1)S(1)} %get-tuple-element.180), channel_id=1, source_target_pairs={{0,1},{1,0},{2,3},{3,2},{4,5},{5,4},{6,7},{7,6},{8,9},{9,8},{10,11... | collective-permute-start | bytes 589832 | tf_op jit(solution)/shard_map/ppermute | solution.py:622
  122.2 9.3 %collective-permute-start.31 = (bf16[1,24,3840]{2,1,0:T(8,128)(2,1)S(1)}, bf16[1,24,3840]{2,1,0:T(8,128)(2,1)S(1)}, u32[]{:S(2)}, u32[]{:S(2)}) collective-permute-start(bf16[1,24,3840]{2,1,0:T(8,128)(2,1)S(1)} %get-tuple-element.191), channel_id=1, source_target_pairs={{0,2},{1,3},{2,0},{3,1},{4,6},{5,7},{6,4},{7,5},{8,10},{9,11},{10,... | collective-permute-start | bytes 552968 | tf_op jit(solution)/shard_map/ppermute | solution.py:622
  127.1 20.2 %collective-permute-start.27 = (bf16[1,24,2816]{2,1,0:T(8,128)(2,1)S(1)}, bf16[1,24,2816]{2,1,0:T(8,128)(2,1)S(1)}, u32[]{:S(2)}, u32[]{:S(2)}) collective-permute-start(bf16[1,24,2816]{2,1,0:T(8,128)(2,1)S(1)} %get-tuple-element.186), channel_id=1, source_target_pairs={{0,1},{1,0},{2,3},{3,2},{4,5},{5,4},{6,7},{7,6},{8,9},{9,8},{10,11... | collective-permute-start | bytes 405512 | tf_op jit(solution)/shard_map/ppermute | solution.py:622
  127.2 20.1 %collective-permute-start.28 = (bf16[1,24,2816]{2,1,0:T(8,128)(2,1)S(1)}, bf16[1,24,2816]{2,1,0:T(8,128)(2,1)S(1)}, u32[]{:S(2)}, u32[]{:S(2)}) collective-permute-start(bf16[1,24,2816]{2,1,0:T(8,128)(2,1)S(1)} %get-tuple-element.187), channel_id=1, source_target_pairs={{0,2},{1,3},{2,0},{3,1},{4,6},{5,7},{6,4},{7,5},{8,10},{9,11},{10,... | collective-permute-start | bytes 405512 | tf_op jit(solution)/shard_map/ppermute | solution.py:622
  129.8 17.5 %collective-permute-start.29 = (bf16[1,24,2816]{2,1,0:T(8,128)(2,1)S(1)}, bf16[1,24,2816]{2,1,0:T(8,128)(2,1)S(1)}, u32[]{:S(2)}, u32[]{:S(2)}) collective-permute-start(bf16[1,24,2816]{2,1,0:T(8,128)(2,1)S(1)} %get-tuple-element.188), channel_id=1, source_target_pairs={{0,3},{1,2},{2,1},{3,0},{4,7},{5,6},{6,5},{7,4},{8,11},{9,10},{10,... | collective-permute-start | bytes 405512 | tf_op jit(solution)/shard_map/ppermute | solution.py:622
  131.5 14.0 %collective-permute-start.30 = (bf16[1,96,512]{2,1,0:T(8,128)(2,1)S(1)}, bf16[1,96,512]{2,1,0:T(8,128)(2,1)S(1)}, u32[]{:S(2)}, u32[]{:S(2)}) collective-permute-start(bf16[1,96,512]{2,1,0:T(8,128)(2,1)S(1)} %get-tuple-element.189), channel_id=1, source_target_pairs={{0,2},{1,3},{2,0},{3,1},{4,6},{5,7},{6,4},{7,5},{8,10},{9,11},{10,... | collective-permute-start | bytes 294920 | tf_op jit(solution)/shard_map/ppermute | solution.py:622
  145.6 1.0 copy-start.8
  147.3 1.0 copy-start.6
  (6 other events, 4.6 us)
